TPU v7x, 32 devices: a whole 2x2x4 slice. The times are simulated.
32 devices in a mesh: face: 2 (over x), px: 4 (over y, core), py: 4 (over z).
Axes of the slice: x: 2, y: 2, z: 4, core: 2. Of those that a mesh axis runs over, the one named last changes fastest.
Arguments:
- tracer_mass: float32 [40, 128, 512], P(None, ('face', 'px'), 'py'), may hold values from -6 to 6
- recon_table: float32 [10, 25], replicated, may hold values from -1.25 to 1.25
- intersection_weights: float32 [4, 10, 128, 512], P(None, None, ('face', 'px'), 'py'), may hold values from -1 to 1
- intersection_cells: int32 [4, 128, 512], P(None, ('face', 'px'), 'py'), may hold values from 0 to 8
- rotation_codes: int32 [4, 128, 512], P(None, ('face', 'px'), 'py'), may hold values from 0 to 3
Outputs:
- advected: float32 [40, 128, 512], P(None, ('face', 'px'), 'py')
Inputs may be any that keep to these rules, and one draw needn't show every extreme that they name: `intersection_cells`: the index of the 3 x 3 neighbour, row-major from offset (-1, -1). `rotation_codes`: a count of quarter turns.
All inputs are finite; a program needn't handle non-finite values.
Results may differ from a plain program's by a relative error of at most 0.0001.
Values sent between devices are 32-bit elements; how exact they have to be, the bound alone decides.
No kernel may reach another device: no remote copies, remote signals or barrier semaphores. Data moves between devices by JAX's collectives and lax.ppermute only.
A program may use at most 256 MiB of HBM per device.

v0:
```python
import jax
import jax.numpy as jnp
from jax import lax
from jax.experimental import pallas as pl
from jax.experimental.pallas import tpu as pltpu
from jax.sharding import PartitionSpec as P

F32 = jnp.float32
ROW_AXES = ("face", "px")
COLUMN_AXES = "py"
SWAPPED = (0, 2, 1, 5, 4, 3, 9, 8, 7, 6)
POWERS = ((0, 0), (1, 0), (0, 1), (2, 0), (1, 1), (0, 2), (3, 0), (2, 1), (1, 2), (0, 3))
TERMS = 10
OFFSETS = 49
GROUP = 4
SPAN = 9
PER = 14
COEF_PER = 42
VMEM = pl.BlockSpec(memory_space=pltpu.VMEM)
ANY = pl.BlockSpec(memory_space=pl.ANY)
HBM = pl.BlockSpec(memory_space=pltpu.HBM)


def params():
    return pltpu.CompilerParams(vmem_limit_bytes=40 * 1024 * 1024)


def cost(operations):
    return pl.CostEstimate(flops=operations, bytes_accessed=1 << 20, transcendentals=0)


def swap(block, axes, odd_first):
    count = lax.axis_size(axes)
    pairs = []
    for low in range(1 if odd_first else 0, count - 1, 2):
        pairs += [(low, low + 1), (low + 1, low)]
    return lax.ppermute(block, axes, pairs)


def is_even(axes):
    return lax.rem(lax.axis_index(axes), 2) == 0


def turn(value, amount):
    amount %= 128
    return pltpu.roll(value, amount, 1) if amount else value


def lanes(rows=8):
    return lax.broadcasted_iota(jnp.int32, (rows, 128), 1)


def fill_stencil(recon, weights, cells, codes, turned, spread, stencil, tiles):
    zero = jnp.zeros((8, 128), F32)
    for g in range(tiles):
        rows = pl.ds(8 * g, 8)
        for m in range(4):
            code = codes[m, rows, :]
            odd = (code & 1) == 1
            sign_x = jnp.where(code >= 2, -1.0, 1.0).astype(F32)
            sign_y = jnp.where((code == 1) | (code == 2), -1.0, 1.0).astype(F32)
            sign_xy = sign_x * sign_y
            values = [weights[m, t, rows, :] for t in range(TERMS)]
            for t, (a, b) in enumerate(POWERS):
                value = values[t]
                if SWAPPED[t] != t:
                    value = jnp.where(odd, values[SWAPPED[t]], value)
                if a % 2 and b % 2:
                    value = value * sign_xy
                elif a % 2:
                    value = value * sign_x
                elif b % 2:
                    value = value * sign_y
                turned[t, m * tiles + g] = value

    combos = 4 * tiles

    def one_tap(tap, carry):
        total = [None] * combos
        for t in range(TERMS):
            scale = recon[t, tap]
            for c in range(combos):
                term = turned[t, c] * scale
                total[c] = term if t == 0 else total[c] + term
        for c in range(combos):
            spread[tap, c] = total[c]
        return carry

    lax.fori_loop(0, 25, one_tap, 0)

    for g in range(tiles):
        rows = pl.ds(8 * g, 8)
        masks = []
        for m in range(4):
            cell = cells[m, rows, :]
            first = jnp.where(cell < 3, 0, jnp.where(cell < 6, 3, 6))
            across = cell - first
            masks.append((cell < 3, cell < 6, across == 0, across <= 1))
        for ox in range(7):
            total = [None] * 7
            for m in range(4):
                low_x, mid_x, low_y, mid_y = masks[m]

                def tap(jx, jy):
                    if 0 <= jx < 5 and 0 <= jy < 5:
                        return spread[jx * 5 + jy, m * tiles + g]
                    return zero

                line = [
                    jnp.where(low_x, tap(ox, jy), jnp.where(mid_x, tap(ox - 1, jy), tap(ox - 2, jy)))
                    for jy in range(5)
                ]
                padded = [zero, zero] + line + [zero, zero]
                for oy in range(7):
                    value = jnp.where(
                        low_y, padded[oy + 2], jnp.where(mid_y, padded[oy + 1], padded[oy])
                    )
                    total[oy] = value if m == 0 else total[oy] + value
            for oy in range(7):
                stencil[ox * 7 + oy, rows, :] = total[oy]


def coefficients(
    recon_hbm, mass_hbm, weights_hbm, cells_hbm, codes_hbm, mass, stencil, send_a, send_b,
    recon, weights, cells, codes, turned, spread, sems,
):
    sources = (recon_hbm, codes_hbm, weights_hbm, cells_hbm, mass_hbm)
    targets = (recon, codes, weights, cells, mass)
    copies = [pltpu.make_async_copy(a, b, sems.at[i]) for i, (a, b) in enumerate(zip(sources, targets))]
    for copy in copies:
        copy.start()
    for copy in copies:
        copy.wait()
    stacks, width = mass.shape[:2]
    fill_stencil(recon, weights, cells, codes, turned, spread, stencil, width // 8)
    even = is_even(ROW_AXES)
    for send, low_edge in ((send_a, jnp.logical_not(even)), (send_b, even)):
        mass_at = jnp.where(low_edge, 0, width - 6)
        stencil_at = jnp.where(low_edge, 0, width - 3)
        for s in range(stacks):
            send[6 * s : 6 * s + 6, :] = mass[s, pl.ds(mass_at, 6), :]
        for o in range(OFFSETS):
            at = 6 * stacks + 3 * o
            send[at : at + 3, :] = stencil[o, pl.ds(stencil_at, 3), :]


def pack_stacks(load, stacks, tile):
    lane = lanes()
    left = jnp.zeros((8, 128), F32)
    right = jnp.zeros((8, 128), F32)
    for s in range(PER * tile, min(stacks, PER * tile + PER)):
        at = SPAN * (s % PER)
        value = load(s)
        left = jnp.where((lane >= at + 3) & (lane < at + 9), turn(value, at + 3), left)
        right = jnp.where((lane >= at) & (lane < at + 6), turn(value, at - 122), right)
    return left, right


def pack_coefficients(load, tile):
    lane = lanes()
    left = jnp.zeros((8, 128), F32)
    right = jnp.zeros((8, 128), F32)
    for o in range(COEF_PER * tile, min(OFFSETS, COEF_PER * tile + COEF_PER)):
        at = 3 * (o % COEF_PER)
        here = (lane >= at) & (lane < at + 3)
        value = load(o)
        left = jnp.where(here, turn(value, at), left)
        right = jnp.where(here, turn(value, at - 125), right)
    return left, right


def fill_picks(picks):
    lane = lanes(1)
    group = (lane * 57) >> 9
    at = lane - SPAN * group
    source = lax.broadcasted_iota(jnp.int32, (128, 128), 0)
    for dy in range(-3, 4):
        q = at - dy
        halo = (q >= 3) & (q < 6)
        right = jnp.where(halo, 57 + q, jnp.where((q >= 0) & (q < 3) & (at >= 3), 125 + q, -1))
        left = jnp.where(halo, 61 + q, jnp.where((q >= 6) & (q < 9) & (at < 6), q - 6, -1))
        for side, wanted in enumerate((right, left)):
            wanted = jnp.where(group < PER, wanted, -1)
            picked = jnp.where(source == wanted, 1.0, 0.0).astype(jnp.bfloat16)
            picks[dy + 3, 0:128, 128 * side : 128 * side + 128] = picked
            picks[dy + 3, 128:256, 128 * side : 128 * side + 128] = picked


def pack_own(mass, stencil, left, right, picks):
    fill_picks(picks)
    stacks, width = mass.shape[:2]
    tiles = -(-stacks // PER)
    for half in range(width // 8):
        rows = pl.ds(8 * half, 8)
        for tile in range(tiles):
            at = width * tile + 8 * half
            left[at : at + 8, :], right[at : at + 8, :] = pack_stacks(
                lambda s: mass[s, rows, :], stacks, tile
            )
        for tile in range(2):
            at = width * (tiles + tile) + 8 * half
            left[at : at + 8, :], right[at : at + 8, :] = pack_coefficients(
                lambda o: stencil[o, rows, :], tile
            )


def join_halo(own_left, own_right, got_a, got_b, send_left, send_right, stacks, width):
    tiles = -(-stacks // PER)
    for send, own in ((send_left, own_left), (send_right, own_right)):
        for tile in range(tiles):
            send[tile, 0:width, :] = own[width * tile : width * tile + width, :]
            send[tile, width + 12 : width + 16, :] = jnp.zeros((4, 128), F32)
        for tile in range(2):
            at = width * (tiles + tile)
            send[tiles + tile, 0:width, :] = own[at : at + width, :]
            send[tiles + tile, width + 6 : width + 16, :] = jnp.zeros((10, 128), F32)

    def place(above, below):
        for got, mass_at, coef_at in ((above, width, width), (below, width + 6, width + 3)):
            for tile in range(tiles):
                left, right = pack_stacks(lambda s: got[6 * s : 6 * s + 8, :], stacks, tile)
                send_left[tile, mass_at : mass_at + 6, :] = left[0:6]
                send_right[tile, mass_at : mass_at + 6, :] = right[0:6]
            for tile in range(2):
                base = 6 * stacks
                left, right = pack_coefficients(lambda o: got[base + 3 * o : base + 3 * o + 8, :], tile)
                send_left[tiles + tile, coef_at : coef_at + 3, :] = left[0:3]
                send_right[tiles + tile, coef_at : coef_at + 3, :] = right[0:3]

    even = is_even(ROW_AXES)

    @pl.when(even)
    def _():
        place(got_b, got_a)

    @pl.when(jnp.logical_not(even))
    def _():
        place(got_a, got_b)


def choose(even, first, second, first_out, second_out):
    @pl.when(even)
    def _():
        first_out[...] = first[...]
        second_out[...] = second[...]

    @pl.when(jnp.logical_not(even))
    def _():
        first_out[...] = second[...]
        second_out[...] = first[...]


def pack_all(mass, own_left, own_right, got_a, got_b, send_a, send_b, left, right):
    stacks, width = mass.shape[:2]
    join_halo(own_left, own_right, got_a, got_b, left, right, stacks, width)
    choose(is_even(COLUMN_AXES), right, left, send_a, send_b)


def main_sum(load, coef, coef_at, tile):
    fields = [[load(k, 8 * tile + dx) for k in range(GROUP)] for dx in range(7)]
    total = [None] * GROUP
    for dy in range(7):
        part = [None] * GROUP
        for dx in range(7):
            at = coef_at + 8 * tile
            scale = coef[dx * 7 + dy, at : at + 8, :]
            for k in range(GROUP):
                term = scale * fields[dx][k]
                part[k] = term if dx == 0 else part[k] + term
        for k in range(GROUP):
            moved = turn(part[k], 3 - dy)
            total[k] = moved if dy == 0 else total[k] + moved
    return total


def some_steps(field, shifted, partial, stacks, first):
    def some_stacks(group, carry):
        for tile in range(partial.shape[1] // 8):
            total = main_sum(
                lambda k, at: field[first + group * GROUP + k, at : at + 8, :], shifted, 0, tile
            )
            for k in range(GROUP):
                partial[group * GROUP + k, 8 * tile : 8 * tile + 8, :] = total[k]
        return carry

    lax.fori_loop(0, stacks // GROUP, some_stacks, 0)


def hand_on(send, got, partial, out):
    out[...] = send[...]


def step_one(mass, stencil, got_a, got_b, partial, wide, shifted, field):
    stacks, width = mass.shape[:2]

    def place(above, below):
        for s in range(stacks):
            field[s, 0:6, :] = above[6 * s : 6 * s + 6, :]
            field[s, width + 6 : width + 12, :] = below[6 * s : 6 * s + 6, :]
        for o in range(OFFSETS):
            at = 6 * stacks + 3 * o
            wide[o, 0:3, :] = above[at : at + 3, :]
            wide[o, width + 3 : width + 6, :] = below[at : at + 3, :]

    even = is_even(ROW_AXES)

    @pl.when(even)
    def _():
        place(got_b, got_a)

    @pl.when(jnp.logical_not(even))
    def _():
        place(got_a, got_b)

    for s in range(stacks):
        field[s, 6 : width + 6, :] = mass[s, :, :]
        field[s, width + 12 : width + 16, :] = jnp.zeros((4, 128), F32)
    for o in range(OFFSETS):
        wide[o, 3 : width + 3, :] = stencil[o, :, :]
        wide[o, width + 6 : width + 8, :] = jnp.zeros((2, 128), F32)
    lane = lanes()
    for tile in range((width + 8) // 8):
        rows = pl.ds(8 * tile, 8)
        for dy in range(-3, 4):
            values = [turn(wide[dx * 7 + dy + 3, rows, :], dy) for dx in range(7)]
            if dy > 0:
                values = [jnp.where(lane >= dy, value, 0.0) for value in values]
            elif dy < 0:
                values = [jnp.where(lane < 128 + dy, value, 0.0) for value in values]
            for dx in range(7):
                shifted[dx * 7 + dy + 3, rows, :] = values[dx]
    some_steps(field, shifted, partial, partial.shape[0], 0)


def more_step_one(field, shifted, partial, own_shifted):
    width = own_shifted.shape[1]
    for o in range(OFFSETS):
        own_shifted[o, :, :] = shifted[o, 3 : width + 3, :]
    some_steps(field, shifted, partial, partial.shape[0], field.shape[0] - partial.shape[0])


def packed_sum(load, coef, coef_at, tile, tiles, dys):
    fields = [[load(t, 8 * tile + dx) for t in range(tiles)] for dx in range(7)]
    total = [None] * tiles
    for dy in dys:
        part = [None] * tiles
        for dx in range(7):
            at = coef_at + 8 * tile
            scale = coef[dx * 7 + dy + 3, at : at + 8, :]
            for t in range(tiles):
                term = scale * fields[dx][t]
                part[t] = term if dx == 0 else part[t] + term
        for t in range(tiles):
            moved = turn(part[t], -dy)
            total[t] = moved if total[t] is None else total[t] + moved
    return total


def place_in_group(rows=8):
    lane = lanes(rows)
    return lane - SPAN * ((lane * 57) >> 9)


def side_coefficients(
    wide, send_a, send_b, got_a, got_b, picks,
    right_set, left_set, right_coef, left_coef, right_halo, left_halo, rows_of,
):
    tall = wide.shape[1]
    width = tall - 8
    tiles = right_set.shape[0]
    lane = lanes()

    def gather(sent_right, sent_left, from_right, from_left):
        place = place_in_group(width + 16)
        for tile in range(tiles):
            right = jnp.where(place < 3, turn(sent_right[tile], -3), from_right[tile])
            left = jnp.where(place >= 6, turn(sent_left[tile], 3), from_left[tile])
            for target, value in ((right_set, right), (left_set, left)):
                target[tile, 6 : width + 6, :] = value[0:width]
                target[tile, 0:6, :] = value[width : width + 6]
                target[tile, width + 6 : width + 16, :] = value[width + 6 : width + 16]
        for tile in range(2):
            for target, source in ((right_halo, from_right), (left_halo, from_left)):
                target[tile, 3 : width + 3, :] = source[tiles + tile, 0:width, :]
                target[tile, 0:3, :] = source[tiles + tile, width : width + 3, :]
                target[tile, width + 3 : width + 8, :] = source[tiles + tile, width + 3 : width + 8, :]

    even = is_even(COLUMN_AXES)

    @pl.when(even)
    def _():
        gather(send_a, send_b, got_a, got_b)

    @pl.when(jnp.logical_not(even))
    def _():
        gather(send_b, send_a, got_b, got_a)

    from_right = (lane >= 60) & (lane < 63)
    from_left = (lane >= 64) & (lane < 67)
    for tile in range(tall // 8):
        rows = pl.ds(8 * tile, 8)
        right_rows = [right_halo[t, rows, :] for t in range(2)]
        left_rows = [left_halo[t, rows, :] for t in range(2)]
        for dy in range(7):
            values = []
            for dx in range(7):
                o = dx * 7 + dy
                at = 3 * (o % COEF_PER)
                right = turn(right_rows[o // COEF_PER], 60 - at)
                left = turn(left_rows[o // COEF_PER], 64 - at)
                values.append(
                    jnp.where(from_right, right, jnp.where(from_left, left, wide[o, rows, :]))
                )
            for dx in range(7):
                at = tall * dx + 8 * tile
                rows_of[dy, at : at + 8, :] = values[dx]

    for dy in range(7):
        value = rows_of[dy]
        high = value.astype(jnp.bfloat16)
        low = (value - high.astype(F32)).astype(jnp.bfloat16)
        both = jnp.concatenate([high, low], axis=1)
        spread = jnp.dot(both, picks[dy], preferred_element_type=F32)
        for dx in range(7):
            right_coef[dx * 7 + dy, :, :] = spread[tall * dx : tall * dx + tall, 0:128]
            left_coef[dx * 7 + dy, :, :] = spread[tall * dx : tall * dx + tall, 128:256]


def halo_steps(
    right_set, left_set, right_coef, left_coef, partial, more_partial, field, edges,
    edge_one, edge_two, right_next, left_next,
):
    tiles = right_set.shape[0]
    place = place_in_group()
    everywhere = range(-3, 4)
    for tile in range(edge_one.shape[1] // 8):
        rows = pl.ds(8 * tile, 8)
        right = packed_sum(
            lambda t, at: right_set[t, at : at + 8, :], right_coef, 0, tile, tiles, everywhere
        )
        left = packed_sum(
            lambda t, at: left_set[t, at : at + 8, :], left_coef, 0, tile, tiles, everywhere
        )
        halo = (place >= 3) & (place < 6)
        for t in range(tiles):
            right_next[t, rows, :] = jnp.where(halo, right[t], 0.0)
            left_next[t, rows, :] = jnp.where(halo, left[t], 0.0)
            edge_one[t, rows, :] = jnp.where(place < 3, right[t], turn(left[t], -3))
    for tile in range(edge_two.shape[1] // 8):
        rows = pl.ds(8 * tile, 8)
        right = packed_sum(
            lambda t, at: right_next[t, at : at + 8, :], right_coef, 3, tile, tiles, range(1, 4)
        )
        left = packed_sum(
            lambda t, at: left_next[t, at : at + 8, :], left_coef, 3, tile, tiles, range(-3, 0)
        )
        for t in range(tiles):
            edge_two[t, rows, :] = jnp.where(place < 3, right[t], turn(left[t], -3))

    lane = lanes()
    at_edge = (lane < 3) | (lane >= 125)
    stacks, more = field.shape[0], partial.shape[0]
    for t in range(tiles):
        members = range(PER * t, min(stacks, PER * t + PER))
        for tile in range(edge_one.shape[1] // 8):
            rows = pl.ds(8 * tile, 8)
            packed = edge_one[t, rows, :]
            values = []
            for s in members:
                value = partial[s, rows, :] if s < more else more_partial[s - more, rows, :]
                values.append(value + jnp.where(at_edge, turn(packed, 125 - SPAN * (s % PER)), 0.0))
            for s, value in zip(members, values):
                field[s, rows, :] = value
        for tile in range(edge_two.shape[1] // 8):
            rows = pl.ds(8 * tile, 8)
            packed = edge_two[t, rows, :]
            values = [jnp.where(at_edge, turn(packed, 125 - SPAN * (s % PER)), 0.0) for s in members]
            for s, value in zip(members, values):
                edges[s, rows, :] = value


def step_two(field, own_shifted, edges, out):
    def some_stacks(group, carry):
        for tile in range(out.shape[1] // 8):
            total = main_sum(lambda k, at: field[group * GROUP + k, at : at + 8, :], own_shifted, 0, tile)
            rows = pl.ds(8 * tile, 8)
            values = [total[k] + edges[group * GROUP + k, rows, :] for k in range(GROUP)]
            for k in range(GROUP):
                out[group * GROUP + k, rows, :] = values[k]
        return carry

    lax.fori_loop(0, out.shape[0] // GROUP, some_stacks, 0)


def local(tracer_mass, recon_table, intersection_weights, intersection_cells, rotation_codes):
    stacks, width, columns = tracer_mass.shape
    shape = lambda *sizes: jax.ShapeDtypeStruct(sizes, F32)
    scratch = lambda *sizes: pltpu.VMEM(sizes, F32)
    edge = -(-(6 * stacks + 3 * OFFSETS) // 8) * 8
    tiles = -(-stacks // PER)
    combos = 4 * (width // 8)

    mass, stencil, send_a, send_b = pl.pallas_call(
        coefficients,
        out_shape=(shape(*tracer_mass.shape), shape(OFFSETS, width, 128), shape(edge, 128), shape(edge, 128)),
        in_specs=[HBM] * 5,
        out_specs=(VMEM,) * 4,
        scratch_shapes=[
            pltpu.SMEM(recon_table.shape, F32),
            scratch(*intersection_weights.shape),
            pltpu.VMEM(intersection_cells.shape, jnp.int32),
            pltpu.VMEM(rotation_codes.shape, jnp.int32),
            scratch(TERMS, combos, 8, 128),
            scratch(25, combos, 8, 128),
            pltpu.SemaphoreType.DMA((5,)),
        ],
        compiler_params=params(),
        cost_estimate=cost(8 * 10**6),
        name="coefficients",
    )(*(
        pltpu.with_memory_space_constraint(value, pltpu.HBM)
        for value in (recon_table, tracer_mass, intersection_weights, intersection_cells, rotation_codes)
    ))
    got_a = swap(send_a, ROW_AXES, False)
    got_b = swap(send_b, ROW_AXES, True)

    tall, low = width + 16, width + 8
    picks = jax.ShapeDtypeStruct((7, 256, 256), jnp.bfloat16)
    own_left, own_right, picks = pl.pallas_call(
        pack_own,
        out_shape=(shape(width * (tiles + 2), 128),) * 2 + (picks,),
        in_specs=[VMEM] * 2,
        out_specs=(VMEM,) * 3,
        compiler_params=params(),
        cost_estimate=cost(10**6),
        name="pack_own",
    )(mass, stencil)

    send = (tiles + 2, tall, 128)
    send_a, send_b = pl.pallas_call(
        pack_all,
        out_shape=(shape(*send),) * 2,
        in_specs=[VMEM] * 5,
        out_specs=(VMEM,) * 2,
        scratch_shapes=[scratch(*send)] * 2,
        compiler_params=params(),
        cost_estimate=cost(10**6),
        name="pack_all",
    )(mass, own_left, own_right, got_a, got_b)
    column_a = swap(send_a, COLUMN_AXES, False)

    later = GROUP * (stacks // (2 * GROUP) - 1)
    partial, wide, shifted, field = pl.pallas_call(
        step_one,
        out_shape=(
            shape(stacks - later, low, 128), shape(OFFSETS, low, 128), shape(OFFSETS, low, 128),
            shape(stacks, tall, 128),
        ),
        in_specs=[VMEM] * 4,
        out_specs=(VMEM,) * 4,
        compiler_params=params(),
        cost_estimate=cost(8 * 10**6),
        name="step_one",
    )(mass, stencil, got_a, got_b)

    send_b = pl.pallas_call(
        hand_on,
        out_shape=shape(*send),
        in_specs=[VMEM, ANY, ANY],
        out_specs=VMEM,
        compiler_params=params(),
        cost_estimate=cost(10**4),
        name="hand_on",
    )(send_b, column_a, partial)
    column_b = swap(send_b, COLUMN_AXES, True)

    more_partial, own_shifted = pl.pallas_call(
        more_step_one,
        out_shape=(shape(later, low, 128), shape(OFFSETS, width, 128)),
        in_specs=[VMEM] * 2,
        out_specs=(VMEM,) * 2,
        compiler_params=params(),
        cost_estimate=cost(4 * 10**6),
        name="more_step_one",
    )(field, shifted)

    sides = pl.pallas_call(
        side_coefficients,
        out_shape=(shape(tiles, tall, 128),) * 2 + (shape(OFFSETS, low, 128),) * 2,
        in_specs=[VMEM] * 6,
        out_specs=(VMEM,) * 4,
        scratch_shapes=[scratch(2, low, 128)] * 2 + [scratch(7, 7 * low, 128)],
        compiler_params=params(),
        cost_estimate=cost(4 * 10**6),
        name="side_coefficients",
    )(wide, send_a, send_b, column_a, column_b, picks)

    field, edges = pl.pallas_call(
        halo_steps,
        out_shape=(shape(stacks, low, 128), shape(stacks, width, 128)),
        in_specs=[VMEM] * 6,
        out_specs=(VMEM,) * 2,
        scratch_shapes=[scratch(tiles, low, 128), scratch(tiles, width, 128)] + [scratch(tiles, low, 128)] * 2,
        compiler_params=params(),
        cost_estimate=cost(4 * 10**6),
        name="halo_steps",
    )(*sides, partial, more_partial)

    return pl.pallas_call(
        step_two,
        out_shape=shape(stacks, width, columns),
        in_specs=[VMEM] * 3,
        out_specs=VMEM,
        compiler_params=params(),
        cost_estimate=cost(8 * 10**6),
        name="step_two",
    )(field, own_shifted, edges)


def solution(mesh):
    in_specs = (
        P(None, ("face", "px"), "py"),
        P(),
        P(None, None, ("face", "px"), "py"),
        P(None, ("face", "px"), "py"),
        P(None, ("face", "px"), "py"),
    )
    out_specs = P(None, ("face", "px"), "py")
    return jax.shard_map(local, mesh=mesh, in_specs=in_specs, out_specs=out_specs, check_vma=False)
```

profile of v0, /device:TPU:12, one launch (start us, length us, event | category | flops | bytes accessed | tf_op | source)
XLA Modules:
  0.0 26.6 jit_solution(3741484378624665552)
XLA Ops:
  0.0 2.2 %coefficients.1 = (f32[40,16,128]{2,1,0:T(8,128)S(1)}, f32[49,16,128]{2,1,0:T(8,128)S(1)}, f32[392,128]{1,0:T(8,128)S(1)}, f32[392,128]{1,0:T(8,128)S(1)}) custom-call(f32[10,25]{1,0:T(8,128)} %recon_hbm.1, f32[40,16,128]{2,1,0:T(8,128)} %mass_hbm.1, f32[4,10,16,128]{3,2,1,0:T(8,128)} %weights_hbm.1, s32[4,16,128]{2,1,0:T(8,128)} %cells_hbm.1, ...), custom_call_target="tpu_custom_call" | custom-call | flops 8000000 | bytes 1048576 | tf_op jit(solution)/shard_map/coefficients/pallas_call | solution.py:503
  2.3 0.1 collective-permute-start
  2.3 2.5 %collective-permute-start.1 = (f32[392,128]{1,0:T(8,128)S(1)}, f32[392,128]{1,0:T(8,128)S(1)}, u32[]{:S(2)}, u32[]{:S(2)}) collective-permute-start(f32[392,128]{1,0:T(8,128)S(1)} %get-tuple-element.29), channel_id=1, source_target_pairs={{4,8},{8,4},{12,16},{16,12},{20,24},{24,20},{5,9},{9,5},{13,17},{1... | collective-permute-start | bytes 602120 | tf_op jit(solution)/shard_map/ppermute | solution.py:37
  4.8 0.5 %pack_own.1 = (f32[80,128]{1,0:T(8,128)S(1)}, f32[80,128]{1,0:T(8,128)S(1)}, bf16[7,256,256]{2,1,0:T(8,128)(2,1)S(1)}) custom-call(f32[40,16,128]{2,1,0:T(8,128)S(1)} %get-tuple-element.26.mass, f32[49,16,128]{2,1,0:T(8,128)S(1)} %get-tuple-element.27.stencil), custom_call_target="tpu_custom_call" | custom-call | flops 1000000 | bytes 1048576 | tf_op jit(solution)/shard_map/pack_own/pallas_call | solution.py:529
  5.4 0.0 collective-permute-done.got_a
  5.4 6.1 %collective-permute-done.1.got_b = f32[392,128]{1,0:T(8,128)S(1)} collective-permute-done((f32[392,128]{1,0:T(8,128)S(1)}, f32[392,128]{1,0:T(8,128)S(1)}, u32[]{:S(2)}, u32[]{:S(2)}) %collective-permute-start.1) | collective-permute-done | bytes 200736 | tf_op jit(solution)/shard_map/ppermute | solution.py:37
  11.5 0.5 %pack_all.1 = (f32[5,32,128]{2,1,0:T(8,128)S(1)}, f32[5,32,128]{2,1,0:T(8,128)S(1)}) custom-call(f32[40,16,128]{2,1,0:T(8,128)S(1)} %get-tuple-element.26.mass, f32[80,128]{1,0:T(8,128)S(1)} %get-tuple-element.31.own_left, f32[80,128]{1,0:T(8,128)S(1)} %get-tuple-element.32.own_right, f32[392,128]{1,0:T(8,128)S(1)} %collective-permute-done.got_a, ...), custom_call_target="tpu_custom_call" | custom-call | flops 1000000 | bytes 1048576 | tf_op jit(solution)/shard_map/pack_all/pallas_call | solution.py:540
  12.0 0.5 %collective-permute-start.2 = (f32[5,32,128]{2,1,0:T(8,128)S(1)}, f32[5,32,128]{2,1,0:T(8,128)S(1)}, u32[]{:S(2)}, u32[]{:S(2)}) collective-permute-start(f32[5,32,128]{2,1,0:T(8,128)S(1)} %get-tuple-element.33.send_a), channel_id=1, source_target_pairs={{0,1},{1,0},{2,3},{3,2},{4,5},{5,4},{6,7},{7,6},{8,9},{9,8},{10,11... | collective-permute-start | bytes 245768 | tf_op jit(solution)/shard_map/ppermute | solution.py:37
  12.5 1.7 %step_one.1 = (f32[24,24,128]{2,1,0:T(8,128)S(1)}, f32[49,24,128]{2,1,0:T(8,128)S(1)}, f32[49,24,128]{2,1,0:T(8,128)S(1)}, f32[40,32,128]{2,1,0:T(8,128)S(1)}) custom-call(f32[40,16,128]{2,1,0:T(8,128)S(1)} %get-tuple-element.26.mass, f32[49,16,128]{2,1,0:T(8,128)S(1)} %get-tuple-element.27.stencil, f32[392,128]{1,0:T(8,128)S(1)} %collective-permute-done.got_a, ...), custom_call_target="tpu_custom_call" | custom-call | flops 8000000 | bytes 1048576 | tf_op jit(solution)/shard_map/step_one/pallas_call | solution.py:553
  14.2 2.3 %collective-permute-done.2.got.got_a = f32[5,32,128]{2,1,0:T(8,128)S(1)} collective-permute-done((f32[5,32,128]{2,1,0:T(8,128)S(1)}, f32[5,32,128]{2,1,0:T(8,128)S(1)}, u32[]{:S(2)}, u32[]{:S(2)}) %collective-permute-start.2) | collective-permute-done | bytes 81952 | tf_op jit(solution)/shard_map/ppermute | solution.py:37
  16.5 3.5 %collective-permute-start.3 = (f32[5,32,128]{2,1,0:T(8,128)S(1)}, f32[5,32,128]{2,1,0:T(8,128)S(1)}, u32[]{:S(2)}, u32[]{:S(2)}) collective-permute-start(f32[5,32,128]{2,1,0:T(8,128)S(1)} %hand_on.1.send_b), channel_id=1, source_target_pairs={{1,2},{2,1},{5,6},{6,5},{9,10},{10,9},{13,14},{14,13},{17,18},{18,... | collective-permute-start | bytes 245768 | tf_op jit(solution)/shard_map/ppermute | solution.py:37
  20.0 1.0 %more_step_one.1 = (f32[16,24,128]{2,1,0:T(8,128)S(1)}, f32[49,16,128]{2,1,0:T(8,128)S(1)}) custom-call(f32[40,32,128]{2,1,0:T(8,128)S(1)} %get-tuple-element.41.field, f32[49,24,128]{2,1,0:T(8,128)S(1)} %get-tuple-element.42.shifted), custom_call_target="tpu_custom_call" | custom-call | flops 4000000 | bytes 1048576 | tf_op jit(solution)/shard_map/more_step_one/pallas_call | solution.py:577
  21.0 1.9 %collective-permute-done.3.got_b = f32[5,32,128]{2,1,0:T(8,128)S(1)} collective-permute-done((f32[5,32,128]{2,1,0:T(8,128)S(1)}, f32[5,32,128]{2,1,0:T(8,128)S(1)}, u32[]{:S(2)}, u32[]{:S(2)}) %collective-permute-start.3) | collective-permute-done | bytes 81952 | tf_op jit(solution)/shard_map/ppermute | solution.py:37
  22.8 0.6 %side_coefficients.1 = (f32[3,32,128]{2,1,0:T(8,128)S(1)}, f32[3,32,128]{2,1,0:T(8,128)S(1)}, f32[49,24,128]{2,1,0:T(8,128)S(1)}, f32[49,24,128]{2,1,0:T(8,128)S(1)}) custom-call(f32[49,24,128]{2,1,0:T(8,128)S(1)} %get-tuple-element.30.wide, f32[5,32,128]{2,1,0:T(8,128)S(1)} %get-tuple-element.33.send_a, f32[5,32,128]{2,1,0:T(8,128)S(1)} %hand_on.1.send_b, ...), custom_call_target="tpu_custom_call" | custom-call | flops 4000000 | bytes 1048576 | tf_op jit(solution)/shard_map/side_coefficients/pallas_call | solution.py:587
  23.4 0.7 %halo_steps.1 = (f32[40,24,128]{2,1,0:T(8,128)S(1)}, f32[40,16,128]{2,1,0:T(8,128)S(1)}) custom-call(f32[3,32,128]{2,1,0:T(8,128)S(1)} %get-tuple-element.37.right_set, f32[3,32,128]{2,1,0:T(8,128)S(1)} %get-tuple-element.38.left_set, f32[49,24,128]{2,1,0:T(8,128)S(1)} %get-tuple-element.39.right_coef, f32[49,24,128]{2,1,0:T(8,128)S(1)} %get-tuple-element.40.left_coef, ...), custom_call_target="tpu_custom_call" | custom-call | flops 4000000 | bytes 1048576 | tf_op jit(solution)/shard_map/halo_steps/pallas_call | solution.py:598
  24.2 2.4 %step_two.1 = f32[40,16,128]{2,1,0:T(8,128)} custom-call(f32[40,24,128]{2,1,0:T(8,128)S(1)} %get-tuple-element.44.field, f32[49,16,128]{2,1,0:T(8,128)S(1)} %get-tuple-element.45.own_shifted, f32[40,16,128]{2,1,0:T(8,128)S(1)} %get-tuple-element.46.edges), custom_call_target="tpu_custom_call" | custom-call | flops 8000000 | bytes 1048576 | tf_op jit(solution)/shard_map/step_two/pallas_call | solution.py:609
  (1 shorter events, 0.0 us)
Async XLA Ops:
  2.3 3.1 %collective-permute-start = (f32[392,128]{1,0:T(8,128)S(1)}, f32[392,128]{1,0:T(8,128)S(1)}, u32[]{:S(2)}, u32[]{:S(2)}) collective-permute-start(f32[392,128]{1,0:T(8,128)S(1)} %get-tuple-element.28), channel_id=1, source_target_pairs={{0,4},{4,0},{8,12},{12,8},{16,20},{20,16},{24,28},{28,24},{1,5},{5... | collective-permute-start | bytes 602120 | tf_op jit(solution)/shard_map/ppermute | solution.py:37
  2.3 9.2 %collective-permute-start.1 = (f32[392,128]{1,0:T(8,128)S(1)}, f32[392,128]{1,0:T(8,128)S(1)}, u32[]{:S(2)}, u32[]{:S(2)}) collective-permute-start(f32[392,128]{1,0:T(8,128)S(1)} %get-tuple-element.29), channel_id=1, source_target_pairs={{4,8},{8,4},{12,16},{16,12},{20,24},{24,20},{5,9},{9,5},{13,17},{1... | collective-permute-start | bytes 602120 | tf_op jit(solution)/shard_map/ppermute | solution.py:37
  12.0 4.5 %collective-permute-start.2 = (f32[5,32,128]{2,1,0:T(8,128)S(1)}, f32[5,32,128]{2,1,0:T(8,128)S(1)}, u32[]{:S(2)}, u32[]{:S(2)}) collective-permute-start(f32[5,32,128]{2,1,0:T(8,128)S(1)} %get-tuple-element.33.send_a), channel_id=1, source_target_pairs={{0,1},{1,0},{2,3},{3,2},{4,5},{5,4},{6,7},{7,6},{8,9},{9,8},{10,11... | collective-permute-start | bytes 245768 | tf_op jit(solution)/shard_map/ppermute | solution.py:37
  16.5 6.3 %collective-permute-start.3 = (f32[5,32,128]{2,1,0:T(8,128)S(1)}, f32[5,32,128]{2,1,0:T(8,128)S(1)}, u32[]{:S(2)}, u32[]{:S(2)}) collective-permute-start(f32[5,32,128]{2,1,0:T(8,128)S(1)} %hand_on.1.send_b), channel_id=1, source_target_pairs={{1,2},{2,1},{5,6},{6,5},{9,10},{10,9},{13,14},{14,13},{17,18},{18,... | collective-permute-start | bytes 245768 | tf_op jit(solution)/shard_map/ppermute | solution.py:37
where the time goes:
time: 26.8 us; the launch traced here: 26.6 us
  waiting for transfers between devices  10.3 us (38%)
  Pallas kernels  9.65 us (36%)
  starting transfers between devices  6.56 us (24%)
    ppermute x4, waiting for transfers between devices, swap(): return lax.ppermute(block, axes, pairs)  10.3 us
    ppermute x4, starting transfers between devices, swap(): return lax.ppermute(block, axes, pairs)  6.56 us
    pallas_call x1, Pallas kernels, local(): pl.pallas_call(step_two, out_shape=shape(stacks, width, columns), in_spec...  2.41 us
    pallas_call x1, Pallas kernels, local(): pl.pallas_call(coefficients, out_shape=(shape(*tracer_mass.shape), shape(...  2.25 us
    pallas_call x1, Pallas kernels, local(): pl.pallas_call(step_one, out_shape=(shape(stacks - later, low, 128), shap...  1.71 us
    pallas_call x1, Pallas kernels, local(): pl.pallas_call(more_step_one, out_shape=(shape(later, low, 128), shape(OF...  0.97 us
    pallas_call x1, Pallas kernels, local(): pl.pallas_call(halo_steps, out_shape=(shape(stacks, low, 128), shape(stac...  0.73 us
    pallas_call x1, Pallas kernels, local(): pl.pallas_call(side_coefficients, out_shape=(shape(tiles, tall, 128),) *...  0.59 us
  transfers between devices with their start and end apart: 4, of which 3 were waited for; matrix products, arithmetic and copies ran while one was open for 0% of the time, Pallas kernels for 12%

commit v1 on v0

--- a/solution.py
+++ b/solution.py
@@ -17,7 +17,6 @@
 PER = 14
 COEF_PER = 42
 VMEM = pl.BlockSpec(memory_space=pltpu.VMEM)
-ANY = pl.BlockSpec(memory_space=pl.ANY)
 HBM = pl.BlockSpec(memory_space=pltpu.HBM)
 
 
@@ -31,10 +30,21 @@
 
 def swap(block, axes, odd_first):
     count = lax.axis_size(axes)
-    pairs = []
-    for low in range(1 if odd_first else 0, count - 1, 2):
-        pairs += [(low, low + 1), (low + 1, low)]
-    return lax.ppermute(block, axes, pairs)
+    partner = list(range(count))
+    for low in range(1 if odd_first else 0, count, 2):
+        high = (low + 1) % count
+        partner[low], partner[high] = high, low
+    return lax.ppermute(block, axes, list(enumerate(partner)))
+
+
+def shift(block, axes, step):
+    count = lax.axis_size(axes)
+    return lax.ppermute(block, axes, [(index, (index + step) % count) for index in range(count)])
+
+
+def ends(axes):
+    index = lax.axis_index(axes)
+    return index == 0, index == lax.axis_size(axes) - 1
 
 
 def is_even(axes):
@@ -121,7 +131,7 @@
 
 
 def coefficients(
-    recon_hbm, mass_hbm, weights_hbm, cells_hbm, codes_hbm, mass, stencil, send_a, send_b,
+    recon_hbm, mass_hbm, weights_hbm, cells_hbm, codes_hbm, mass, stencil, send_down, send_up,
     recon, weights, cells, codes, turned, spread, sems,
 ):
     sources = (recon_hbm, codes_hbm, weights_hbm, cells_hbm, mass_hbm)
@@ -133,15 +143,12 @@
         copy.wait()
     stacks, width = mass.shape[:2]
     fill_stencil(recon, weights, cells, codes, turned, spread, stencil, width // 8)
-    even = is_even(ROW_AXES)
-    for send, low_edge in ((send_a, jnp.logical_not(even)), (send_b, even)):
-        mass_at = jnp.where(low_edge, 0, width - 6)
-        stencil_at = jnp.where(low_edge, 0, width - 3)
+    for send, mass_at, stencil_at in ((send_down, width - 6, width - 3), (send_up, 0, 0)):
         for s in range(stacks):
-            send[6 * s : 6 * s + 6, :] = mass[s, pl.ds(mass_at, 6), :]
+            send[6 * s : 6 * s + 6, :] = mass[s, mass_at : mass_at + 6, :]
         for o in range(OFFSETS):
             at = 6 * stacks + 3 * o
-            send[at : at + 3, :] = stencil[o, pl.ds(stencil_at, 3), :]
+            send[at : at + 3, :] = stencil[o, stencil_at : stencil_at + 3, :]
 
 
 def pack_stacks(load, stacks, tile):
@@ -204,7 +211,7 @@
             )
 
 
-def join_halo(own_left, own_right, got_a, got_b, send_left, send_right, stacks, width):
+def join_halo(own_left, own_right, above, below, send_left, send_right, stacks, width):
     tiles = -(-stacks // PER)
     for send, own in ((send_left, own_left), (send_right, own_right)):
         for tile in range(tiles):
@@ -215,27 +222,19 @@
             send[tiles + tile, 0:width, :] = own[at : at + width, :]
             send[tiles + tile, width + 6 : width + 16, :] = jnp.zeros((10, 128), F32)
 
-    def place(above, below):
-        for got, mass_at, coef_at in ((above, width, width), (below, width + 6, width + 3)):
-            for tile in range(tiles):
-                left, right = pack_stacks(lambda s: got[6 * s : 6 * s + 8, :], stacks, tile)
-                send_left[tile, mass_at : mass_at + 6, :] = left[0:6]
-                send_right[tile, mass_at : mass_at + 6, :] = right[0:6]
-            for tile in range(2):
-                base = 6 * stacks
-                left, right = pack_coefficients(lambda o: got[base + 3 * o : base + 3 * o + 8, :], tile)
-                send_left[tiles + tile, coef_at : coef_at + 3, :] = left[0:3]
-                send_right[tiles + tile, coef_at : coef_at + 3, :] = right[0:3]
-
-    even = is_even(ROW_AXES)
-
-    @pl.when(even)
-    def _():
-        place(got_b, got_a)
-
-    @pl.when(jnp.logical_not(even))
-    def _():
-        place(got_a, got_b)
+    first, last = ends(ROW_AXES)
+    for got, outside, mass_at, coef_at in (
+        (above, first, width, width), (below, last, width + 6, width + 3)
+    ):
+        for tile in range(tiles):
+            left, right = pack_stacks(lambda s: got[6 * s : 6 * s + 8, :], stacks, tile)
+            send_left[tile, mass_at : mass_at + 6, :] = jnp.where(outside, 0.0, left[0:6])
+            send_right[tile, mass_at : mass_at + 6, :] = jnp.where(outside, 0.0, right[0:6])
+        for tile in range(2):
+            base = 6 * stacks
+            left, right = pack_coefficients(lambda o: got[base + 3 * o : base + 3 * o + 8, :], tile)
+            send_left[tiles + tile, coef_at : coef_at + 3, :] = jnp.where(outside, 0.0, left[0:3])
+            send_right[tiles + tile, coef_at : coef_at + 3, :] = jnp.where(outside, 0.0, right[0:3])
 
 
 def choose(even, first, second, first_out, second_out):
@@ -250,9 +249,9 @@
         second_out[...] = first[...]
 
 
-def pack_all(mass, own_left, own_right, got_a, got_b, send_a, send_b, left, right):
+def pack_all(mass, own_left, own_right, above, below, send_a, send_b, left, right):
     stacks, width = mass.shape[:2]
-    join_halo(own_left, own_right, got_a, got_b, left, right, stacks, width)
+    join_halo(own_left, own_right, above, below, left, right, stacks, width)
     choose(is_even(COLUMN_AXES), right, left, send_a, send_b)
 
 
@@ -273,50 +272,20 @@
     return total
 
 
-def some_steps(field, shifted, partial, stacks, first):
-    def some_stacks(group, carry):
-        for tile in range(partial.shape[1] // 8):
-            total = main_sum(
-                lambda k, at: field[first + group * GROUP + k, at : at + 8, :], shifted, 0, tile
-            )
-            for k in range(GROUP):
-                partial[group * GROUP + k, 8 * tile : 8 * tile + 8, :] = total[k]
-        return carry
-
-    lax.fori_loop(0, stacks // GROUP, some_stacks, 0)
-
-
-def hand_on(send, got, partial, out):
-    out[...] = send[...]
-
-
-def step_one(mass, stencil, got_a, got_b, partial, wide, shifted, field):
+def step_one(mass, stencil, above, below, partial, wide, shifted, own_shifted, field):
     stacks, width = mass.shape[:2]
-
-    def place(above, below):
-        for s in range(stacks):
-            field[s, 0:6, :] = above[6 * s : 6 * s + 6, :]
-            field[s, width + 6 : width + 12, :] = below[6 * s : 6 * s + 6, :]
-        for o in range(OFFSETS):
-            at = 6 * stacks + 3 * o
-            wide[o, 0:3, :] = above[at : at + 3, :]
-            wide[o, width + 3 : width + 6, :] = below[at : at + 3, :]
-
-    even = is_even(ROW_AXES)
-
-    @pl.when(even)
-    def _():
-        place(got_b, got_a)
-
-    @pl.when(jnp.logical_not(even))
-    def _():
-        place(got_a, got_b)
-
+    first, last = ends(ROW_AXES)
     for s in range(stacks):
+        at = 6 * s
+        field[s, 0:6, :] = jnp.where(first, 0.0, above[at : at + 6, :])
         field[s, 6 : width + 6, :] = mass[s, :, :]
+        field[s, width + 6 : width + 12, :] = jnp.where(last, 0.0, below[at : at + 6, :])
         field[s, width + 12 : width + 16, :] = jnp.zeros((4, 128), F32)
     for o in range(OFFSETS):
+        at = 6 * stacks + 3 * o
+        wide[o, 0:3, :] = jnp.where(first, 0.0, above[at : at + 3, :])
         wide[o, 3 : width + 3, :] = stencil[o, :, :]
+        wide[o, width + 3 : width + 6, :] = jnp.where(last, 0.0, below[at : at + 3, :])
         wide[o, width + 6 : width + 8, :] = jnp.zeros((2, 128), F32)
     lane = lanes()
     for tile in range((width + 8) // 8):
@@ -329,14 +298,17 @@
                 values = [jnp.where(lane < 128 + dy, value, 0.0) for value in values]
             for dx in range(7):
                 shifted[dx * 7 + dy + 3, rows, :] = values[dx]
-    some_steps(field, shifted, partial, partial.shape[0], 0)
-
-
-def more_step_one(field, shifted, partial, own_shifted):
-    width = own_shifted.shape[1]
     for o in range(OFFSETS):
         own_shifted[o, :, :] = shifted[o, 3 : width + 3, :]
-    some_steps(field, shifted, partial, partial.shape[0], field.shape[0] - partial.shape[0])
+
+    def some_stacks(group, carry):
+        for tile in range(partial.shape[1] // 8):
+            total = main_sum(lambda k, at: field[group * GROUP + k, at : at + 8, :], shifted, 0, tile)
+            for k in range(GROUP):
+                partial[group * GROUP + k, 8 * tile : 8 * tile + 8, :] = total[k]
+        return carry
+
+    lax.fori_loop(0, stacks // GROUP, some_stacks, 0)
 
 
 def packed_sum(load, coef, coef_at, tile, tiles, dys):
@@ -370,8 +342,12 @@
     tiles = right_set.shape[0]
     lane = lanes()
 
-    def gather(sent_right, sent_left, from_right, from_left):
+    first, last = ends(COLUMN_AXES)
+
+    def gather(sent_right, sent_left, got_right, got_left):
         place = place_in_group(width + 16)
+        from_right = [jnp.where(last, 0.0, got_right[tile]) for tile in range(tiles + 2)]
+        from_left = [jnp.where(first, 0.0, got_left[tile]) for tile in range(tiles + 2)]
         for tile in range(tiles):
             right = jnp.where(place < 3, turn(sent_right[tile], -3), from_right[tile])
             left = jnp.where(place >= 6, turn(sent_left[tile], 3), from_left[tile])
@@ -381,9 +357,10 @@
                 target[tile, width + 6 : width + 16, :] = value[width + 6 : width + 16]
         for tile in range(2):
             for target, source in ((right_halo, from_right), (left_halo, from_left)):
-                target[tile, 3 : width + 3, :] = source[tiles + tile, 0:width, :]
-                target[tile, 0:3, :] = source[tiles + tile, width : width + 3, :]
-                target[tile, width + 3 : width + 8, :] = source[tiles + tile, width + 3 : width + 8, :]
+                value = source[tiles + tile]
+                target[tile, 3 : width + 3, :] = value[0:width]
+                target[tile, 0:3, :] = value[width : width + 3]
+                target[tile, width + 3 : width + 8, :] = value[width + 3 : width + 8]
 
     even = is_even(COLUMN_AXES)
 
@@ -427,7 +404,7 @@
 
 
 def halo_steps(
-    right_set, left_set, right_coef, left_coef, partial, more_partial, field, edges,
+    right_set, left_set, right_coef, left_coef, partial, field, edges,
     edge_one, edge_two, right_next, left_next,
 ):
     tiles = right_set.shape[0]
@@ -459,16 +436,16 @@
 
     lane = lanes()
     at_edge = (lane < 3) | (lane >= 125)
-    stacks, more = field.shape[0], partial.shape[0]
+    stacks = field.shape[0]
     for t in range(tiles):
         members = range(PER * t, min(stacks, PER * t + PER))
         for tile in range(edge_one.shape[1] // 8):
             rows = pl.ds(8 * tile, 8)
             packed = edge_one[t, rows, :]
-            values = []
-            for s in members:
-                value = partial[s, rows, :] if s < more else more_partial[s - more, rows, :]
-                values.append(value + jnp.where(at_edge, turn(packed, 125 - SPAN * (s % PER)), 0.0))
+            values = [
+                partial[s, rows, :] + jnp.where(at_edge, turn(packed, 125 - SPAN * (s % PER)), 0.0)
+                for s in members
+            ]
             for s, value in zip(members, values):
                 field[s, rows, :] = value
         for tile in range(edge_two.shape[1] // 8):
@@ -500,7 +477,7 @@
     tiles = -(-stacks // PER)
     combos = 4 * (width // 8)
 
-    mass, stencil, send_a, send_b = pl.pallas_call(
+    mass, stencil, send_down, send_up = pl.pallas_call(
         coefficients,
         out_shape=(shape(*tracer_mass.shape), shape(OFFSETS, width, 128), shape(edge, 128), shape(edge, 128)),
         in_specs=[HBM] * 5,
@@ -521,8 +498,8 @@
         pltpu.with_memory_space_constraint(value, pltpu.HBM)
         for value in (recon_table, tracer_mass, intersection_weights, intersection_cells, rotation_codes)
     ))
-    got_a = swap(send_a, ROW_AXES, False)
-    got_b = swap(send_b, ROW_AXES, True)
+    above = shift(send_down, ROW_AXES, 1)
+    below = shift(send_up, ROW_AXES, -1)
 
     tall, low = width + 16, width + 8
     picks = jax.ShapeDtypeStruct((7, 256, 256), jnp.bfloat16)
@@ -546,43 +523,24 @@
         compiler_params=params(),
         cost_estimate=cost(10**6),
         name="pack_all",
-    )(mass, own_left, own_right, got_a, got_b)
+    )(mass, own_left, own_right, above, below)
     column_a = swap(send_a, COLUMN_AXES, False)
 
-    later = GROUP * (stacks // (2 * GROUP) - 1)
-    partial, wide, shifted, field = pl.pallas_call(
+    column_b = swap(send_b, COLUMN_AXES, True)
+
+    partial, wide, shifted, own_shifted = pl.pallas_call(
         step_one,
         out_shape=(
-            shape(stacks - later, low, 128), shape(OFFSETS, low, 128), shape(OFFSETS, low, 128),
-            shape(stacks, tall, 128),
+            shape(stacks, low, 128), shape(OFFSETS, low, 128), shape(OFFSETS, low, 128),
+            shape(OFFSETS, width, 128),
         ),
         in_specs=[VMEM] * 4,
         out_specs=(VMEM,) * 4,
-        compiler_params=params(),
-        cost_estimate=cost(8 * 10**6),
+        scratch_shapes=[scratch(stacks, tall, 128)],
+        compiler_params=params(),
+        cost_estimate=cost(12 * 10**6),
         name="step_one",
-    )(mass, stencil, got_a, got_b)
-
-    send_b = pl.pallas_call(
-        hand_on,
-        out_shape=shape(*send),
-        in_specs=[VMEM, ANY, ANY],
-        out_specs=VMEM,
-        compiler_params=params(),
-        cost_estimate=cost(10**4),
-        name="hand_on",
-    )(send_b, column_a, partial)
-    column_b = swap(send_b, COLUMN_AXES, True)
-
-    more_partial, own_shifted = pl.pallas_call(
-        more_step_one,
-        out_shape=(shape(later, low, 128), shape(OFFSETS, width, 128)),
-        in_specs=[VMEM] * 2,
-        out_specs=(VMEM,) * 2,
-        compiler_params=params(),
-        cost_estimate=cost(4 * 10**6),
-        name="more_step_one",
-    )(field, shifted)
+    )(mass, stencil, above, below)
 
     sides = pl.pallas_call(
         side_coefficients,
@@ -598,13 +556,13 @@
     field, edges = pl.pallas_call(
         halo_steps,
         out_shape=(shape(stacks, low, 128), shape(stacks, width, 128)),
-        in_specs=[VMEM] * 6,
+        in_specs=[VMEM] * 5,
         out_specs=(VMEM,) * 2,
         scratch_shapes=[scratch(tiles, low, 128), scratch(tiles, width, 128)] + [scratch(tiles, low, 128)] * 2,
         compiler_params=params(),
         cost_estimate=cost(4 * 10**6),
         name="halo_steps",
-    )(*sides, partial, more_partial)
+    )(*sides, partial)
 
     return pl.pallas_call(
         step_two,

time: 26.8 us -> 23.1 us (0.86)
  the two profiles are of different devices: /device:TPU:12 before, /device:TPU:0 now
where the time goes in v1:
time: 23.1 us; the launch traced here: 22.9 us
  Pallas kernels  10.1 us (44%)
  starting transfers between devices  8.38 us (36%)
  waiting for transfers between devices  4.35 us (19%)
    ppermute x2, starting transfers between devices, swap(): return lax.ppermute(block, axes, list(enumerate(partner)))  4.92 us
    ppermute x2, starting transfers between devices, shift(): lax.ppermute(block, axes, [(index, (index + step) % count) for index in r...  3.45 us
    pallas_call x1, Pallas kernels, local(): pl.pallas_call(step_one, out_shape=(shape(stacks, low, 128), shape(OFFSET...  3.14 us
    ppermute x2, waiting for transfers between devices, shift(): lax.ppermute(block, axes, [(index, (index + step) % count) for index in r...  2.87 us
    pallas_call x1, Pallas kernels, local(): pl.pallas_call(step_two, out_shape=shape(stacks, width, columns), in_spec...  2.47 us
    pallas_call x1, Pallas kernels, local(): pl.pallas_call(coefficients, out_shape=(shape(*tracer_mass.shape), shape(...  2.23 us
    ppermute x2, waiting for transfers between devices, swap(): return lax.ppermute(block, axes, list(enumerate(partner)))  1.48 us
    pallas_call x1, Pallas kernels, local(): pl.pallas_call(halo_steps, out_shape=(shape(stacks, low, 128), shape(stac...  0.72 us
  transfers between devices with their start and end apart: 4, of which 2 were waited for; matrix products, arithmetic and copies ran while one was open for 0% of the time, Pallas kernels for 16%

profile of v1, /device:TPU:0, one launch (start us, length us, event | category | flops | bytes accessed | tf_op | source)
XLA Modules:
  0.0 22.9 jit_solution(510466376241892599)
XLA Ops:
  0.0 2.2 %coefficients.1 = (f32[40,16,128]{2,1,0:T(8,128)S(1)}, f32[49,16,128]{2,1,0:T(8,128)S(1)}, f32[392,128]{1,0:T(8,128)S(1)}, f32[392,128]{1,0:T(8,128)S(1)}) custom-call(f32[10,25]{1,0:T(8,128)} %recon_hbm.1, f32[40,16,128]{2,1,0:T(8,128)} %mass_hbm.1, f32[4,10,16,128]{3,2,1,0:T(8,128)} %weights_hbm.1, s32[4,16,128]{2,1,0:T(8,128)} %cells_hbm.1, ...), custom_call_target="tpu_custom_call" | custom-call | flops 8000000 | bytes 1048576 | tf_op jit(solution)/shard_map/coefficients/pallas_call | solution.py:480
  2.2 0.5 %collective-permute-start = (f32[392,128]{1,0:T(8,128)S(1)}, f32[392,128]{1,0:T(8,128)S(1)}, u32[]{:S(2)}, u32[]{:S(2)}) collective-permute-start(f32[392,128]{1,0:T(8,128)S(1)} %get-tuple-element.25), channel_id=1, source_target_pairs={{0,4},{4,8},{8,12},{12,16},{16,20},{20,24},{24,28},{28,0},{1,5},{5... | collective-permute-start | bytes 602120 | tf_op jit(solution)/shard_map/ppermute | solution.py:42
  2.7 2.9 %collective-permute-start.1 = (f32[392,128]{1,0:T(8,128)S(1)}, f32[392,128]{1,0:T(8,128)S(1)}, u32[]{:S(2)}, u32[]{:S(2)}) collective-permute-start(f32[392,128]{1,0:T(8,128)S(1)} %get-tuple-element.26), channel_id=1, source_target_pairs={{0,28},{4,0},{8,4},{12,8},{16,12},{20,16},{24,20},{28,24},{1,29},{... | collective-permute-start | bytes 602120 | tf_op jit(solution)/shard_map/ppermute | solution.py:42
  5.7 0.5 %pack_own.1 = (f32[80,128]{1,0:T(8,128)S(1)}, f32[80,128]{1,0:T(8,128)S(1)}, bf16[7,256,256]{2,1,0:T(8,128)(2,1)S(1)}) custom-call(f32[40,16,128]{2,1,0:T(8,128)S(1)} %get-tuple-element.23.mass, f32[49,16,128]{2,1,0:T(8,128)S(1)} %get-tuple-element.24.stencil), custom_call_target="tpu_custom_call" | custom-call | flops 1000000 | bytes 1048576 | tf_op jit(solution)/shard_map/pack_own/pallas_call | solution.py:506
  6.2 2.9 %collective-permute-done.above = f32[392,128]{1,0:T(8,128)S(1)} collective-permute-done((f32[392,128]{1,0:T(8,128)S(1)}, f32[392,128]{1,0:T(8,128)S(1)}, u32[]{:S(2)}, u32[]{:S(2)}) %collective-permute-start) | collective-permute-done | bytes 200736 | tf_op jit(solution)/shard_map/ppermute | solution.py:42
  9.1 0.0 collective-permute-done.1.below
  9.1 0.5 %pack_all.1 = (f32[5,32,128]{2,1,0:T(8,128)S(1)}, f32[5,32,128]{2,1,0:T(8,128)S(1)}) custom-call(f32[40,16,128]{2,1,0:T(8,128)S(1)} %get-tuple-element.23.mass, f32[80,128]{1,0:T(8,128)S(1)} %get-tuple-element.28.own_left, f32[80,128]{1,0:T(8,128)S(1)} %get-tuple-element.29.own_right, f32[392,128]{1,0:T(8,128)S(1)} %collective-permute-done.above, ...), custom_call_target="tpu_custom_call" | custom-call | flops 1000000 | bytes 1048576 | tf_op jit(solution)/shard_map/pack_all/pallas_call | solution.py:517
  9.5 2.5 %collective-permute-start.2 = (f32[5,32,128]{2,1,0:T(8,128)S(1)}, f32[5,32,128]{2,1,0:T(8,128)S(1)}, u32[]{:S(2)}, u32[]{:S(2)}) collective-permute-start(f32[5,32,128]{2,1,0:T(8,128)S(1)} %get-tuple-element.30.send_a), channel_id=1, source_target_pairs={{0,1},{1,0},{2,3},{3,2},{4,5},{5,4},{6,7},{7,6},{8,9},{9,8},{10,11... | collective-permute-start | bytes 245768 | tf_op jit(solution)/shard_map/ppermute | solution.py:37
  12.0 2.5 %collective-permute-start.3 = (f32[5,32,128]{2,1,0:T(8,128)S(1)}, f32[5,32,128]{2,1,0:T(8,128)S(1)}, u32[]{:S(2)}, u32[]{:S(2)}) collective-permute-start(f32[5,32,128]{2,1,0:T(8,128)S(1)} %get-tuple-element.31.send_b), channel_id=1, source_target_pairs={{0,3},{1,2},{2,1},{3,0},{4,7},{5,6},{6,5},{7,4},{8,11},{9,10},{10,... | collective-permute-start | bytes 245768 | tf_op jit(solution)/shard_map/ppermute | solution.py:37
  14.5 3.1 %step_one.1 = (f32[40,24,128]{2,1,0:T(8,128)S(1)}, f32[49,24,128]{2,1,0:T(8,128)S(1)}, f32[49,24,128]{2,1,0:T(8,128)}, f32[49,16,128]{2,1,0:T(8,128)S(1)}) custom-call(f32[40,16,128]{2,1,0:T(8,128)S(1)} %get-tuple-element.23.mass, f32[49,16,128]{2,1,0:T(8,128)S(1)} %get-tuple-element.24.stencil, f32[392,128]{1,0:T(8,128)S(1)} %collective-permute-done.above, ...), custom_call_target="tpu_custom_call" | custom-call | flops 12000000 | bytes 1048576 | tf_op jit(solution)/shard_map/step_one/pallas_call | solution.py:531
  17.6 0.0 collective-permute-done.2.got_a
  17.6 1.5 %collective-permute-done.3.got_b = f32[5,32,128]{2,1,0:T(8,128)S(1)} collective-permute-done((f32[5,32,128]{2,1,0:T(8,128)S(1)}, f32[5,32,128]{2,1,0:T(8,128)S(1)}, u32[]{:S(2)}, u32[]{:S(2)}) %collective-permute-start.3) | collective-permute-done | bytes 81952 | tf_op jit(solution)/shard_map/ppermute | solution.py:37
  19.1 0.6 %side_coefficients.1 = (f32[3,32,128]{2,1,0:T(8,128)S(1)}, f32[3,32,128]{2,1,0:T(8,128)S(1)}, f32[49,24,128]{2,1,0:T(8,128)S(1)}, f32[49,24,128]{2,1,0:T(8,128)S(1)}) custom-call(f32[49,24,128]{2,1,0:T(8,128)S(1)} %get-tuple-element.27.wide, f32[5,32,128]{2,1,0:T(8,128)S(1)} %get-tuple-element.30.send_a, f32[5,32,128]{2,1,0:T(8,128)S(1)} %get-tuple-element.31.send_b, ...), custom_call_target="tpu_custom_call" | custom-call | flops 4000000 | bytes 1048576 | tf_op jit(solution)/shard_map/side_coefficients/pallas_call | solution.py:545
  19.7 0.7 %halo_steps.1 = (f32[40,24,128]{2,1,0:T(8,128)S(1)}, f32[40,16,128]{2,1,0:T(8,128)S(1)}) custom-call(f32[3,32,128]{2,1,0:T(8,128)S(1)} %get-tuple-element.33.right_set, f32[3,32,128]{2,1,0:T(8,128)S(1)} %get-tuple-element.34.left_set, f32[49,24,128]{2,1,0:T(8,128)S(1)} %get-tuple-element.35.right_coef, f32[49,24,128]{2,1,0:T(8,128)S(1)} %get-tuple-element.36.left_coef, ...), custom_call_target="tpu_custom_call" | custom-call | flops 4000000 | bytes 1048576 | tf_op jit(solution)/shard_map/halo_steps/pallas_call | solution.py:556
  20.4 2.5 %step_two.1 = f32[40,16,128]{2,1,0:T(8,128)} custom-call(f32[40,24,128]{2,1,0:T(8,128)S(1)} %get-tuple-element.38.field, f32[49,16,128]{2,1,0:T(8,128)S(1)} %get-tuple-element.39.own_shifted, f32[40,16,128]{2,1,0:T(8,128)S(1)} %get-tuple-element.40.edges), custom_call_target="tpu_custom_call" | custom-call | flops 8000000 | bytes 1048576 | tf_op jit(solution)/shard_map/step_two/pallas_call | solution.py:567
Async XLA Ops:
  2.2 6.8 %collective-permute-start = (f32[392,128]{1,0:T(8,128)S(1)}, f32[392,128]{1,0:T(8,128)S(1)}, u32[]{:S(2)}, u32[]{:S(2)}) collective-permute-start(f32[392,128]{1,0:T(8,128)S(1)} %get-tuple-element.25), channel_id=1, source_target_pairs={{0,4},{4,8},{8,12},{12,16},{16,20},{20,24},{24,28},{28,0},{1,5},{5... | collective-permute-start | bytes 602120 | tf_op jit(solution)/shard_map/ppermute | solution.py:42
  2.7 6.3 %collective-permute-start.1 = (f32[392,128]{1,0:T(8,128)S(1)}, f32[392,128]{1,0:T(8,128)S(1)}, u32[]{:S(2)}, u32[]{:S(2)}) collective-permute-start(f32[392,128]{1,0:T(8,128)S(1)} %get-tuple-element.26), channel_id=1, source_target_pairs={{0,28},{4,0},{8,4},{12,8},{16,12},{20,16},{24,20},{28,24},{1,29},{... | collective-permute-start | bytes 602120 | tf_op jit(solution)/shard_map/ppermute | solution.py:42
  9.5 8.1 %collective-permute-start.2 = (f32[5,32,128]{2,1,0:T(8,128)S(1)}, f32[5,32,128]{2,1,0:T(8,128)S(1)}, u32[]{:S(2)}, u32[]{:S(2)}) collective-permute-start(f32[5,32,128]{2,1,0:T(8,128)S(1)} %get-tuple-element.30.send_a), channel_id=1, source_target_pairs={{0,1},{1,0},{2,3},{3,2},{4,5},{5,4},{6,7},{7,6},{8,9},{9,8},{10,11... | collective-permute-start | bytes 245768 | tf_op jit(solution)/shard_map/ppermute | solution.py:37
  12.0 7.1 %collective-permute-start.3 = (f32[5,32,128]{2,1,0:T(8,128)S(1)}, f32[5,32,128]{2,1,0:T(8,128)S(1)}, u32[]{:S(2)}, u32[]{:S(2)}) collective-permute-start(f32[5,32,128]{2,1,0:T(8,128)S(1)} %get-tuple-element.31.send_b), channel_id=1, source_target_pairs={{0,3},{1,2},{2,1},{3,0},{4,7},{5,6},{6,5},{7,4},{8,11},{9,10},{10,... | collective-permute-start | bytes 245768 | tf_op jit(solution)/shard_map/ppermute | solution.py:37

commit v2 on v1

--- a/solution.py
+++ b/solution.py
@@ -1,3 +1,5 @@
+import functools
+
 import jax
 import jax.numpy as jnp
 from jax import lax
@@ -130,25 +132,32 @@
                 stencil[ox * 7 + oy, rows, :] = total[oy]
 
 
-def coefficients(
-    recon_hbm, mass_hbm, weights_hbm, cells_hbm, codes_hbm, mass, stencil, send_down, send_up,
-    recon, weights, cells, codes, turned, spread, sems,
+def mass_rows(
+    mass_hbm, weights_hbm, cells_hbm, codes_hbm, mass, weights, cells, codes, send_down, send_up, sems
 ):
-    sources = (recon_hbm, codes_hbm, weights_hbm, cells_hbm, mass_hbm)
-    targets = (recon, codes, weights, cells, mass)
+    sources = (mass_hbm, weights_hbm, cells_hbm, codes_hbm)
+    targets = (mass, weights, cells, codes)
     copies = [pltpu.make_async_copy(a, b, sems.at[i]) for i, (a, b) in enumerate(zip(sources, targets))]
     for copy in copies:
         copy.start()
-    for copy in copies:
+    copies[0].wait()
+    stacks, width = mass.shape[:2]
+    for send, at in ((send_down, width - 6), (send_up, 0)):
+        for s in range(stacks):
+            send[6 * s : 6 * s + 6, :] = mass[s, at : at + 6, :]
+    for copy in copies[1:]:
         copy.wait()
-    stacks, width = mass.shape[:2]
+
+
+def coefficients(recon_hbm, weights, cells, codes, stencil, send_down, send_up, recon, turned, spread, sem):
+    copy = pltpu.make_async_copy(recon_hbm, recon, sem.at[0])
+    copy.start()
+    copy.wait()
+    width = stencil.shape[1]
     fill_stencil(recon, weights, cells, codes, turned, spread, stencil, width // 8)
-    for send, mass_at, stencil_at in ((send_down, width - 6, width - 3), (send_up, 0, 0)):
-        for s in range(stacks):
-            send[6 * s : 6 * s + 6, :] = mass[s, mass_at : mass_at + 6, :]
+    for send, at in ((send_down, width - 3), (send_up, 0)):
         for o in range(OFFSETS):
-            at = 6 * stacks + 3 * o
-            send[at : at + 3, :] = stencil[o, stencil_at : stencil_at + 3, :]
+            send[3 * o : 3 * o + 3, :] = stencil[o, at : at + 3, :]
 
 
 def pack_stacks(load, stacks, tile):
@@ -163,16 +172,26 @@
     return left, right
 
 
-def pack_coefficients(load, tile):
+def pack_coefficients(load):
     lane = lanes()
     left = jnp.zeros((8, 128), F32)
     right = jnp.zeros((8, 128), F32)
-    for o in range(COEF_PER * tile, min(OFFSETS, COEF_PER * tile + COEF_PER)):
-        at = 3 * (o % COEF_PER)
+    for o in range(COEF_PER):
+        at = 3 * o
         here = (lane >= at) & (lane < at + 3)
         value = load(o)
         left = jnp.where(here, turn(value, at), left)
         right = jnp.where(here, turn(value, at - 125), right)
+    return left, right
+
+
+def add_spare(load, left, right):
+    lane = lanes()
+    for o in range(COEF_PER, OFFSETS):
+        at = SPAN * (o - COEF_PER)
+        value = load(o)
+        left = jnp.where((lane >= at) & (lane < at + 3), turn(value, at), left)
+        right = jnp.where((lane >= at + 6) & (lane < at + 9), turn(value, at - 119), right)
     return left, right
 
 
@@ -201,40 +220,50 @@
         rows = pl.ds(8 * half, 8)
         for tile in range(tiles):
             at = width * tile + 8 * half
-            left[at : at + 8, :], right[at : at + 8, :] = pack_stacks(
-                lambda s: mass[s, rows, :], stacks, tile
-            )
-        for tile in range(2):
-            at = width * (tiles + tile) + 8 * half
-            left[at : at + 8, :], right[at : at + 8, :] = pack_coefficients(
-                lambda o: stencil[o, rows, :], tile
-            )
-
-
-def join_halo(own_left, own_right, above, below, send_left, send_right, stacks, width):
+            values = pack_stacks(lambda s: mass[s, rows, :], stacks, tile)
+            if tile == 0:
+                values = add_spare(lambda o: stencil[o, rows, :], *values)
+            left[at : at + 8, :], right[at : at + 8, :] = values
+        at = width * tiles + 8 * half
+        left[at : at + 8, :], right[at : at + 8, :] = pack_coefficients(lambda o: stencil[o, rows, :])
+
+
+def pack_mass(own_left, own_right, above, below, left, right):
+    stacks = (above.shape[0] - 8) // 6
     tiles = -(-stacks // PER)
-    for send, own in ((send_left, own_left), (send_right, own_right)):
+    width = own_left.shape[0] // (tiles + 1)
+    tall = width + 12
+    for send, own in ((left, own_left), (right, own_right)):
+        for tile in range(tiles + 1):
+            send[tall * tile : tall * tile + width, :] = own[width * tile : width * tile + width, :]
+        end = tall * tiles + width + 6
+        send[end:, :] = jnp.zeros((send.shape[0] - end, 128), F32)
+    first, last = ends(ROW_AXES)
+    for got, outside, place in ((above, first, width), (below, last, width + 6)):
         for tile in range(tiles):
-            send[tile, 0:width, :] = own[width * tile : width * tile + width, :]
-            send[tile, width + 12 : width + 16, :] = jnp.zeros((4, 128), F32)
-        for tile in range(2):
-            at = width * (tiles + tile)
-            send[tiles + tile, 0:width, :] = own[at : at + width, :]
-            send[tiles + tile, width + 6 : width + 16, :] = jnp.zeros((10, 128), F32)
-
+            at = tall * tile + place
+            packed = pack_stacks(lambda s: got[6 * s : 6 * s + 8, :], stacks, tile)
+            left[at : at + 6, :] = jnp.where(outside, 0.0, packed[0][0:6])
+            right[at : at + 6, :] = jnp.where(outside, 0.0, packed[1][0:6])
+
+
+def pack_all(width, mass_left, mass_right, above, below, send_a, send_b, left, right):
+    left[...] = mass_left[...]
+    right[...] = mass_right[...]
+    coef_at = left.shape[0] - (width + 12)
     first, last = ends(ROW_AXES)
-    for got, outside, mass_at, coef_at in (
+    for got, outside, mass_at, place in (
         (above, first, width, width), (below, last, width + 6, width + 3)
     ):
-        for tile in range(tiles):
-            left, right = pack_stacks(lambda s: got[6 * s : 6 * s + 8, :], stacks, tile)
-            send_left[tile, mass_at : mass_at + 6, :] = jnp.where(outside, 0.0, left[0:6])
-            send_right[tile, mass_at : mass_at + 6, :] = jnp.where(outside, 0.0, right[0:6])
-        for tile in range(2):
-            base = 6 * stacks
-            left, right = pack_coefficients(lambda o: got[base + 3 * o : base + 3 * o + 8, :], tile)
-            send_left[tiles + tile, coef_at : coef_at + 3, :] = jnp.where(outside, 0.0, left[0:3])
-            send_right[tiles + tile, coef_at : coef_at + 3, :] = jnp.where(outside, 0.0, right[0:3])
+        load = lambda o: jnp.where(outside, 0.0, got[3 * o : 3 * o + 8, :])
+        at = coef_at + place
+        packed = pack_coefficients(load)
+        left[at : at + 3, :] = packed[0][0:3]
+        right[at : at + 3, :] = packed[1][0:3]
+        packed = add_spare(load, left[mass_at : mass_at + 8, :], right[mass_at : mass_at + 8, :])
+        left[mass_at : mass_at + 3, :] = packed[0][0:3]
+        right[mass_at : mass_at + 3, :] = packed[1][0:3]
+    choose(is_even(COLUMN_AXES), right, left, send_a, send_b)
 
 
 def choose(even, first, second, first_out, second_out):
@@ -247,12 +276,6 @@
     def _():
         first_out[...] = second[...]
         second_out[...] = first[...]
-
-
-def pack_all(mass, own_left, own_right, above, below, send_a, send_b, left, right):
-    stacks, width = mass.shape[:2]
-    join_halo(own_left, own_right, above, below, left, right, stacks, width)
-    choose(is_even(COLUMN_AXES), right, left, send_a, send_b)
 
 
 def main_sum(load, coef, coef_at, tile):
@@ -272,7 +295,7 @@
     return total
 
 
-def step_one(mass, stencil, above, below, partial, wide, shifted, own_shifted, field):
+def step_one(mass, stencil, above, below, coef_above, coef_below, partial, wide, shifted, own_shifted, field):
     stacks, width = mass.shape[:2]
     first, last = ends(ROW_AXES)
     for s in range(stacks):
@@ -282,10 +305,10 @@
         field[s, width + 6 : width + 12, :] = jnp.where(last, 0.0, below[at : at + 6, :])
         field[s, width + 12 : width + 16, :] = jnp.zeros((4, 128), F32)
     for o in range(OFFSETS):
-        at = 6 * stacks + 3 * o
-        wide[o, 0:3, :] = jnp.where(first, 0.0, above[at : at + 3, :])
+        at = 3 * o
+        wide[o, 0:3, :] = jnp.where(first, 0.0, coef_above[at : at + 3, :])
         wide[o, 3 : width + 3, :] = stencil[o, :, :]
-        wide[o, width + 3 : width + 6, :] = jnp.where(last, 0.0, below[at : at + 3, :])
+        wide[o, width + 3 : width + 6, :] = jnp.where(last, 0.0, coef_below[at : at + 3, :])
         wide[o, width + 6 : width + 8, :] = jnp.zeros((2, 128), F32)
     lane = lanes()
     for tile in range((width + 8) // 8):
@@ -345,22 +368,33 @@
     first, last = ends(COLUMN_AXES)
 
     def gather(sent_right, sent_left, got_right, got_left):
-        place = place_in_group(width + 16)
-        from_right = [jnp.where(last, 0.0, got_right[tile]) for tile in range(tiles + 2)]
-        from_left = [jnp.where(first, 0.0, got_left[tile]) for tile in range(tiles + 2)]
-        for tile in range(tiles):
-            right = jnp.where(place < 3, turn(sent_right[tile], -3), from_right[tile])
-            left = jnp.where(place >= 6, turn(sent_left[tile], 3), from_left[tile])
+        part = width + 12
+        place = place_in_group(part)
+        rows = [slice(part * tile, part * tile + part) for tile in range(tiles)]
+        from_right = [jnp.where(last, 0.0, got_right[at, :]) for at in rows]
+        from_left = [jnp.where(first, 0.0, got_left[at, :]) for at in rows]
+        for tile, at in enumerate(rows):
+            right = jnp.where(place < 3, turn(sent_right[at, :], -3), from_right[tile])
+            left = jnp.where(place >= 6, turn(sent_left[at, :], 3), from_left[tile])
             for target, value in ((right_set, right), (left_set, left)):
                 target[tile, 6 : width + 6, :] = value[0:width]
                 target[tile, 0:6, :] = value[width : width + 6]
-                target[tile, width + 6 : width + 16, :] = value[width + 6 : width + 16]
-        for tile in range(2):
-            for target, source in ((right_halo, from_right), (left_halo, from_left)):
-                value = source[tiles + tile]
-                target[tile, 3 : width + 3, :] = value[0:width]
-                target[tile, 0:3, :] = value[width : width + 3]
-                target[tile, width + 3 : width + 8, :] = value[width + 3 : width + 8]
+                target[tile, width + 6 : width + 12, :] = value[width + 6 : width + 12]
+                target[tile, width + 12 : width + 16, :] = jnp.zeros((4, 128), F32)
+        coefs = slice(part * tiles, part * tiles + width + 6)
+        for target, source, got, outside in (
+            (right_halo, from_right, got_right, last), (left_halo, from_left, got_left, first)
+        ):
+            value = jnp.where(outside, 0.0, got[coefs, :])
+            spare = source[0]
+            for tile, own, above, below in (
+                (0, value[0:width], value[width : width + 3], value[width + 3 : width + 6]),
+                (1, spare[0:width], spare[width : width + 3], spare[width + 6 : width + 9]),
+            ):
+                target[tile, 3 : width + 3, :] = own
+                target[tile, 0:3, :] = above
+                target[tile, width + 3 : width + 6, :] = below
+                target[tile, width + 6 : width + 8, :] = jnp.zeros((2, 128), F32)
 
     even = is_even(COLUMN_AXES)
 
@@ -382,9 +416,13 @@
             values = []
             for dx in range(7):
                 o = dx * 7 + dy
-                at = 3 * (o % COEF_PER)
-                right = turn(right_rows[o // COEF_PER], 60 - at)
-                left = turn(left_rows[o // COEF_PER], 64 - at)
+                if o < COEF_PER:
+                    right = turn(right_rows[0], 60 - 3 * o)
+                    left = turn(left_rows[0], 64 - 3 * o)
+                else:
+                    at = SPAN * (o - COEF_PER)
+                    right = turn(right_rows[1], 60 - at)
+                    left = turn(left_rows[1], 58 - at)
                 values.append(
                     jnp.where(from_right, right, jnp.where(from_left, left, wide[o, rows, :]))
                 )
@@ -456,7 +494,13 @@
                 edges[s, rows, :] = value
 
 
-def step_two(field, own_shifted, edges, out):
+def step_two(field, own_shifted, edges, out_hbm, out, sems):
+    groups = out.shape[0] // GROUP
+
+    def piece(group):
+        stacks = pl.ds(group * GROUP, GROUP)
+        return pltpu.make_async_copy(out.at[stacks], out_hbm.at[stacks], sems.at[group])
+
     def some_stacks(group, carry):
         for tile in range(out.shape[1] // 8):
             total = main_sum(lambda k, at: field[group * GROUP + k, at : at + 8, :], own_shifted, 0, tile)
@@ -464,48 +508,63 @@
             values = [total[k] + edges[group * GROUP + k, rows, :] for k in range(GROUP)]
             for k in range(GROUP):
                 out[group * GROUP + k, rows, :] = values[k]
+        piece(group).start()
         return carry
 
-    lax.fori_loop(0, out.shape[0] // GROUP, some_stacks, 0)
+    lax.fori_loop(0, groups, some_stacks, 0)
+    for group in range(groups):
+        piece(group).wait()
 
 
 def local(tracer_mass, recon_table, intersection_weights, intersection_cells, rotation_codes):
     stacks, width, columns = tracer_mass.shape
     shape = lambda *sizes: jax.ShapeDtypeStruct(sizes, F32)
     scratch = lambda *sizes: pltpu.VMEM(sizes, F32)
-    edge = -(-(6 * stacks + 3 * OFFSETS) // 8) * 8
     tiles = -(-stacks // PER)
     combos = 4 * (width // 8)
-
-    mass, stencil, send_down, send_up = pl.pallas_call(
+    tall, low = width + 16, width + 8
+    fixed = lambda *values: [pltpu.with_memory_space_constraint(value, pltpu.HBM) for value in values]
+    whole = lambda value: jax.ShapeDtypeStruct(value.shape, value.dtype)
+    mass_edge, coef_edge = 6 * stacks + 8, -(-(3 * OFFSETS + 5) // 8) * 8
+
+    mass, weights, cells, codes, mass_down, mass_up = pl.pallas_call(
+        mass_rows,
+        out_shape=(
+            whole(tracer_mass), whole(intersection_weights), whole(intersection_cells),
+            whole(rotation_codes), shape(mass_edge, 128), shape(mass_edge, 128),
+        ),
+        in_specs=[HBM] * 4,
+        out_specs=(VMEM,) * 6,
+        scratch_shapes=[pltpu.SemaphoreType.DMA((4,))],
+        compiler_params=params(),
+        cost_estimate=cost(10**6),
+        name="mass_rows",
+    )(*fixed(tracer_mass, intersection_weights, intersection_cells, rotation_codes))
+    above = shift(mass_down, ROW_AXES, 1)
+    below = shift(mass_up, ROW_AXES, -1)
+
+    stencil, coef_down, coef_up = pl.pallas_call(
         coefficients,
-        out_shape=(shape(*tracer_mass.shape), shape(OFFSETS, width, 128), shape(edge, 128), shape(edge, 128)),
-        in_specs=[HBM] * 5,
-        out_specs=(VMEM,) * 4,
+        out_shape=(shape(OFFSETS, width, 128), shape(coef_edge, 128), shape(coef_edge, 128)),
+        in_specs=[HBM] + [VMEM] * 3,
+        out_specs=(VMEM,) * 3,
         scratch_shapes=[
             pltpu.SMEM(recon_table.shape, F32),
-            scratch(*intersection_weights.shape),
-            pltpu.VMEM(intersection_cells.shape, jnp.int32),
-            pltpu.VMEM(rotation_codes.shape, jnp.int32),
             scratch(TERMS, combos, 8, 128),
             scratch(25, combos, 8, 128),
-            pltpu.SemaphoreType.DMA((5,)),
+            pltpu.SemaphoreType.DMA((1,)),
         ],
         compiler_params=params(),
         cost_estimate=cost(8 * 10**6),
         name="coefficients",
-    )(*(
-        pltpu.with_memory_space_constraint(value, pltpu.HBM)
-        for value in (recon_table, tracer_mass, intersection_weights, intersection_cells, rotation_codes)
-    ))
-    above = shift(send_down, ROW_AXES, 1)
-    below = shift(send_up, ROW_AXES, -1)
-
-    tall, low = width + 16, width + 8
+    )(*fixed(recon_table), weights, cells, codes)
+    coef_above = shift(coef_down, ROW_AXES, 1)
+    coef_below = shift(coef_up, ROW_AXES, -1)
+
     picks = jax.ShapeDtypeStruct((7, 256, 256), jnp.bfloat16)
     own_left, own_right, picks = pl.pallas_call(
         pack_own,
-        out_shape=(shape(width * (tiles + 2), 128),) * 2 + (picks,),
+        out_shape=(shape(width * (tiles + 1), 128),) * 2 + (picks,),
         in_specs=[VMEM] * 2,
         out_specs=(VMEM,) * 3,
         compiler_params=params(),
@@ -513,19 +572,27 @@
         name="pack_own",
     )(mass, stencil)
 
-    send = (tiles + 2, tall, 128)
+    send = ((width + 12) * (tiles + 1), 128)
+    mass_left, mass_right = pl.pallas_call(
+        pack_mass,
+        out_shape=(shape(*send),) * 2,
+        in_specs=[VMEM] * 4,
+        out_specs=(VMEM,) * 2,
+        compiler_params=params(),
+        cost_estimate=cost(10**6),
+        name="pack_mass",
+    )(own_left, own_right, above, below)
     send_a, send_b = pl.pallas_call(
-        pack_all,
+        functools.partial(pack_all, width),
         out_shape=(shape(*send),) * 2,
-        in_specs=[VMEM] * 5,
+        in_specs=[VMEM] * 4,
         out_specs=(VMEM,) * 2,
         scratch_shapes=[scratch(*send)] * 2,
         compiler_params=params(),
         cost_estimate=cost(10**6),
         name="pack_all",
-    )(mass, own_left, own_right, above, below)
+    )(mass_left, mass_right, coef_above, coef_below)
     column_a = swap(send_a, COLUMN_AXES, False)
-
     column_b = swap(send_b, COLUMN_AXES, True)
 
     partial, wide, shifted, own_shifted = pl.pallas_call(
@@ -534,13 +601,13 @@
             shape(stacks, low, 128), shape(OFFSETS, low, 128), shape(OFFSETS, low, 128),
             shape(OFFSETS, width, 128),
         ),
-        in_specs=[VMEM] * 4,
+        in_specs=[VMEM] * 6,
         out_specs=(VMEM,) * 4,
         scratch_shapes=[scratch(stacks, tall, 128)],
         compiler_params=params(),
         cost_estimate=cost(12 * 10**6),
         name="step_one",
-    )(mass, stencil, above, below)
+    )(mass, stencil, above, below, coef_above, coef_below)
 
     sides = pl.pallas_call(
         side_coefficients,
@@ -568,7 +635,8 @@
         step_two,
         out_shape=shape(stacks, width, columns),
         in_specs=[VMEM] * 3,
-        out_specs=VMEM,
+        out_specs=HBM,
+        scratch_shapes=[scratch(stacks, width, columns), pltpu.SemaphoreType.DMA((stacks // GROUP,))],
         compiler_params=params(),
         cost_estimate=cost(8 * 10**6),
         name="step_two",

time: 23.1 us -> 23.9 us (1.035)
  starting transfers between devices: 8.38 us -> 11 us
  waiting for transfers between devices: 4.35 us -> 1.82 us
  Pallas kernels: 10.1 us -> 10.8 us
    ppermute x2 -> x4, starting transfers between devices: 3.45 us -> 6.14 us  [shift(): lax.ppermute(block, axes, [(index, (index + step) % count) for index in r...]
    ppermute x2 -> x4, waiting for transfers between devices: 2.87 us -> 1.32 us  [shift(): lax.ppermute(block, axes, [(index, (index + step) % count) for index in r...]
    ppermute x2, waiting for transfers between devices: 1.48 us -> 0.49 us  [swap(): return lax.ppermute(block, axes, list(enumerate(partner)))]
    pallas_call x3 -> x5, Pallas kernels: 3.19 us -> 3.93 us  [the longest x1 1.8 us: local(): pl.pallas_call(coefficients, out_shape=(shape(OFFSETS, width, 128), shape...]
  transfers between devices with their start and end apart: 4 -> 6, of which waited for: 2 -> 2; matrix products, arithmetic and copies ran while one was open for 0% -> 0% of each run, Pallas kernels for 16% -> 24%
where the time goes in v2:
time: 23.9 us; the launch traced here: 23.8 us
  starting transfers between devices  11 us (46%)
  Pallas kernels  10.8 us (45%)
  waiting for transfers between devices  1.82 us (8%)
    ppermute x4, starting transfers between devices, shift(): lax.ppermute(block, axes, [(index, (index + step) % count) for index in r...  6.14 us
    ppermute x2, starting transfers between devices, swap(): return lax.ppermute(block, axes, list(enumerate(partner)))  4.89 us
    pallas_call x1, Pallas kernels, local(): pl.pallas_call(step_one, out_shape=(shape(stacks, low, 128), shape(OFFSET...  3.15 us
    pallas_call x1, Pallas kernels, local(): pl.pallas_call(step_two, out_shape=shape(stacks, width, columns), in_spec...  2.44 us
    pallas_call x1, Pallas kernels, local(): pl.pallas_call(coefficients, out_shape=(shape(OFFSETS, width, 128), shape...  1.8 us
    ppermute x4, waiting for transfers between devices, shift(): lax.ppermute(block, axes, [(index, (index + step) % count) for index in r...  1.32 us
    pallas_call x1, Pallas kernels, local(): pl.pallas_call(mass_rows, out_shape=(whole(tracer_mass), whole(intersecti...  1.11 us
    pallas_call x1, Pallas kernels, local(): pl.pallas_call(halo_steps, out_shape=(shape(stacks, low, 128), shape(stac...  0.73 us
  transfers between devices with their start and end apart: 6, of which 2 were waited for; matrix products, arithmetic and copies ran while one was open for 0% of the time, Pallas kernels for 24%

profile of v2, /device:TPU:0, one launch (start us, length us, event | category | flops | bytes accessed | tf_op | source)
XLA Modules:
  0.0 23.8 jit_solution(5273273962427779647)
XLA Ops:
  0.0 1.1 %mass_rows.1 = (f32[40,16,128]{2,1,0:T(8,128)S(1)}, f32[4,10,16,128]{3,2,1,0:T(8,128)S(1)}, s32[4,16,128]{2,1,0:T(8,128)S(1)}, s32[4,16,128]{2,1,0:T(8,128)S(1)}...) custom-call(f32[40,16,128]{2,1,0:T(8,128)} %mass_hbm.1, f32[4,10,16,128]{3,2,1,0:T(8,128)} %weights_hbm.1, ...), custom_call_target="tpu_custom_call" | custom-call | flops 1000000 | bytes 1048576 | tf_op jit(solution)/shard_map/mass_rows/pallas_call | solution.py:530
  1.1 0.5 %collective-permute-start = (f32[248,128]{1,0:T(8,128)S(1)}, f32[248,128]{1,0:T(8,128)S(1)}, u32[]{:S(2)}, u32[]{:S(2)}) collective-permute-start(f32[248,128]{1,0:T(8,128)S(1)} %get-tuple-element.35), channel_id=1, source_target_pairs={{0,4},{4,8},{8,12},{12,16},{16,20},{20,24},{24,28},{28,0},{1,5},{5... | collective-permute-start | bytes 380936 | tf_op jit(solution)/shard_map/ppermute | solution.py:44
  1.6 2.9 %collective-permute-start.1 = (f32[248,128]{1,0:T(8,128)S(1)}, f32[248,128]{1,0:T(8,128)S(1)}, u32[]{:S(2)}, u32[]{:S(2)}) collective-permute-start(f32[248,128]{1,0:T(8,128)S(1)} %get-tuple-element.36), channel_id=1, source_target_pairs={{0,28},{4,0},{8,4},{12,8},{16,12},{20,16},{24,20},{28,24},{1,29},{... | collective-permute-start | bytes 380936 | tf_op jit(solution)/shard_map/ppermute | solution.py:44
  4.6 1.8 %coefficients.1 = (f32[49,16,128]{2,1,0:T(8,128)S(1)}, f32[152,128]{1,0:T(8,128)S(1)}, f32[152,128]{1,0:T(8,128)S(1)}) custom-call(f32[10,25]{1,0:T(8,128)} %recon_hbm.1, f32[4,10,16,128]{3,2,1,0:T(8,128)S(1)} %get-tuple-element.31.weights, s32[4,16,128]{2,1,0:T(8,128)S(1)} %get-tuple-element.32.cells, s32[4,16,128]{2,1,0:T(8,128)S(1)} %get-tuple-element.33.codes), custom_call_target="tpu_custom_call" | custom-call | flops 8000000 | bytes 1048576 | tf_op jit(solution)/shard_map/coefficients/pallas_call | solution.py:546
  6.4 0.1 collective-permute-start.2
  6.4 2.6 %collective-permute-start.3 = (f32[152,128]{1,0:T(8,128)S(1)}, f32[152,128]{1,0:T(8,128)S(1)}, u32[]{:S(2)}, u32[]{:S(2)}) collective-permute-start(f32[152,128]{1,0:T(8,128)S(1)} %get-tuple-element.38), channel_id=1, source_target_pairs={{0,28},{4,0},{8,4},{12,8},{16,12},{20,16},{24,20},{28,24},{1,29},{... | collective-permute-start | bytes 233480 | tf_op jit(solution)/shard_map/ppermute | solution.py:44
  9.1 0.5 %pack_own.1 = (f32[64,128]{1,0:T(8,128)S(1)}, f32[64,128]{1,0:T(8,128)S(1)}, bf16[7,256,256]{2,1,0:T(8,128)(2,1)S(1)}) custom-call(f32[40,16,128]{2,1,0:T(8,128)S(1)} %get-tuple-element.30.mass, f32[49,16,128]{2,1,0:T(8,128)S(1)} %get-tuple-element.34.stencil), custom_call_target="tpu_custom_call" | custom-call | flops 1000000 | bytes 1048576 | tf_op jit(solution)/shard_map/pack_own/pallas_call | solution.py:565
  9.6 0.0 collective-permute-done.above
  9.6 0.0 collective-permute-done.1.below
  9.6 0.2 pack_mass.1
  9.8 1.3 %collective-permute-done.2.coef_above.above = f32[152,128]{1,0:T(8,128)S(1)} collective-permute-done((f32[152,128]{1,0:T(8,128)S(1)}, f32[152,128]{1,0:T(8,128)S(1)}, u32[]{:S(2)}, u32[]{:S(2)}) %collective-permute-start.2) | collective-permute-done | bytes 77856 | tf_op jit(solution)/shard_map/ppermute | solution.py:44
  11.2 0.0 collective-permute-done.3.coef_below.below
  11.2 0.3 %pack_all.1 = (f32[112,128]{1,0:T(8,128)S(1)}, f32[112,128]{1,0:T(8,128)S(1)}) custom-call(f32[112,128]{1,0:T(8,128)S(1)} %get-tuple-element.42.mass_left, f32[112,128]{1,0:T(8,128)S(1)} %get-tuple-element.43.mass_right, f32[152,128]{1,0:T(8,128)S(1)} %collective-permute-done.2.coef_above.above, f32[152,128]{1,0:T(8,128)S(1)} %collective-permute-done.3.coef_below.below), custom_call_target="tpu_custom_call" | custom-call | flops 1000000 | bytes 1048576 | tf_op jit(solution)/shard_map/pack_all/pallas_call | solution.py:585
  11.5 2.4 %collective-permute-start.4 = (f32[112,128]{1,0:T(8,128)S(1)}, f32[112,128]{1,0:T(8,128)S(1)}, u32[]{:S(2)}, u32[]{:S(2)}) collective-permute-start(f32[112,128]{1,0:T(8,128)S(1)} %get-tuple-element.44.send_a), channel_id=1, source_target_pairs={{0,1},{1,0},{2,3},{3,2},{4,5},{5,4},{6,7},{7,6},{8,9},{9,8},{10,11... | collective-permute-start | bytes 172040 | tf_op jit(solution)/shard_map/ppermute | solution.py:39
  13.9 2.5 %collective-permute-start.5 = (f32[112,128]{1,0:T(8,128)S(1)}, f32[112,128]{1,0:T(8,128)S(1)}, u32[]{:S(2)}, u32[]{:S(2)}) collective-permute-start(f32[112,128]{1,0:T(8,128)S(1)} %get-tuple-element.45.send_b), channel_id=1, source_target_pairs={{0,3},{1,2},{2,1},{3,0},{4,7},{5,6},{6,5},{7,4},{8,11},{9,10},{10,... | collective-permute-start | bytes 172040 | tf_op jit(solution)/shard_map/ppermute | solution.py:39
  16.3 3.1 %step_one.1 = (f32[40,24,128]{2,1,0:T(8,128)S(1)}, f32[49,24,128]{2,1,0:T(8,128)S(1)}, f32[49,24,128]{2,1,0:T(8,128)}, f32[49,16,128]{2,1,0:T(8,128)S(1)}) custom-call(f32[40,16,128]{2,1,0:T(8,128)S(1)} %get-tuple-element.30.mass, f32[49,16,128]{2,1,0:T(8,128)S(1)} %get-tuple-element.34.stencil, f32[248,128]{1,0:T(8,128)S(1)} %collective-permute-done.above, ...), custom_call_target="tpu_custom_call" | custom-call | flops 12000000 | bytes 1048576 | tf_op jit(solution)/shard_map/step_one/pallas_call | solution.py:598
  19.5 0.0 collective-permute-done.4.got_a
  19.5 0.5 %collective-permute-done.5.got_b = f32[112,128]{1,0:T(8,128)S(1)} collective-permute-done((f32[112,128]{1,0:T(8,128)S(1)}, f32[112,128]{1,0:T(8,128)S(1)}, u32[]{:S(2)}, u32[]{:S(2)}) %collective-permute-start.5) | collective-permute-done | bytes 57376 | tf_op jit(solution)/shard_map/ppermute | solution.py:39
  20.0 0.6 %side_coefficients.1 = (f32[3,32,128]{2,1,0:T(8,128)S(1)}, f32[3,32,128]{2,1,0:T(8,128)S(1)}, f32[49,24,128]{2,1,0:T(8,128)S(1)}, f32[49,24,128]{2,1,0:T(8,128)S(1)}) custom-call(f32[49,24,128]{2,1,0:T(8,128)S(1)} %get-tuple-element.39.wide, f32[112,128]{1,0:T(8,128)S(1)} %get-tuple-element.44.send_a, f32[112,128]{1,0:T(8,128)S(1)} %get-tuple-element.45.send_b, ...), custom_call_target="tpu_custom_call" | custom-call | flops 4000000 | bytes 1048576 | tf_op jit(solution)/shard_map/side_coefficients/pallas_call | solution.py:612
  20.6 0.7 %halo_steps.1 = (f32[40,24,128]{2,1,0:T(8,128)S(1)}, f32[40,16,128]{2,1,0:T(8,128)S(1)}) custom-call(f32[3,32,128]{2,1,0:T(8,128)S(1)} %get-tuple-element.47.right_set, f32[3,32,128]{2,1,0:T(8,128)S(1)} %get-tuple-element.48.left_set, f32[49,24,128]{2,1,0:T(8,128)S(1)} %get-tuple-element.49.right_coef, f32[49,24,128]{2,1,0:T(8,128)S(1)} %get-tuple-element.50.left_coef, ...), custom_call_target="tpu_custom_call" | custom-call | flops 4000000 | bytes 1048576 | tf_op jit(solution)/shard_map/halo_steps/pallas_call | solution.py:623
  21.3 2.4 %step_two.1 = f32[40,16,128]{2,1,0:T(8,128)} custom-call(f32[40,24,128]{2,1,0:T(8,128)S(1)} %get-tuple-element.52.field, f32[49,16,128]{2,1,0:T(8,128)S(1)} %get-tuple-element.53.own_shifted, f32[40,16,128]{2,1,0:T(8,128)S(1)} %get-tuple-element.54.edges), custom_call_target="tpu_custom_call" | custom-call | flops 8000000 | bytes 1048576 | tf_op jit(solution)/shard_map/step_two/pallas_call | solution.py:634
Async XLA Ops:
  1.1 8.5 %collective-permute-start = (f32[248,128]{1,0:T(8,128)S(1)}, f32[248,128]{1,0:T(8,128)S(1)}, u32[]{:S(2)}, u32[]{:S(2)}) collective-permute-start(f32[248,128]{1,0:T(8,128)S(1)} %get-tuple-element.35), channel_id=1, source_target_pairs={{0,4},{4,8},{8,12},{12,16},{16,20},{20,24},{24,28},{28,0},{1,5},{5... | collective-permute-start | bytes 380936 | tf_op jit(solution)/shard_map/ppermute | solution.py:44
  1.6 8.0 %collective-permute-start.1 = (f32[248,128]{1,0:T(8,128)S(1)}, f32[248,128]{1,0:T(8,128)S(1)}, u32[]{:S(2)}, u32[]{:S(2)}) collective-permute-start(f32[248,128]{1,0:T(8,128)S(1)} %get-tuple-element.36), channel_id=1, source_target_pairs={{0,28},{4,0},{8,4},{12,8},{16,12},{20,16},{24,20},{28,24},{1,29},{... | collective-permute-start | bytes 380936 | tf_op jit(solution)/shard_map/ppermute | solution.py:44
  6.4 4.8 %collective-permute-start.2 = (f32[152,128]{1,0:T(8,128)S(1)}, f32[152,128]{1,0:T(8,128)S(1)}, u32[]{:S(2)}, u32[]{:S(2)}) collective-permute-start(f32[152,128]{1,0:T(8,128)S(1)} %get-tuple-element.37), channel_id=1, source_target_pairs={{0,4},{4,8},{8,12},{12,16},{16,20},{20,24},{24,28},{28,0},{1,5},{5... | collective-permute-start | bytes 233480 | tf_op jit(solution)/shard_map/ppermute | solution.py:44
  6.4 4.7 %collective-permute-start.3 = (f32[152,128]{1,0:T(8,128)S(1)}, f32[152,128]{1,0:T(8,128)S(1)}, u32[]{:S(2)}, u32[]{:S(2)}) collective-permute-start(f32[152,128]{1,0:T(8,128)S(1)} %get-tuple-element.38), channel_id=1, source_target_pairs={{0,28},{4,0},{8,4},{12,8},{16,12},{20,16},{24,20},{28,24},{1,29},{... | collective-permute-start | bytes 233480 | tf_op jit(solution)/shard_map/ppermute | solution.py:44
  11.5 8.0 %collective-permute-start.4 = (f32[112,128]{1,0:T(8,128)S(1)}, f32[112,128]{1,0:T(8,128)S(1)}, u32[]{:S(2)}, u32[]{:S(2)}) collective-permute-start(f32[112,128]{1,0:T(8,128)S(1)} %get-tuple-element.44.send_a), channel_id=1, source_target_pairs={{0,1},{1,0},{2,3},{3,2},{4,5},{5,4},{6,7},{7,6},{8,9},{9,8},{10,11... | collective-permute-start | bytes 172040 | tf_op jit(solution)/shard_map/ppermute | solution.py:39
  13.9 6.1 %collective-permute-start.5 = (f32[112,128]{1,0:T(8,128)S(1)}, f32[112,128]{1,0:T(8,128)S(1)}, u32[]{:S(2)}, u32[]{:S(2)}) collective-permute-start(f32[112,128]{1,0:T(8,128)S(1)} %get-tuple-element.45.send_b), channel_id=1, source_target_pairs={{0,3},{1,2},{2,1},{3,0},{4,7},{5,6},{6,5},{7,4},{8,11},{9,10},{10,... | collective-permute-start | bytes 172040 | tf_op jit(solution)/shard_map/ppermute | solution.py:39

commit v3 on v2

--- a/solution.py
+++ b/solution.py
@@ -2,6 +2,7 @@
 
 import jax
 import jax.numpy as jnp
+import numpy as np
 from jax import lax
 from jax.experimental import pallas as pl
 from jax.experimental.pallas import tpu as pltpu
@@ -19,6 +20,7 @@
 PER = 14
 COEF_PER = 42
 VMEM = pl.BlockSpec(memory_space=pltpu.VMEM)
+ANY = pl.BlockSpec(memory_space=pl.ANY)
 HBM = pl.BlockSpec(memory_space=pltpu.HBM)
 
 
@@ -132,32 +134,37 @@
                 stencil[ox * 7 + oy, rows, :] = total[oy]
 
 
-def mass_rows(
-    mass_hbm, weights_hbm, cells_hbm, codes_hbm, mass, weights, cells, codes, send_down, send_up, sems
+def edge_rows(
+    recon_hbm, mass_hbm, weights_hbm, cells_hbm, codes_hbm,
+    mass, weights, cells, codes, send_down, send_up,
+    recon, edge_weights, edge_cells, edge_codes, edge_stencil, turned, spread, sems,
 ):
-    sources = (mass_hbm, weights_hbm, cells_hbm, codes_hbm)
-    targets = (mass, weights, cells, codes)
+    sources = (recon_hbm, codes_hbm, weights_hbm, cells_hbm, mass_hbm)
+    targets = (recon, codes, weights, cells, mass)
     copies = [pltpu.make_async_copy(a, b, sems.at[i]) for i, (a, b) in enumerate(zip(sources, targets))]
     for copy in copies:
         copy.start()
-    copies[0].wait()
+    for copy in copies:
+        copy.wait()
     stacks, width = mass.shape[:2]
-    for send, at in ((send_down, width - 6), (send_up, 0)):
+    for target, source in ((edge_weights, weights), (edge_cells, cells), (edge_codes, codes)):
+        for index in np.ndindex(*source.shape[:-2]):
+            target[index + (slice(0, 3), slice(None))] = source[index + (slice(0, 3), slice(None))]
+            target[index + (slice(3, 8), slice(None))] = source[index + (slice(width - 5, width), slice(None))]
+    fill_stencil(recon, edge_weights, edge_cells, edge_codes, turned, spread, edge_stencil, 1)
+    for send, mass_at, stencil_at in ((send_down, width - 6, 5), (send_up, 0, 0)):
         for s in range(stacks):
-            send[6 * s : 6 * s + 6, :] = mass[s, at : at + 6, :]
-    for copy in copies[1:]:
-        copy.wait()
-
-
-def coefficients(recon_hbm, weights, cells, codes, stencil, send_down, send_up, recon, turned, spread, sem):
+            send[6 * s : 6 * s + 6, :] = mass[s, mass_at : mass_at + 6, :]
+        for o in range(OFFSETS):
+            at = 6 * stacks + 3 * o
+            send[at : at + 3, :] = edge_stencil[o, stencil_at : stencil_at + 3, :]
+
+
+def coefficients(recon_hbm, weights, cells, codes, stencil, recon, turned, spread, sem):
     copy = pltpu.make_async_copy(recon_hbm, recon, sem.at[0])
     copy.start()
     copy.wait()
-    width = stencil.shape[1]
-    fill_stencil(recon, weights, cells, codes, turned, spread, stencil, width // 8)
-    for send, at in ((send_down, width - 3), (send_up, 0)):
-        for o in range(OFFSETS):
-            send[3 * o : 3 * o + 3, :] = stencil[o, at : at + 3, :]
+    fill_stencil(recon, weights, cells, codes, turned, spread, stencil, stencil.shape[1] // 8)
 
 
 def pack_stacks(load, stacks, tile):
@@ -193,6 +200,28 @@
         left = jnp.where((lane >= at) & (lane < at + 3), turn(value, at), left)
         right = jnp.where((lane >= at + 6) & (lane < at + 9), turn(value, at - 119), right)
     return left, right
+
+
+def fill_near(near):
+    lane = lanes(1)
+    group = (lane * 57) >> 9
+    at = lane - SPAN * group
+    source = lax.broadcasted_iota(jnp.int32, (128, 128), 0)
+    for dy in range(-3, 4):
+        q = at - dy
+        right = jnp.where((at >= 3) & (q >= 0) & (q < 6), 122 + q, -1)
+        left = jnp.where((at < 6) & (q >= 3) & (q < 9), q - 3, -1)
+        for side, wanted in enumerate((right, left)):
+            wanted = jnp.where(group < PER, wanted, -1)
+            picked = jnp.where(source == wanted, 1.0, 0.0).astype(jnp.bfloat16)
+            near[dy + 3, 0:128, 128 * side : 128 * side + 128] = picked
+            near[dy + 3, 128:256, 128 * side : 128 * side + 128] = picked
+
+
+def replicate(value, picks):
+    high = value.astype(jnp.bfloat16)
+    low = (value - high.astype(F32)).astype(jnp.bfloat16)
+    return jnp.dot(jnp.concatenate([high, low], axis=1), picks, preferred_element_type=F32)
 
 
 def fill_picks(picks):
@@ -212,8 +241,9 @@
             picks[dy + 3, 128:256, 128 * side : 128 * side + 128] = picked
 
 
-def pack_own(mass, stencil, left, right, picks):
+def pack_own(mass, stencil, left, right, picks, near):
     fill_picks(picks)
+    fill_near(near)
     stacks, width = mass.shape[:2]
     tiles = -(-stacks // PER)
     for half in range(width // 8):
@@ -228,8 +258,7 @@
         left[at : at + 8, :], right[at : at + 8, :] = pack_coefficients(lambda o: stencil[o, rows, :])
 
 
-def pack_mass(own_left, own_right, above, below, left, right):
-    stacks = (above.shape[0] - 8) // 6
+def pack_all(stacks, own_left, own_right, above, below, middle, send_a, send_b, left, right):
     tiles = -(-stacks // PER)
     width = own_left.shape[0] // (tiles + 1)
     tall = width + 12
@@ -239,30 +268,25 @@
         end = tall * tiles + width + 6
         send[end:, :] = jnp.zeros((send.shape[0] - end, 128), F32)
     first, last = ends(ROW_AXES)
-    for got, outside, place in ((above, first, width), (below, last, width + 6)):
+    for got, outside, place, coef_place in (
+        (above, first, width, width), (below, last, width + 6, width + 3)
+    ):
+        coef = lambda o: got[6 * stacks + 3 * o : 6 * stacks + 3 * o + 8, :]
         for tile in range(tiles):
             at = tall * tile + place
             packed = pack_stacks(lambda s: got[6 * s : 6 * s + 8, :], stacks, tile)
+            if tile == 0:
+                spare = add_spare(coef, *packed)
+                packed = [
+                    jnp.where(lax.broadcasted_iota(jnp.int32, (8, 128), 0) < 3, with_spare, without)
+                    for with_spare, without in zip(spare, packed)
+                ]
             left[at : at + 6, :] = jnp.where(outside, 0.0, packed[0][0:6])
             right[at : at + 6, :] = jnp.where(outside, 0.0, packed[1][0:6])
-
-
-def pack_all(width, mass_left, mass_right, above, below, send_a, send_b, left, right):
-    left[...] = mass_left[...]
-    right[...] = mass_right[...]
-    coef_at = left.shape[0] - (width + 12)
-    first, last = ends(ROW_AXES)
-    for got, outside, mass_at, place in (
-        (above, first, width, width), (below, last, width + 6, width + 3)
-    ):
-        load = lambda o: jnp.where(outside, 0.0, got[3 * o : 3 * o + 8, :])
-        at = coef_at + place
-        packed = pack_coefficients(load)
-        left[at : at + 3, :] = packed[0][0:3]
-        right[at : at + 3, :] = packed[1][0:3]
-        packed = add_spare(load, left[mass_at : mass_at + 8, :], right[mass_at : mass_at + 8, :])
-        left[mass_at : mass_at + 3, :] = packed[0][0:3]
-        right[mass_at : mass_at + 3, :] = packed[1][0:3]
+        at = tall * tiles + coef_place
+        packed = pack_coefficients(coef)
+        left[at : at + 3, :] = jnp.where(outside, 0.0, packed[0][0:3])
+        right[at : at + 3, :] = jnp.where(outside, 0.0, packed[1][0:3])
     choose(is_even(COLUMN_AXES), right, left, send_a, send_b)
 
 
@@ -295,7 +319,45 @@
     return total
 
 
-def step_one(mass, stencil, above, below, coef_above, coef_below, partial, wide, shifted, own_shifted, field):
+def shift_rows(load, store, dys=range(-3, 4)):
+    lane = lanes()
+    for dy in dys:
+        values = [turn(load(dx * 7 + dy + 3), dy) for dx in range(7)]
+        if dy > 0:
+            values = [jnp.where(lane >= dy, value, 0.0) for value in values]
+        elif dy < 0:
+            values = [jnp.where(lane < 128 + dy, value, 0.0) for value in values]
+        for dx in range(7):
+            store(dx * 7 + dy + 3, values[dx])
+
+
+def own_part(mass, stencil, near, middle, own_shifted, right_near, left_near):
+    stacks, width = mass.shape[:2]
+    for tile in range(width // 8):
+        rows = pl.ds(8 * tile, 8)
+
+        def store(o, value):
+            own_shifted[o, rows, :] = value
+
+        shift_rows(lambda o: stencil[o, rows, :], store)
+
+    def some_stacks(group, carry):
+        for tile in range((width - 8) // 8):
+            total = main_sum(lambda k, at: mass[group * GROUP + k, 2 + at : 10 + at, :], own_shifted, 5, tile)
+            for k in range(GROUP):
+                middle[group * GROUP + k, 8 * tile : 8 * tile + 8, :] = total[k]
+        return carry
+
+    lax.fori_loop(0, stacks // GROUP, some_stacks, 0)
+    for dy in range(7):
+        value = jnp.concatenate([stencil[dx * 7 + dy, :, :] for dx in range(7)], axis=0)
+        spread = replicate(value, near[dy])
+        for dx in range(7):
+            right_near[dx * 7 + dy, :, :] = spread[width * dx : width * dx + width, 0:128]
+            left_near[dx * 7 + dy, :, :] = spread[width * dx : width * dx + width, 128:256]
+
+
+def both_steps(mass, stencil, above, below, middle, own_shifted, second, wide, shifted, field, partial):
     stacks, width = mass.shape[:2]
     first, last = ends(ROW_AXES)
     for s in range(stacks):
@@ -305,30 +367,31 @@
         field[s, width + 6 : width + 12, :] = jnp.where(last, 0.0, below[at : at + 6, :])
         field[s, width + 12 : width + 16, :] = jnp.zeros((4, 128), F32)
     for o in range(OFFSETS):
-        at = 3 * o
-        wide[o, 0:3, :] = jnp.where(first, 0.0, coef_above[at : at + 3, :])
+        at = 6 * stacks + 3 * o
+        wide[o, 0:3, :] = jnp.where(first, 0.0, above[at : at + 3, :])
         wide[o, 3 : width + 3, :] = stencil[o, :, :]
-        wide[o, width + 3 : width + 6, :] = jnp.where(last, 0.0, coef_below[at : at + 3, :])
+        wide[o, width + 3 : width + 6, :] = jnp.where(last, 0.0, below[at : at + 3, :])
         wide[o, width + 6 : width + 8, :] = jnp.zeros((2, 128), F32)
-    lane = lanes()
-    for tile in range((width + 8) // 8):
+    tiles = (0, width // 8)
+    for tile in tiles:
         rows = pl.ds(8 * tile, 8)
-        for dy in range(-3, 4):
-            values = [turn(wide[dx * 7 + dy + 3, rows, :], dy) for dx in range(7)]
-            if dy > 0:
-                values = [jnp.where(lane >= dy, value, 0.0) for value in values]
-            elif dy < 0:
-                values = [jnp.where(lane < 128 + dy, value, 0.0) for value in values]
-            for dx in range(7):
-                shifted[dx * 7 + dy + 3, rows, :] = values[dx]
-    for o in range(OFFSETS):
-        own_shifted[o, :, :] = shifted[o, 3 : width + 3, :]
+
+        def store(o, value):
+            shifted[o, rows, :] = value
+
+        shift_rows(lambda o: wide[o, rows, :], store)
 
     def some_stacks(group, carry):
-        for tile in range(partial.shape[1] // 8):
+        for k in range(GROUP):
+            partial[k, 8:width, :] = middle[group * GROUP + k, :, :]
+        for tile in tiles:
             total = main_sum(lambda k, at: field[group * GROUP + k, at : at + 8, :], shifted, 0, tile)
             for k in range(GROUP):
-                partial[group * GROUP + k, 8 * tile : 8 * tile + 8, :] = total[k]
+                partial[k, 8 * tile : 8 * tile + 8, :] = total[k]
+        for tile in range(width // 8):
+            total = main_sum(lambda k, at: partial[k, at : at + 8, :], own_shifted, 0, tile)
+            for k in range(GROUP):
+                second[group * GROUP + k, 8 * tile : 8 * tile + 8, :] = total[k]
         return carry
 
     lax.fori_loop(0, stacks // GROUP, some_stacks, 0)
@@ -431,24 +494,21 @@
                 rows_of[dy, at : at + 8, :] = values[dx]
 
     for dy in range(7):
-        value = rows_of[dy]
-        high = value.astype(jnp.bfloat16)
-        low = (value - high.astype(F32)).astype(jnp.bfloat16)
-        both = jnp.concatenate([high, low], axis=1)
-        spread = jnp.dot(both, picks[dy], preferred_element_type=F32)
+        spread = replicate(rows_of[dy], picks[dy])
         for dx in range(7):
             right_coef[dx * 7 + dy, :, :] = spread[tall * dx : tall * dx + tall, 0:128]
             left_coef[dx * 7 + dy, :, :] = spread[tall * dx : tall * dx + tall, 128:256]
 
 
 def halo_steps(
-    right_set, left_set, right_coef, left_coef, partial, field, edges,
-    edge_one, edge_two, right_next, left_next,
+    right_set, left_set, right_coef, left_coef, right_near, left_near, second, out_hbm,
+    right_next, left_next, right_out, left_out, out, sems,
 ):
     tiles = right_set.shape[0]
+    stacks, width = out.shape[:2]
     place = place_in_group()
     everywhere = range(-3, 4)
-    for tile in range(edge_one.shape[1] // 8):
+    for tile in range(right_next.shape[1] // 8):
         rows = pl.ds(8 * tile, 8)
         right = packed_sum(
             lambda t, at: right_set[t, at : at + 8, :], right_coef, 0, tile, tiles, everywhere
@@ -456,64 +516,41 @@
         left = packed_sum(
             lambda t, at: left_set[t, at : at + 8, :], left_coef, 0, tile, tiles, everywhere
         )
-        halo = (place >= 3) & (place < 6)
         for t in range(tiles):
-            right_next[t, rows, :] = jnp.where(halo, right[t], 0.0)
-            left_next[t, rows, :] = jnp.where(halo, left[t], 0.0)
-            edge_one[t, rows, :] = jnp.where(place < 3, right[t], turn(left[t], -3))
-    for tile in range(edge_two.shape[1] // 8):
+            right_next[t, rows, :] = jnp.where(place >= 3, turn(right[t], 3), 0.0)
+            left_next[t, rows, :] = jnp.where(place < 6, turn(left[t], -3), 0.0)
+    for tile in range(width // 8):
         rows = pl.ds(8 * tile, 8)
         right = packed_sum(
-            lambda t, at: right_next[t, at : at + 8, :], right_coef, 3, tile, tiles, range(1, 4)
+            lambda t, at: right_next[t, at : at + 8, :], right_near, 0, tile, tiles, everywhere
         )
         left = packed_sum(
-            lambda t, at: left_next[t, at : at + 8, :], left_coef, 3, tile, tiles, range(-3, 0)
+            lambda t, at: left_next[t, at : at + 8, :], left_near, 0, tile, tiles, everywhere
         )
         for t in range(tiles):
-            edge_two[t, rows, :] = jnp.where(place < 3, right[t], turn(left[t], -3))
+            right_out[t, rows, :] = right[t]
+            left_out[t, rows, :] = left[t]
 
     lane = lanes()
-    at_edge = (lane < 3) | (lane >= 125)
-    stacks = field.shape[0]
+    copies = []
     for t in range(tiles):
-        members = range(PER * t, min(stacks, PER * t + PER))
-        for tile in range(edge_one.shape[1] // 8):
+        low, high = PER * t, min(stacks, PER * t + PER)
+        for tile in range(width // 8):
             rows = pl.ds(8 * tile, 8)
-            packed = edge_one[t, rows, :]
-            values = [
-                partial[s, rows, :] + jnp.where(at_edge, turn(packed, 125 - SPAN * (s % PER)), 0.0)
-                for s in members
-            ]
-            for s, value in zip(members, values):
-                field[s, rows, :] = value
-        for tile in range(edge_two.shape[1] // 8):
-            rows = pl.ds(8 * tile, 8)
-            packed = edge_two[t, rows, :]
-            values = [jnp.where(at_edge, turn(packed, 125 - SPAN * (s % PER)), 0.0) for s in members]
-            for s, value in zip(members, values):
-                edges[s, rows, :] = value
-
-
-def step_two(field, own_shifted, edges, out_hbm, out, sems):
-    groups = out.shape[0] // GROUP
-
-    def piece(group):
-        stacks = pl.ds(group * GROUP, GROUP)
-        return pltpu.make_async_copy(out.at[stacks], out_hbm.at[stacks], sems.at[group])
-
-    def some_stacks(group, carry):
-        for tile in range(out.shape[1] // 8):
-            total = main_sum(lambda k, at: field[group * GROUP + k, at : at + 8, :], own_shifted, 0, tile)
-            rows = pl.ds(8 * tile, 8)
-            values = [total[k] + edges[group * GROUP + k, rows, :] for k in range(GROUP)]
-            for k in range(GROUP):
-                out[group * GROUP + k, rows, :] = values[k]
-        piece(group).start()
-        return carry
-
-    lax.fori_loop(0, groups, some_stacks, 0)
-    for group in range(groups):
-        piece(group).wait()
+            right, left = right_out[t, rows, :], left_out[t, rows, :]
+            values = []
+            for s in range(low, high):
+                at = SPAN * (s - low)
+                change = jnp.where(lane < 6, turn(left, -at - 3), 0.0)
+                change = jnp.where(lane >= 122, turn(right, 122 - at), change)
+                values.append(second[s, rows, :] + change)
+            for s, value in zip(range(low, high), values):
+                out[s, rows, :] = value
+        piece = pl.ds(low, high - low)
+        copies.append(pltpu.make_async_copy(out.at[piece], out_hbm.at[piece], sems.at[t]))
+        copies[-1].start()
+    for copy in copies:
+        copy.wait()
 
 
 def local(tracer_mass, recon_table, intersection_weights, intersection_cells, rotation_codes):
@@ -525,29 +562,41 @@
     tall, low = width + 16, width + 8
     fixed = lambda *values: [pltpu.with_memory_space_constraint(value, pltpu.HBM) for value in values]
     whole = lambda value: jax.ShapeDtypeStruct(value.shape, value.dtype)
-    mass_edge, coef_edge = 6 * stacks + 8, -(-(3 * OFFSETS + 5) // 8) * 8
-
-    mass, weights, cells, codes, mass_down, mass_up = pl.pallas_call(
-        mass_rows,
+    edge = -(-(6 * stacks + 3 * OFFSETS + 5) // 8) * 8
+    integers = lambda *sizes: pltpu.VMEM(sizes, jnp.int32)
+    picks = jax.ShapeDtypeStruct((7, 256, 256), jnp.bfloat16)
+    regions = intersection_cells.shape[0]
+
+    mass, weights, cells, codes, send_down, send_up = pl.pallas_call(
+        edge_rows,
         out_shape=(
             whole(tracer_mass), whole(intersection_weights), whole(intersection_cells),
-            whole(rotation_codes), shape(mass_edge, 128), shape(mass_edge, 128),
+            whole(rotation_codes), shape(edge, 128), shape(edge, 128),
         ),
-        in_specs=[HBM] * 4,
+        in_specs=[HBM] * 5,
         out_specs=(VMEM,) * 6,
-        scratch_shapes=[pltpu.SemaphoreType.DMA((4,))],
-        compiler_params=params(),
-        cost_estimate=cost(10**6),
-        name="mass_rows",
-    )(*fixed(tracer_mass, intersection_weights, intersection_cells, rotation_codes))
-    above = shift(mass_down, ROW_AXES, 1)
-    below = shift(mass_up, ROW_AXES, -1)
-
-    stencil, coef_down, coef_up = pl.pallas_call(
+        scratch_shapes=[
+            pltpu.SMEM(recon_table.shape, F32),
+            scratch(regions, TERMS, 8, 128),
+            integers(regions, 8, 128),
+            integers(regions, 8, 128),
+            scratch(OFFSETS, 8, 128),
+            scratch(TERMS, regions, 8, 128),
+            scratch(25, regions, 8, 128),
+            pltpu.SemaphoreType.DMA((5,)),
+        ],
+        compiler_params=params(),
+        cost_estimate=cost(4 * 10**6),
+        name="edge_rows",
+    )(*fixed(recon_table, tracer_mass, intersection_weights, intersection_cells, rotation_codes))
+    above = shift(send_down, ROW_AXES, 1)
+    below = shift(send_up, ROW_AXES, -1)
+
+    stencil = pl.pallas_call(
         coefficients,
-        out_shape=(shape(OFFSETS, width, 128), shape(coef_edge, 128), shape(coef_edge, 128)),
+        out_shape=shape(OFFSETS, width, 128),
         in_specs=[HBM] + [VMEM] * 3,
-        out_specs=(VMEM,) * 3,
+        out_specs=VMEM,
         scratch_shapes=[
             pltpu.SMEM(recon_table.shape, F32),
             scratch(TERMS, combos, 8, 128),
@@ -558,56 +607,51 @@
         cost_estimate=cost(8 * 10**6),
         name="coefficients",
     )(*fixed(recon_table), weights, cells, codes)
-    coef_above = shift(coef_down, ROW_AXES, 1)
-    coef_below = shift(coef_up, ROW_AXES, -1)
-
-    picks = jax.ShapeDtypeStruct((7, 256, 256), jnp.bfloat16)
-    own_left, own_right, picks = pl.pallas_call(
+
+    own_left, own_right, picks, near = pl.pallas_call(
         pack_own,
-        out_shape=(shape(width * (tiles + 1), 128),) * 2 + (picks,),
+        out_shape=(shape(width * (tiles + 1), 128),) * 2 + (picks, picks),
         in_specs=[VMEM] * 2,
-        out_specs=(VMEM,) * 3,
+        out_specs=(VMEM,) * 4,
         compiler_params=params(),
         cost_estimate=cost(10**6),
         name="pack_own",
     )(mass, stencil)
 
+    middle, own_shifted, right_near, left_near = pl.pallas_call(
+        own_part,
+        out_shape=(shape(stacks, width - 8, 128),) + (shape(OFFSETS, width, 128),) * 3,
+        in_specs=[VMEM] * 3,
+        out_specs=(VMEM,) * 4,
+        compiler_params=params(),
+        cost_estimate=cost(4 * 10**6),
+        name="own_part",
+    )(mass, stencil, near)
+
     send = ((width + 12) * (tiles + 1), 128)
-    mass_left, mass_right = pl.pallas_call(
-        pack_mass,
+    send_a, send_b = pl.pallas_call(
+        functools.partial(pack_all, stacks),
         out_shape=(shape(*send),) * 2,
-        in_specs=[VMEM] * 4,
-        out_specs=(VMEM,) * 2,
-        compiler_params=params(),
-        cost_estimate=cost(10**6),
-        name="pack_mass",
-    )(own_left, own_right, above, below)
-    send_a, send_b = pl.pallas_call(
-        functools.partial(pack_all, width),
-        out_shape=(shape(*send),) * 2,
-        in_specs=[VMEM] * 4,
+        in_specs=[VMEM] * 4 + [ANY],
         out_specs=(VMEM,) * 2,
         scratch_shapes=[scratch(*send)] * 2,
         compiler_params=params(),
         cost_estimate=cost(10**6),
         name="pack_all",
-    )(mass_left, mass_right, coef_above, coef_below)
+    )(own_left, own_right, above, below, middle)
     column_a = swap(send_a, COLUMN_AXES, False)
     column_b = swap(send_b, COLUMN_AXES, True)
 
-    partial, wide, shifted, own_shifted = pl.pallas_call(
-        step_one,
-        out_shape=(
-            shape(stacks, low, 128), shape(OFFSETS, low, 128), shape(OFFSETS, low, 128),
-            shape(OFFSETS, width, 128),
-        ),
+    second, wide = pl.pallas_call(
+        both_steps,
+        out_shape=(shape(stacks, width, 128), shape(OFFSETS, low, 128)),
         in_specs=[VMEM] * 6,
-        out_specs=(VMEM,) * 4,
-        scratch_shapes=[scratch(stacks, tall, 128)],
+        out_specs=(VMEM,) * 2,
+        scratch_shapes=[scratch(OFFSETS, low, 128), scratch(stacks, tall, 128), scratch(GROUP, low, 128)],
         compiler_params=params(),
         cost_estimate=cost(12 * 10**6),
-        name="step_one",
-    )(mass, stencil, above, below, coef_above, coef_below)
+        name="both_steps",
+    )(mass, stencil, above, below, middle, own_shifted)
 
     sides = pl.pallas_call(
         side_coefficients,
@@ -620,27 +664,17 @@
         name="side_coefficients",
     )(wide, send_a, send_b, column_a, column_b, picks)
 
-    field, edges = pl.pallas_call(
+    return pl.pallas_call(
         halo_steps,
-        out_shape=(shape(stacks, low, 128), shape(stacks, width, 128)),
-        in_specs=[VMEM] * 5,
-        out_specs=(VMEM,) * 2,
-        scratch_shapes=[scratch(tiles, low, 128), scratch(tiles, width, 128)] + [scratch(tiles, low, 128)] * 2,
+        out_shape=shape(stacks, width, columns),
+        in_specs=[VMEM] * 7,
+        out_specs=HBM,
+        scratch_shapes=[scratch(tiles, low, 128)] * 2 + [scratch(tiles, width, 128)] * 2
+        + [scratch(stacks, width, columns), pltpu.SemaphoreType.DMA((tiles,))],
         compiler_params=params(),
         cost_estimate=cost(4 * 10**6),
         name="halo_steps",
-    )(*sides, partial)
-
-    return pl.pallas_call(
-        step_two,
-        out_shape=shape(stacks, width, columns),
-        in_specs=[VMEM] * 3,
-        out_specs=HBM,
-        scratch_shapes=[scratch(stacks, width, columns), pltpu.SemaphoreType.DMA((stacks // GROUP,))],
-        compiler_params=params(),
-        cost_estimate=cost(8 * 10**6),
-        name="step_two",
-    )(field, own_shifted, edges)
+    )(*sides, right_near, left_near, second)
 
 
 def solution(mesh):

time: 23.9 us -> 21 us (0.88)
  starting transfers between devices: 11 us -> 8.26 us
  waiting for transfers between devices: 1.82 us -> 0.33 us
  Pallas kernels: 10.8 us -> 12.2 us
    ppermute x4 -> x2, starting transfers between devices: 6.14 us -> 3.45 us  [shift(): lax.ppermute(block, axes, [(index, (index + step) % count) for index in r...]
    ppermute x4 -> x2, waiting for transfers between devices: 1.32 us -> 0.01 us  [shift(): lax.ppermute(block, axes, [(index, (index + step) % count) for index in r...]
    pallas_call x7 -> x6, Pallas kernels: 9.75 us -> 10.9 us  [the longest x1 3.75 us: local(): pl.pallas_call(both_steps, out_shape=(shape(stacks, width, 128), shape(OF...]
  transfers between devices with their start and end apart: 6 -> 4, of which waited for: 2 -> 1; matrix products, arithmetic and copies ran while one was open for 0% -> 0% of each run, Pallas kernels for 24% -> 37%
where the time goes in v3:
time: 21 us; the launch traced here: 20.8 us
  Pallas kernels  12.2 us (58%)
  starting transfers between devices  8.26 us (39%)
  waiting for transfers between devices  0.33 us (2%)
    ppermute x2, starting transfers between devices, swap(): return lax.ppermute(block, axes, list(enumerate(partner)))  4.81 us
    pallas_call x1, Pallas kernels, local(): pl.pallas_call(both_steps, out_shape=(shape(stacks, width, 128), shape(OF...  3.75 us
    ppermute x2, starting transfers between devices, shift(): lax.ppermute(block, axes, [(index, (index + step) % count) for index in r...  3.45 us
    pallas_call x1, Pallas kernels, local(): pl.pallas_call(edge_rows, out_shape=(whole(tracer_mass), whole(intersecti...  1.88 us
    pallas_call x1, Pallas kernels, local(): pl.pallas_call(coefficients, out_shape=shape(OFFSETS, width, 128), in_spe...  1.78 us
    pallas_call x1, Pallas kernels, local(): pl.pallas_call(own_part, out_shape=(shape(stacks, width - 8, 128),) + (sh...  1.62 us
    pallas_call x1, Pallas kernels, local(): pl.pallas_call(halo_steps, out_shape=shape(stacks, width, columns), in_sp...  1.44 us
    pallas_call x1, Pallas kernels, local(): pl.pallas_call(pack_own, out_shape=(shape(width * (tiles + 1), 128),) * 2...  0.64 us
  transfers between devices with their start and end apart: 4, of which 1 were waited for; matrix products, arithmetic and copies ran while one was open for 0% of the time, Pallas kernels for 37%

profile of v3, /device:TPU:0, one launch (start us, length us, event | category | flops | bytes accessed | tf_op | source)
XLA Modules:
  0.0 20.8 jit_solution(3559194301195373286)
XLA Ops:
  0.0 1.9 %edge_rows.1 = (f32[40,16,128]{2,1,0:T(8,128)S(1)}, f32[4,10,16,128]{3,2,1,0:T(8,128)S(1)}, s32[4,16,128]{2,1,0:T(8,128)S(1)}, s32[4,16,128]{2,1,0:T(8,128)S(1)}...) custom-call(f32[10,25]{1,0:T(8,128)} %recon_hbm.3, f32[40,16,128]{2,1,0:T(8,128)} %mass_hbm.1, ...), custom_call_target="tpu_custom_call" | custom-call | flops 4000000 | bytes 1048576 | tf_op jit(solution)/shard_map/edge_rows/pallas_call | solution.py:570
  1.9 0.5 %collective-permute-start = (f32[392,128]{1,0:T(8,128)S(1)}, f32[392,128]{1,0:T(8,128)S(1)}, u32[]{:S(2)}, u32[]{:S(2)}) collective-permute-start(f32[392,128]{1,0:T(8,128)S(1)} %get-tuple-element.31), channel_id=1, source_target_pairs={{0,4},{4,8},{8,12},{12,16},{16,20},{20,24},{24,28},{28,0},{1,5},{5... | collective-permute-start | bytes 602120 | tf_op jit(solution)/shard_map/ppermute | solution.py:46
  2.4 2.9 %collective-permute-start.1 = (f32[392,128]{1,0:T(8,128)S(1)}, f32[392,128]{1,0:T(8,128)S(1)}, u32[]{:S(2)}, u32[]{:S(2)}) collective-permute-start(f32[392,128]{1,0:T(8,128)S(1)} %get-tuple-element.32), channel_id=1, source_target_pairs={{0,28},{4,0},{8,4},{12,8},{16,12},{20,16},{24,20},{28,24},{1,29},{... | collective-permute-start | bytes 602120 | tf_op jit(solution)/shard_map/ppermute | solution.py:46
  5.3 1.8 %coefficients.1.stencil = f32[49,16,128]{2,1,0:T(8,128)S(1)} custom-call(f32[10,25]{1,0:T(8,128)} %recon_hbm.3, f32[4,10,16,128]{3,2,1,0:T(8,128)S(1)} %get-tuple-element.28.weights, s32[4,16,128]{2,1,0:T(8,128)S(1)} %get-tuple-element.29.cells, s32[4,16,128]{2,1,0:T(8,128)S(1)} %get-tuple-element.30.codes), custom_call_target="tpu_custom_call" | custom-call | flops 8000000 | bytes 1048576 | tf_op jit(solution)/shard_map/coefficients/pallas_call | solution.py:595
  7.1 0.6 %pack_own.1 = (f32[64,128]{1,0:T(8,128)S(1)}, f32[64,128]{1,0:T(8,128)S(1)}, bf16[7,256,256]{2,1,0:T(8,128)(2,1)S(1)}, bf16[7,256,256]{2,1,0:T(8,128)(2,1)S(1)}) custom-call(f32[40,16,128]{2,1,0:T(8,128)S(1)} %get-tuple-element.27.mass, f32[49,16,128]{2,1,0:T(8,128)S(1)} %coefficients.1.stencil), custom_call_target="tpu_custom_call" | custom-call | flops 1000000 | bytes 1048576 | tf_op jit(solution)/shard_map/pack_own/pallas_call | solution.py:611
  7.8 1.6 %own_part.1 = (f32[40,8,128]{2,1,0:T(8,128)S(1)}, f32[49,16,128]{2,1,0:T(8,128)S(1)}, f32[49,16,128]{2,1,0:T(8,128)S(1)}, f32[49,16,128]{2,1,0:T(8,128)S(1)}) custom-call(f32[40,16,128]{2,1,0:T(8,128)S(1)} %get-tuple-element.27.mass, f32[49,16,128]{2,1,0:T(8,128)S(1)} %coefficients.1.stencil, bf16[7,256,256]{2,1,0:T(8,128)(2,1)S(1)} %get-tuple-element.33.near), custom_call_target="tpu_custom_call" | custom-call | flops 4000000 | bytes 1048576 | tf_op jit(solution)/shard_map/own_part/pallas_call | solution.py:621
  9.4 0.0 collective-permute-done.above
  9.4 0.0 collective-permute-done.1.below
  9.4 0.5 %pack_all.1 = (f32[112,128]{1,0:T(8,128)S(1)}, f32[112,128]{1,0:T(8,128)S(1)}) custom-call(f32[64,128]{1,0:T(8,128)S(1)} %get-tuple-element.37.own_left, f32[64,128]{1,0:T(8,128)S(1)} %get-tuple-element.38.own_right, f32[392,128]{1,0:T(8,128)S(1)} %collective-permute-done.above, f32[392,128]{1,0:T(8,128)S(1)} %collective-permute-done.1.below, ...), custom_call_target="tpu_custom_call" | custom-call | flops 1000000 | bytes 1048576 | tf_op jit(solution)/shard_map/pack_all/pallas_call | solution.py:632
  9.9 2.3 %collective-permute-start.2 = (f32[112,128]{1,0:T(8,128)S(1)}, f32[112,128]{1,0:T(8,128)S(1)}, u32[]{:S(2)}, u32[]{:S(2)}) collective-permute-start(f32[112,128]{1,0:T(8,128)S(1)} %get-tuple-element.39.send_a), channel_id=1, source_target_pairs={{0,1},{1,0},{2,3},{3,2},{4,5},{5,4},{6,7},{7,6},{8,9},{9,8},{10,11... | collective-permute-start | bytes 172040 | tf_op jit(solution)/shard_map/ppermute | solution.py:41
  12.2 2.5 %collective-permute-start.3 = (f32[112,128]{1,0:T(8,128)S(1)}, f32[112,128]{1,0:T(8,128)S(1)}, u32[]{:S(2)}, u32[]{:S(2)}) collective-permute-start(f32[112,128]{1,0:T(8,128)S(1)} %get-tuple-element.40.send_b), channel_id=1, source_target_pairs={{0,3},{1,2},{2,1},{3,0},{4,7},{5,6},{6,5},{7,4},{8,11},{9,10},{10,... | collective-permute-start | bytes 172040 | tf_op jit(solution)/shard_map/ppermute | solution.py:41
  14.7 3.8 %both_steps.1 = (f32[40,16,128]{2,1,0:T(8,128)S(1)}, f32[49,24,128]{2,1,0:T(8,128)S(1)}) custom-call(f32[40,16,128]{2,1,0:T(8,128)S(1)} %get-tuple-element.27.mass, f32[49,16,128]{2,1,0:T(8,128)S(1)} %coefficients.1.stencil, f32[392,128]{1,0:T(8,128)S(1)} %collective-permute-done.above, f32[392,128]{1,0:T(8,128)S(1)} %collective-permute-done.1.below, ...), custom_call_target="tpu_custom_call" | custom-call | flops 12000000 | bytes 1048576 | tf_op jit(solution)/shard_map/both_steps/pallas_call | solution.py:645
  18.5 0.0 collective-permute-done.2.got_a
  18.5 0.3 %collective-permute-done.3.got_b = f32[112,128]{1,0:T(8,128)S(1)} collective-permute-done((f32[112,128]{1,0:T(8,128)S(1)}, f32[112,128]{1,0:T(8,128)S(1)}, u32[]{:S(2)}, u32[]{:S(2)}) %collective-permute-start.3) | collective-permute-done | bytes 57376 | tf_op jit(solution)/shard_map/ppermute | solution.py:41
  18.8 0.6 %side_coefficients.1 = (f32[3,32,128]{2,1,0:T(8,128)S(1)}, f32[3,32,128]{2,1,0:T(8,128)S(1)}, f32[49,24,128]{2,1,0:T(8,128)S(1)}, f32[49,24,128]{2,1,0:T(8,128)S(1)}) custom-call(f32[49,24,128]{2,1,0:T(8,128)S(1)} %get-tuple-element.36.wide, f32[112,128]{1,0:T(8,128)S(1)} %get-tuple-element.39.send_a, f32[112,128]{1,0:T(8,128)S(1)} %get-tuple-element.40.send_b, ...), custom_call_target="tpu_custom_call" | custom-call | flops 4000000 | bytes 1048576 | tf_op jit(solution)/shard_map/side_coefficients/pallas_call | solution.py:656
  19.4 1.4 %halo_steps.1 = f32[40,16,128]{2,1,0:T(8,128)} custom-call(f32[3,32,128]{2,1,0:T(8,128)S(1)} %get-tuple-element.42.right_set, f32[3,32,128]{2,1,0:T(8,128)S(1)} %get-tuple-element.43.left_set, f32[49,24,128]{2,1,0:T(8,128)S(1)} %get-tuple-element.44.right_coef, f32[49,24,128]{2,1,0:T(8,128)S(1)} %get-tuple-element.45.left_coef, ...), custom_call_target="tpu_custom_call" | custom-call | flops 4000000 | bytes 1048576 | tf_op jit(solution)/shard_map/halo_steps/pallas_call | solution.py:667
Async XLA Ops:
  1.9 7.5 %collective-permute-start = (f32[392,128]{1,0:T(8,128)S(1)}, f32[392,128]{1,0:T(8,128)S(1)}, u32[]{:S(2)}, u32[]{:S(2)}) collective-permute-start(f32[392,128]{1,0:T(8,128)S(1)} %get-tuple-element.31), channel_id=1, source_target_pairs={{0,4},{4,8},{8,12},{12,16},{16,20},{20,24},{24,28},{28,0},{1,5},{5... | collective-permute-start | bytes 602120 | tf_op jit(solution)/shard_map/ppermute | solution.py:46
  2.4 7.0 %collective-permute-start.1 = (f32[392,128]{1,0:T(8,128)S(1)}, f32[392,128]{1,0:T(8,128)S(1)}, u32[]{:S(2)}, u32[]{:S(2)}) collective-permute-start(f32[392,128]{1,0:T(8,128)S(1)} %get-tuple-element.32), channel_id=1, source_target_pairs={{0,28},{4,0},{8,4},{12,8},{16,12},{20,16},{24,20},{28,24},{1,29},{... | collective-permute-start | bytes 602120 | tf_op jit(solution)/shard_map/ppermute | solution.py:46
  9.9 8.6 %collective-permute-start.2 = (f32[112,128]{1,0:T(8,128)S(1)}, f32[112,128]{1,0:T(8,128)S(1)}, u32[]{:S(2)}, u32[]{:S(2)}) collective-permute-start(f32[112,128]{1,0:T(8,128)S(1)} %get-tuple-element.39.send_a), channel_id=1, source_target_pairs={{0,1},{1,0},{2,3},{3,2},{4,5},{5,4},{6,7},{7,6},{8,9},{9,8},{10,11... | collective-permute-start | bytes 172040 | tf_op jit(solution)/shard_map/ppermute | solution.py:41
  12.2 6.6 %collective-permute-start.3 = (f32[112,128]{1,0:T(8,128)S(1)}, f32[112,128]{1,0:T(8,128)S(1)}, u32[]{:S(2)}, u32[]{:S(2)}) collective-permute-start(f32[112,128]{1,0:T(8,128)S(1)} %get-tuple-element.40.send_b), channel_id=1, source_target_pairs={{0,3},{1,2},{2,1},{3,0},{4,7},{5,6},{6,5},{7,4},{8,11},{9,10},{10,... | collective-permute-start | bytes 172040 | tf_op jit(solution)/shard_map/ppermute | solution.py:41

commit v4 on v3

--- a/solution.py
+++ b/solution.py
@@ -89,18 +89,21 @@
 
     combos = 4 * tiles
 
-    def one_tap(tap, carry):
-        total = [None] * combos
+    def five_taps(jx, carry):
+        total = [[None] * combos for jy in range(5)]
         for t in range(TERMS):
-            scale = recon[t, tap]
+            values = [turned[t, c] for c in range(combos)]
+            for jy in range(5):
+                scale = recon[t, 5 * jx + jy]
+                for c in range(combos):
+                    term = values[c] * scale
+                    total[jy][c] = term if t == 0 else total[jy][c] + term
+        for jy in range(5):
             for c in range(combos):
-                term = turned[t, c] * scale
-                total[c] = term if t == 0 else total[c] + term
-        for c in range(combos):
-            spread[tap, c] = total[c]
+                spread[5 * jx + jy, c] = total[jy][c]
         return carry
 
-    lax.fori_loop(0, 25, one_tap, 0)
+    lax.fori_loop(0, 5, five_taps, 0)
 
     for g in range(tiles):
         rows = pl.ds(8 * g, 8)
@@ -173,10 +176,14 @@
     right = jnp.zeros((8, 128), F32)
     for s in range(PER * tile, min(stacks, PER * tile + PER)):
         at = SPAN * (s % PER)
-        value = load(s)
-        left = jnp.where((lane >= at + 3) & (lane < at + 9), turn(value, at + 3), left)
-        right = jnp.where((lane >= at) & (lane < at + 6), turn(value, at - 122), right)
-    return left, right
+        moved = turn(load(s), at - 122)
+        right = jnp.where((lane >= at) & (lane < at + 6), moved, right)
+        left = jnp.where(on_ring(lane, at + 6, at + 12), moved, left)
+    return turn(left, -3), right
+
+
+def on_ring(lane, low, high):
+    return (lane >= low) | (lane < high - 128) if high > 128 else (lane >= low) & (lane < high)
 
 
 def pack_coefficients(load):
@@ -185,11 +192,10 @@
     right = jnp.zeros((8, 128), F32)
     for o in range(COEF_PER):
         at = 3 * o
-        here = (lane >= at) & (lane < at + 3)
-        value = load(o)
-        left = jnp.where(here, turn(value, at), left)
-        right = jnp.where(here, turn(value, at - 125), right)
-    return left, right
+        moved = turn(load(o), at - 125)
+        right = jnp.where((lane >= at) & (lane < at + 3), moved, right)
+        left = jnp.where(on_ring(lane, at + 3, at + 6), moved, left)
+    return turn(left, -3), right
 
 
 def add_spare(load, left, right):
@@ -381,20 +387,31 @@
 
         shift_rows(lambda o: wide[o, rows, :], store)
 
-    def some_stacks(group, carry):
+    def first_step(group, carry):
+        totals = [
+            main_sum(lambda k, at: field[group * GROUP + k, at : at + 8, :], shifted, 0, tile)
+            for tile in tiles
+        ]
         for k in range(GROUP):
-            partial[k, 8:width, :] = middle[group * GROUP + k, :, :]
-        for tile in tiles:
-            total = main_sum(lambda k, at: field[group * GROUP + k, at : at + 8, :], shifted, 0, tile)
-            for k in range(GROUP):
-                partial[k, 8 * tile : 8 * tile + 8, :] = total[k]
-        for tile in range(width // 8):
-            total = main_sum(lambda k, at: partial[k, at : at + 8, :], own_shifted, 0, tile)
-            for k in range(GROUP):
+            s = group * GROUP + k
+            partial[s, 8:width, :] = middle[s, :, :]
+            for tile, total in zip(tiles, totals):
+                partial[s, 8 * tile : 8 * tile + 8, :] = total[k]
+        return carry
+
+    lax.fori_loop(0, stacks // GROUP, first_step, 0)
+
+    def second_step(group, carry):
+        totals = [
+            main_sum(lambda k, at: partial[group * GROUP + k, at : at + 8, :], own_shifted, 0, tile)
+            for tile in range(width // 8)
+        ]
+        for k in range(GROUP):
+            for tile, total in enumerate(totals):
                 second[group * GROUP + k, 8 * tile : 8 * tile + 8, :] = total[k]
         return carry
 
-    lax.fori_loop(0, stacks // GROUP, some_stacks, 0)
+    lax.fori_loop(0, stacks // GROUP, second_step, 0)
 
 
 def packed_sum(load, coef, coef_at, tile, tiles, dys):
@@ -647,7 +664,7 @@
         out_shape=(shape(stacks, width, 128), shape(OFFSETS, low, 128)),
         in_specs=[VMEM] * 6,
         out_specs=(VMEM,) * 2,
-        scratch_shapes=[scratch(OFFSETS, low, 128), scratch(stacks, tall, 128), scratch(GROUP, low, 128)],
+        scratch_shapes=[scratch(OFFSETS, low, 128), scratch(stacks, tall, 128), scratch(stacks, low, 128)],
         compiler_params=params(),
         cost_estimate=cost(12 * 10**6),
         name="both_steps",

time: 21 us -> 20.9 us (level)
  the two profiles are of different devices: /device:TPU:0 before, /device:TPU:1 now
where the time goes in v4:
time: 20.9 us; the launch traced here: 20.6 us
  Pallas kernels  11.9 us (57%)
  starting transfers between devices  6.97 us (33%)
  waiting for transfers between devices  1.73 us (8%)
    ppermute x2, starting transfers between devices, swap(): return lax.ppermute(block, axes, list(enumerate(partner)))  4.28 us
    pallas_call x1, Pallas kernels, local(): pl.pallas_call(both_steps, out_shape=(shape(stacks, width, 128), shape(OF...  3.83 us
    ppermute x2, starting transfers between devices, shift(): lax.ppermute(block, axes, [(index, (index + step) % count) for index in r...  2.68 us
    ppermute x2, waiting for transfers between devices, shift(): lax.ppermute(block, axes, [(index, (index + step) % count) for index in r...  1.72 us
    pallas_call x1, Pallas kernels, local(): pl.pallas_call(edge_rows, out_shape=(whole(tracer_mass), whole(intersecti...  1.7 us
    pallas_call x1, Pallas kernels, local(): pl.pallas_call(own_part, out_shape=(shape(stacks, width - 8, 128),) + (sh...  1.62 us
    pallas_call x1, Pallas kernels, local(): pl.pallas_call(coefficients, out_shape=shape(OFFSETS, width, 128), in_spe...  1.58 us
    pallas_call x1, Pallas kernels, local(): pl.pallas_call(halo_steps, out_shape=shape(stacks, width, columns), in_sp...  1.44 us
  transfers between devices with their start and end apart: 4, of which 1 were waited for; matrix products, arithmetic and copies ran while one was open for 0% of the time, Pallas kernels for 37%

profile of v4, /device:TPU:1, one launch (start us, length us, event | category | flops | bytes accessed | tf_op | source)
XLA Modules:
  0.0 20.6 jit_solution(16318985365819375283)
XLA Ops:
  0.0 1.7 %edge_rows.1 = (f32[40,16,128]{2,1,0:T(8,128)S(1)}, f32[4,10,16,128]{3,2,1,0:T(8,128)S(1)}, s32[4,16,128]{2,1,0:T(8,128)S(1)}, s32[4,16,128]{2,1,0:T(8,128)S(1)}...) custom-call(f32[10,25]{1,0:T(8,128)} %recon_hbm.3, f32[40,16,128]{2,1,0:T(8,128)} %mass_hbm.1, ...), custom_call_target="tpu_custom_call" | custom-call | flops 4000000 | bytes 1048576 | tf_op jit(solution)/shard_map/edge_rows/pallas_call | solution.py:587
  1.7 2.7 %collective-permute-start = (f32[392,128]{1,0:T(8,128)S(1)}, f32[392,128]{1,0:T(8,128)S(1)}, u32[]{:S(2)}, u32[]{:S(2)}) collective-permute-start(f32[392,128]{1,0:T(8,128)S(1)} %get-tuple-element.31), channel_id=1, source_target_pairs={{0,4},{4,8},{8,12},{12,16},{16,20},{20,24},{24,28},{28,0},{1,5},{5... | collective-permute-start | bytes 602120 | tf_op jit(solution)/shard_map/ppermute | solution.py:46
  4.4 0.0 collective-permute-start.1
  4.4 1.6 %coefficients.1.stencil = f32[49,16,128]{2,1,0:T(8,128)S(1)} custom-call(f32[10,25]{1,0:T(8,128)} %recon_hbm.3, f32[4,10,16,128]{3,2,1,0:T(8,128)S(1)} %get-tuple-element.28.weights, s32[4,16,128]{2,1,0:T(8,128)S(1)} %get-tuple-element.29.cells, s32[4,16,128]{2,1,0:T(8,128)S(1)} %get-tuple-element.30.codes), custom_call_target="tpu_custom_call" | custom-call | flops 8000000 | bytes 1048576 | tf_op jit(solution)/shard_map/coefficients/pallas_call | solution.py:612
  6.0 0.7 %pack_own.1 = (f32[64,128]{1,0:T(8,128)S(1)}, f32[64,128]{1,0:T(8,128)S(1)}, bf16[7,256,256]{2,1,0:T(8,128)(2,1)S(1)}, bf16[7,256,256]{2,1,0:T(8,128)(2,1)S(1)}) custom-call(f32[40,16,128]{2,1,0:T(8,128)S(1)} %get-tuple-element.27.mass, f32[49,16,128]{2,1,0:T(8,128)S(1)} %coefficients.1.stencil), custom_call_target="tpu_custom_call" | custom-call | flops 1000000 | bytes 1048576 | tf_op jit(solution)/shard_map/pack_own/pallas_call | solution.py:628
  6.7 1.6 %own_part.1 = (f32[40,8,128]{2,1,0:T(8,128)S(1)}, f32[49,16,128]{2,1,0:T(8,128)S(1)}, f32[49,16,128]{2,1,0:T(8,128)S(1)}, f32[49,16,128]{2,1,0:T(8,128)S(1)}) custom-call(f32[40,16,128]{2,1,0:T(8,128)S(1)} %get-tuple-element.27.mass, f32[49,16,128]{2,1,0:T(8,128)S(1)} %coefficients.1.stencil, bf16[7,256,256]{2,1,0:T(8,128)(2,1)S(1)} %get-tuple-element.33.near), custom_call_target="tpu_custom_call" | custom-call | flops 4000000 | bytes 1048576 | tf_op jit(solution)/shard_map/own_part/pallas_call | solution.py:638
  8.3 0.0 collective-permute-done.above
  8.3 1.7 %collective-permute-done.1.below = f32[392,128]{1,0:T(8,128)S(1)} collective-permute-done((f32[392,128]{1,0:T(8,128)S(1)}, f32[392,128]{1,0:T(8,128)S(1)}, u32[]{:S(2)}, u32[]{:S(2)}) %collective-permute-start.1) | collective-permute-done | bytes 200736 | tf_op jit(solution)/shard_map/ppermute | solution.py:46
  10.0 0.4 %pack_all.1 = (f32[112,128]{1,0:T(8,128)S(1)}, f32[112,128]{1,0:T(8,128)S(1)}) custom-call(f32[64,128]{1,0:T(8,128)S(1)} %get-tuple-element.37.own_left, f32[64,128]{1,0:T(8,128)S(1)} %get-tuple-element.38.own_right, f32[392,128]{1,0:T(8,128)S(1)} %collective-permute-done.above, f32[392,128]{1,0:T(8,128)S(1)} %collective-permute-done.1.below, ...), custom_call_target="tpu_custom_call" | custom-call | flops 1000000 | bytes 1048576 | tf_op jit(solution)/shard_map/pack_all/pallas_call | solution.py:649
  10.5 2.1 %collective-permute-start.2 = (f32[112,128]{1,0:T(8,128)S(1)}, f32[112,128]{1,0:T(8,128)S(1)}, u32[]{:S(2)}, u32[]{:S(2)}) collective-permute-start(f32[112,128]{1,0:T(8,128)S(1)} %get-tuple-element.39.send_a), channel_id=1, source_target_pairs={{0,1},{1,0},{2,3},{3,2},{4,5},{5,4},{6,7},{7,6},{8,9},{9,8},{10,11... | collective-permute-start | bytes 172040 | tf_op jit(solution)/shard_map/ppermute | solution.py:41
  12.6 2.2 %collective-permute-start.3 = (f32[112,128]{1,0:T(8,128)S(1)}, f32[112,128]{1,0:T(8,128)S(1)}, u32[]{:S(2)}, u32[]{:S(2)}) collective-permute-start(f32[112,128]{1,0:T(8,128)S(1)} %get-tuple-element.40.send_b), channel_id=1, source_target_pairs={{0,3},{1,2},{2,1},{3,0},{4,7},{5,6},{6,5},{7,4},{8,11},{9,10},{10,... | collective-permute-start | bytes 172040 | tf_op jit(solution)/shard_map/ppermute | solution.py:41
  14.7 3.8 %both_steps.1 = (f32[40,16,128]{2,1,0:T(8,128)S(1)}, f32[49,24,128]{2,1,0:T(8,128)S(1)}) custom-call(f32[40,16,128]{2,1,0:T(8,128)S(1)} %get-tuple-element.27.mass, f32[49,16,128]{2,1,0:T(8,128)S(1)} %coefficients.1.stencil, f32[392,128]{1,0:T(8,128)S(1)} %collective-permute-done.above, f32[392,128]{1,0:T(8,128)S(1)} %collective-permute-done.1.below, ...), custom_call_target="tpu_custom_call" | custom-call | flops 12000000 | bytes 1048576 | tf_op jit(solution)/shard_map/both_steps/pallas_call | solution.py:662
  18.6 0.0 collective-permute-done.2.got_a
  18.6 0.0 collective-permute-done.3.got_b
  18.6 0.6 %side_coefficients.1 = (f32[3,32,128]{2,1,0:T(8,128)S(1)}, f32[3,32,128]{2,1,0:T(8,128)S(1)}, f32[49,24,128]{2,1,0:T(8,128)S(1)}, f32[49,24,128]{2,1,0:T(8,128)S(1)}) custom-call(f32[49,24,128]{2,1,0:T(8,128)S(1)} %get-tuple-element.36.wide, f32[112,128]{1,0:T(8,128)S(1)} %get-tuple-element.39.send_a, f32[112,128]{1,0:T(8,128)S(1)} %get-tuple-element.40.send_b, ...), custom_call_target="tpu_custom_call" | custom-call | flops 4000000 | bytes 1048576 | tf_op jit(solution)/shard_map/side_coefficients/pallas_call | solution.py:673
  19.2 1.4 %halo_steps.1 = f32[40,16,128]{2,1,0:T(8,128)} custom-call(f32[3,32,128]{2,1,0:T(8,128)S(1)} %get-tuple-element.42.right_set, f32[3,32,128]{2,1,0:T(8,128)S(1)} %get-tuple-element.43.left_set, f32[49,24,128]{2,1,0:T(8,128)S(1)} %get-tuple-element.44.right_coef, f32[49,24,128]{2,1,0:T(8,128)S(1)} %get-tuple-element.45.left_coef, ...), custom_call_target="tpu_custom_call" | custom-call | flops 4000000 | bytes 1048576 | tf_op jit(solution)/shard_map/halo_steps/pallas_call | solution.py:684
Async XLA Ops:
  1.7 6.6 %collective-permute-start = (f32[392,128]{1,0:T(8,128)S(1)}, f32[392,128]{1,0:T(8,128)S(1)}, u32[]{:S(2)}, u32[]{:S(2)}) collective-permute-start(f32[392,128]{1,0:T(8,128)S(1)} %get-tuple-element.31), channel_id=1, source_target_pairs={{0,4},{4,8},{8,12},{12,16},{16,20},{20,24},{24,28},{28,0},{1,5},{5... | collective-permute-start | bytes 602120 | tf_op jit(solution)/shard_map/ppermute | solution.py:46
  4.4 5.6 %collective-permute-start.1 = (f32[392,128]{1,0:T(8,128)S(1)}, f32[392,128]{1,0:T(8,128)S(1)}, u32[]{:S(2)}, u32[]{:S(2)}) collective-permute-start(f32[392,128]{1,0:T(8,128)S(1)} %get-tuple-element.32), channel_id=1, source_target_pairs={{0,28},{4,0},{8,4},{12,8},{16,12},{20,16},{24,20},{28,24},{1,29},{... | collective-permute-start | bytes 602120 | tf_op jit(solution)/shard_map/ppermute | solution.py:46
  10.5 8.1 %collective-permute-start.2 = (f32[112,128]{1,0:T(8,128)S(1)}, f32[112,128]{1,0:T(8,128)S(1)}, u32[]{:S(2)}, u32[]{:S(2)}) collective-permute-start(f32[112,128]{1,0:T(8,128)S(1)} %get-tuple-element.39.send_a), channel_id=1, source_target_pairs={{0,1},{1,0},{2,3},{3,2},{4,5},{5,4},{6,7},{7,6},{8,9},{9,8},{10,11... | collective-permute-start | bytes 172040 | tf_op jit(solution)/shard_map/ppermute | solution.py:41
  12.6 6.0 %collective-permute-start.3 = (f32[112,128]{1,0:T(8,128)S(1)}, f32[112,128]{1,0:T(8,128)S(1)}, u32[]{:S(2)}, u32[]{:S(2)}) collective-permute-start(f32[112,128]{1,0:T(8,128)S(1)} %get-tuple-element.40.send_b), channel_id=1, source_target_pairs={{0,3},{1,2},{2,1},{3,0},{4,7},{5,6},{6,5},{7,4},{8,11},{9,10},{10,... | collective-permute-start | bytes 172040 | tf_op jit(solution)/shard_map/ppermute | solution.py:41

commit v5 on v4

--- a/solution.py
+++ b/solution.py
@@ -32,13 +32,19 @@
     return pl.CostEstimate(flops=operations, bytes_accessed=1 << 20, transcendentals=0)
 
 
-def swap(block, axes, odd_first):
-    count = lax.axis_size(axes)
-    partner = list(range(count))
-    for low in range(1 if odd_first else 0, count, 2):
-        high = (low + 1) % count
-        partner[low], partner[high] = high, low
-    return lax.ppermute(block, axes, list(enumerate(partner)))
+def column_swap(block, odd_first):
+    chains, count = lax.axis_size(ROW_AXES), lax.axis_size(COLUMN_AXES)
+    column = list(range(count))
+    for low in range(1 if odd_first else 0, count - 1, 2):
+        column[low], column[low + 1] = low + 1, low
+    pairs = []
+    for chain in range(chains):
+        for place in range(count):
+            target = (chain, column[place])
+            if column[place] == place and chains % 2 == 0:
+                target = (chain ^ 1, place)
+            pairs.append((chain * count + place, target[0] * count + target[1]))
+    return lax.ppermute(block, ROW_AXES + (COLUMN_AXES,), pairs)
 
 
 def shift(block, axes, step):
@@ -177,13 +183,13 @@
     for s in range(PER * tile, min(stacks, PER * tile + PER)):
         at = SPAN * (s % PER)
         moved = turn(load(s), at - 122)
-        right = jnp.where((lane >= at) & (lane < at + 6), moved, right)
-        left = jnp.where(on_ring(lane, at + 6, at + 12), moved, left)
+        right = jnp.where(lane >= at, moved, right)
+        left = jnp.where(from_place(lane, at + 6, at + 12), moved, left)
     return turn(left, -3), right
 
 
-def on_ring(lane, low, high):
-    return (lane >= low) | (lane < high - 128) if high > 128 else (lane >= low) & (lane < high)
+def from_place(lane, low, high):
+    return (lane >= low) | (lane < high - 128) if high > 128 else lane >= low
 
 
 def pack_coefficients(load):
@@ -193,8 +199,8 @@
     for o in range(COEF_PER):
         at = 3 * o
         moved = turn(load(o), at - 125)
-        right = jnp.where((lane >= at) & (lane < at + 3), moved, right)
-        left = jnp.where(on_ring(lane, at + 3, at + 6), moved, left)
+        right = jnp.where(lane >= at, moved, right)
+        left = jnp.where(from_place(lane, at + 3, at + 6), moved, left)
     return turn(left, -3), right
 
 
@@ -347,14 +353,15 @@
 
         shift_rows(lambda o: stencil[o, rows, :], store)
 
-    def some_stacks(group, carry):
-        for tile in range((width - 8) // 8):
-            total = main_sum(lambda k, at: mass[group * GROUP + k, 2 + at : 10 + at, :], own_shifted, 5, tile)
-            for k in range(GROUP):
-                middle[group * GROUP + k, 8 * tile : 8 * tile + 8, :] = total[k]
+    def some_stacks(turn_at, carry):
+        for_groups(
+            turn_at, stacks, range((width - 8) // 8), own_shifted, 5,
+            lambda s, tile, at: mass[s, 2 + at : 10 + at, :],
+            lambda s, tile, value: store_rows(middle, s, 8 * tile, value),
+        )
         return carry
 
-    lax.fori_loop(0, stacks // GROUP, some_stacks, 0)
+    lax.fori_loop(0, turns(stacks), some_stacks, 0)
     for dy in range(7):
         value = jnp.concatenate([stencil[dx * 7 + dy, :, :] for dx in range(7)], axis=0)
         spread = replicate(value, near[dy])
@@ -366,52 +373,91 @@
 def both_steps(mass, stencil, above, below, middle, own_shifted, second, wide, shifted, field, partial):
     stacks, width = mass.shape[:2]
     first, last = ends(ROW_AXES)
+    coefs = 6 * stacks
     for s in range(stacks):
-        at = 6 * s
-        field[s, 0:6, :] = jnp.where(first, 0.0, above[at : at + 6, :])
-        field[s, 6 : width + 6, :] = mass[s, :, :]
-        field[s, width + 6 : width + 12, :] = jnp.where(last, 0.0, below[at : at + 6, :])
-        field[s, width + 12 : width + 16, :] = jnp.zeros((4, 128), F32)
+        field[0, s, 2:8, :] = above[6 * s : 6 * s + 6, :]
+        field[0, s, 8:16, :] = mass[s, 0:8, :]
+        field[1, s, 0:8, :] = mass[s, width - 8 : width, :]
+        field[1, s, 8:16, :] = below[6 * s : 6 * s + 8, :]
     for o in range(OFFSETS):
-        at = 6 * stacks + 3 * o
-        wide[o, 0:3, :] = jnp.where(first, 0.0, above[at : at + 3, :])
+        at = coefs + 3 * o
+        wide[o, 0:3, :] = above[at : at + 3, :]
         wide[o, 3 : width + 3, :] = stencil[o, :, :]
-        wide[o, width + 3 : width + 6, :] = jnp.where(last, 0.0, below[at : at + 3, :])
+        wide[o, width + 3 : width + 6, :] = below[at : at + 3, :]
         wide[o, width + 6 : width + 8, :] = jnp.zeros((2, 128), F32)
-    tiles = (0, width // 8)
-    for tile in tiles:
+
+    @pl.when(first)
+    def _():
+        for s in range(stacks):
+            field[0, s, 2:8, :] = jnp.zeros((6, 128), F32)
+        for o in range(OFFSETS):
+            wide[o, 0:3, :] = jnp.zeros((3, 128), F32)
+
+    @pl.when(last)
+    def _():
+        for s in range(stacks):
+            field[1, s, 8:16, :] = jnp.zeros((8, 128), F32)
+        for o in range(OFFSETS):
+            wide[o, width + 3 : width + 6, :] = jnp.zeros((3, 128), F32)
+
+    for end, tile in enumerate((0, width // 8)):
         rows = pl.ds(8 * tile, 8)
 
         def store(o, value):
-            shifted[o, rows, :] = value
+            shifted[end, o, :, :] = value
 
         shift_rows(lambda o: wide[o, rows, :], store)
 
-    def first_step(group, carry):
-        totals = [
-            main_sum(lambda k, at: field[group * GROUP + k, at : at + 8, :], shifted, 0, tile)
-            for tile in tiles
+    def first_step(turn_at, carry):
+        sums = [
+            for_groups(
+                turn_at, stacks, (0,), shifted.at[end], 0, lambda s, tile, at: field[end, s, 2 + at : 10 + at, :]
+            )
+            for end in range(2)
         ]
-        for k in range(GROUP):
-            s = group * GROUP + k
+        for end, tile in enumerate((0, width // 8)):
+            for s, _, value in sums[end]:
+                store_rows(partial, s, 8 * tile, value)
+        for s, _, _ in sums[0]:
             partial[s, 8:width, :] = middle[s, :, :]
-            for tile, total in zip(tiles, totals):
-                partial[s, 8 * tile : 8 * tile + 8, :] = total[k]
         return carry
 
-    lax.fori_loop(0, stacks // GROUP, first_step, 0)
-
-    def second_step(group, carry):
-        totals = [
-            main_sum(lambda k, at: partial[group * GROUP + k, at : at + 8, :], own_shifted, 0, tile)
-            for tile in range(width // 8)
-        ]
-        for k in range(GROUP):
-            for tile, total in enumerate(totals):
-                second[group * GROUP + k, 8 * tile : 8 * tile + 8, :] = total[k]
+    lax.fori_loop(0, turns(stacks), first_step, 0)
+
+    def second_step(turn_at, carry):
+        for_groups(
+            turn_at, stacks, range(width // 8), own_shifted, 0,
+            lambda s, tile, at: partial[s, at : at + 8, :],
+            lambda s, tile, value: store_rows(second, s, 8 * tile, value),
+        )
         return carry
 
-    lax.fori_loop(0, stacks // GROUP, second_step, 0)
+    lax.fori_loop(0, turns(stacks), second_step, 0)
+
+
+def store_rows(target, s, at, value):
+    target[s, at : at + 8, :] = value
+
+
+def per_turn(stacks):
+    return 2 * GROUP if stacks % (2 * GROUP) == 0 else GROUP
+
+
+def turns(stacks):
+    return stacks // per_turn(stacks)
+
+
+def for_groups(turn_at, stacks, tiles, coef, coef_at, load, store=None):
+    sums = []
+    for part in range(per_turn(stacks) // GROUP):
+        start = turn_at * per_turn(stacks) + part * GROUP
+        for tile in tiles:
+            total = main_sum(lambda k, at: load(start + k, tile, at), coef, coef_at, tile)
+            sums += [(start + k, tile, total[k]) for k in range(GROUP)]
+    if store is not None:
+        for s, tile, value in sums:
+            store(s, tile, value)
+    return sums
 
 
 def packed_sum(load, coef, coef_at, tile, tiles, dys):
@@ -656,15 +702,15 @@
         cost_estimate=cost(10**6),
         name="pack_all",
     )(own_left, own_right, above, below, middle)
-    column_a = swap(send_a, COLUMN_AXES, False)
-    column_b = swap(send_b, COLUMN_AXES, True)
+    column_a = column_swap(send_a, False)
+    column_b = column_swap(send_b, True)
 
     second, wide = pl.pallas_call(
         both_steps,
         out_shape=(shape(stacks, width, 128), shape(OFFSETS, low, 128)),
         in_specs=[VMEM] * 6,
         out_specs=(VMEM,) * 2,
-        scratch_shapes=[scratch(OFFSETS, low, 128), scratch(stacks, tall, 128), scratch(stacks, low, 128)],
+        scratch_shapes=[scratch(2, OFFSETS, 8, 128), scratch(2, stacks, 16, 128), scratch(stacks, low, 128)],
         compiler_params=params(),
         cost_estimate=cost(12 * 10**6),
         name="both_steps",

time: 20.9 us -> 18.6 us (0.89)
  the two profiles are of different devices: /device:TPU:1 before, /device:TPU:0 now
where the time goes in v5:
time: 18.6 us; the launch traced here: 18.3 us
  Pallas kernels  10.9 us (59%)
  starting transfers between devices  7.33 us (39%)
    ppermute x2, starting transfers between devices, column_swap(): return lax.ppermute(block, ROW_AXES + (COLUMN_AXES,), pairs)  3.88 us
    ppermute x2, starting transfers between devices, shift(): lax.ppermute(block, axes, [(index, (index + step) % count) for index in r...  3.45 us
    pallas_call x1, Pallas kernels, local(): pl.pallas_call(both_steps, out_shape=(shape(stacks, width, 128), shape(OF...  3.22 us
    pallas_call x1, Pallas kernels, local(): pl.pallas_call(edge_rows, out_shape=(whole(tracer_mass), whole(intersecti...  1.7 us
    pallas_call x1, Pallas kernels, local(): pl.pallas_call(coefficients, out_shape=shape(OFFSETS, width, 128), in_spe...  1.58 us
    pallas_call x1, Pallas kernels, local(): pl.pallas_call(halo_steps, out_shape=shape(stacks, width, columns), in_sp...  1.44 us
    pallas_call x1, Pallas kernels, local(): pl.pallas_call(own_part, out_shape=(shape(stacks, width - 8, 128),) + (sh...  1.27 us
    pallas_call x1, Pallas kernels, local(): pl.pallas_call(pack_own, out_shape=(shape(width * (tiles + 1), 128),) * 2...  0.66 us
  transfers between devices with their start and end apart: 4, of which 0 were waited for; matrix products, arithmetic and copies ran while one was open for 0% of the time, Pallas kernels for 37%

profile of v5, /device:TPU:0, one launch (start us, length us, event | category | flops | bytes accessed | tf_op | source)
XLA Modules:
  0.0 18.3 jit_solution(5174011909826417062)
XLA Ops:
  0.0 1.7 %edge_rows.1 = (f32[40,16,128]{2,1,0:T(8,128)S(1)}, f32[4,10,16,128]{3,2,1,0:T(8,128)S(1)}, s32[4,16,128]{2,1,0:T(8,128)S(1)}, s32[4,16,128]{2,1,0:T(8,128)S(1)}...) custom-call(f32[10,25]{1,0:T(8,128)} %recon_hbm.3, f32[40,16,128]{2,1,0:T(8,128)} %mass_hbm.1, ...), custom_call_target="tpu_custom_call" | custom-call | flops 4000000 | bytes 1048576 | tf_op jit(solution)/shard_map/edge_rows/pallas_call | solution.py:633
  1.7 0.5 %collective-permute-start = (f32[392,128]{1,0:T(8,128)S(1)}, f32[392,128]{1,0:T(8,128)S(1)}, u32[]{:S(2)}, u32[]{:S(2)}) collective-permute-start(f32[392,128]{1,0:T(8,128)S(1)} %get-tuple-element.31), channel_id=1, source_target_pairs={{0,4},{4,8},{8,12},{12,16},{16,20},{20,24},{24,28},{28,0},{1,5},{5... | collective-permute-start | bytes 602120 | tf_op jit(solution)/shard_map/ppermute | solution.py:52
  2.2 2.9 %collective-permute-start.1 = (f32[392,128]{1,0:T(8,128)S(1)}, f32[392,128]{1,0:T(8,128)S(1)}, u32[]{:S(2)}, u32[]{:S(2)}) collective-permute-start(f32[392,128]{1,0:T(8,128)S(1)} %get-tuple-element.32), channel_id=1, source_target_pairs={{0,28},{4,0},{8,4},{12,8},{16,12},{20,16},{24,20},{28,24},{1,29},{... | collective-permute-start | bytes 602120 | tf_op jit(solution)/shard_map/ppermute | solution.py:52
  5.2 1.6 %coefficients.1.stencil = f32[49,16,128]{2,1,0:T(8,128)S(1)} custom-call(f32[10,25]{1,0:T(8,128)} %recon_hbm.3, f32[4,10,16,128]{3,2,1,0:T(8,128)S(1)} %get-tuple-element.28.weights, s32[4,16,128]{2,1,0:T(8,128)S(1)} %get-tuple-element.29.cells, s32[4,16,128]{2,1,0:T(8,128)S(1)} %get-tuple-element.30.codes), custom_call_target="tpu_custom_call" | custom-call | flops 8000000 | bytes 1048576 | tf_op jit(solution)/shard_map/coefficients/pallas_call | solution.py:658
  6.8 0.7 %pack_own.1 = (f32[64,128]{1,0:T(8,128)S(1)}, f32[64,128]{1,0:T(8,128)S(1)}, bf16[7,256,256]{2,1,0:T(8,128)(2,1)S(1)}, bf16[7,256,256]{2,1,0:T(8,128)(2,1)S(1)}) custom-call(f32[40,16,128]{2,1,0:T(8,128)S(1)} %get-tuple-element.27.mass, f32[49,16,128]{2,1,0:T(8,128)S(1)} %coefficients.1.stencil), custom_call_target="tpu_custom_call" | custom-call | flops 1000000 | bytes 1048576 | tf_op jit(solution)/shard_map/pack_own/pallas_call | solution.py:674
  7.4 1.3 %own_part.1 = (f32[40,8,128]{2,1,0:T(8,128)S(1)}, f32[49,16,128]{2,1,0:T(8,128)S(1)}, f32[49,16,128]{2,1,0:T(8,128)S(1)}, f32[49,16,128]{2,1,0:T(8,128)S(1)}) custom-call(f32[40,16,128]{2,1,0:T(8,128)S(1)} %get-tuple-element.27.mass, f32[49,16,128]{2,1,0:T(8,128)S(1)} %coefficients.1.stencil, bf16[7,256,256]{2,1,0:T(8,128)(2,1)S(1)} %get-tuple-element.33.near), custom_call_target="tpu_custom_call" | custom-call | flops 4000000 | bytes 1048576 | tf_op jit(solution)/shard_map/own_part/pallas_call | solution.py:684
  8.7 0.0 collective-permute-done.above
  8.7 0.0 collective-permute-done.1.below
  8.7 0.4 %pack_all.1 = (f32[112,128]{1,0:T(8,128)S(1)}, f32[112,128]{1,0:T(8,128)S(1)}) custom-call(f32[64,128]{1,0:T(8,128)S(1)} %get-tuple-element.37.own_left, f32[64,128]{1,0:T(8,128)S(1)} %get-tuple-element.38.own_right, f32[392,128]{1,0:T(8,128)S(1)} %collective-permute-done.above, f32[392,128]{1,0:T(8,128)S(1)} %collective-permute-done.1.below, ...), custom_call_target="tpu_custom_call" | custom-call | flops 1000000 | bytes 1048576 | tf_op jit(solution)/shard_map/pack_all/pallas_call | solution.py:695
  9.2 2.3 %collective-permute-start.2 = (f32[112,128]{1,0:T(8,128)S(1)}, f32[112,128]{1,0:T(8,128)S(1)}, u32[]{:S(2)}, u32[]{:S(2)}) collective-permute-start(f32[112,128]{1,0:T(8,128)S(1)} %get-tuple-element.39.send_a), channel_id=1, source_target_pairs={{0,1},{1,0},{2,3},{3,2},{4,5},{5,4},{6,7},{7,6},{8,9},{9,8},{10,11... | collective-permute-start | bytes 172040 | tf_op jit(solution)/shard_map/ppermute | solution.py:47
  11.5 1.5 %collective-permute-start.3 = (f32[112,128]{1,0:T(8,128)S(1)}, f32[112,128]{1,0:T(8,128)S(1)}, u32[]{:S(2)}, u32[]{:S(2)}) collective-permute-start(f32[112,128]{1,0:T(8,128)S(1)} %get-tuple-element.40.send_b), channel_id=1, source_target_pairs={{0,4},{1,2},{2,1},{3,7},{4,0},{5,6},{6,5},{7,3},{8,12},{9,10},{10,... | collective-permute-start | bytes 172040 | tf_op jit(solution)/shard_map/ppermute | solution.py:47
  13.0 3.2 %both_steps.1 = (f32[40,16,128]{2,1,0:T(8,128)S(1)}, f32[49,24,128]{2,1,0:T(8,128)S(1)}) custom-call(f32[40,16,128]{2,1,0:T(8,128)S(1)} %get-tuple-element.27.mass, f32[49,16,128]{2,1,0:T(8,128)S(1)} %coefficients.1.stencil, f32[392,128]{1,0:T(8,128)S(1)} %collective-permute-done.above, f32[392,128]{1,0:T(8,128)S(1)} %collective-permute-done.1.below, ...), custom_call_target="tpu_custom_call" | custom-call | flops 12000000 | bytes 1048576 | tf_op jit(solution)/shard_map/both_steps/pallas_call | solution.py:708
  16.3 0.0 collective-permute-done.2.got_a
  16.3 0.0 collective-permute-done.3.got_b
  16.3 0.6 %side_coefficients.1 = (f32[3,32,128]{2,1,0:T(8,128)S(1)}, f32[3,32,128]{2,1,0:T(8,128)S(1)}, f32[49,24,128]{2,1,0:T(8,128)S(1)}, f32[49,24,128]{2,1,0:T(8,128)S(1)}) custom-call(f32[49,24,128]{2,1,0:T(8,128)S(1)} %get-tuple-element.36.wide, f32[112,128]{1,0:T(8,128)S(1)} %get-tuple-element.39.send_a, f32[112,128]{1,0:T(8,128)S(1)} %get-tuple-element.40.send_b, ...), custom_call_target="tpu_custom_call" | custom-call | flops 4000000 | bytes 1048576 | tf_op jit(solution)/shard_map/side_coefficients/pallas_call | solution.py:719
  16.9 1.4 %halo_steps.1 = f32[40,16,128]{2,1,0:T(8,128)} custom-call(f32[3,32,128]{2,1,0:T(8,128)S(1)} %get-tuple-element.42.right_set, f32[3,32,128]{2,1,0:T(8,128)S(1)} %get-tuple-element.43.left_set, f32[49,24,128]{2,1,0:T(8,128)S(1)} %get-tuple-element.44.right_coef, f32[49,24,128]{2,1,0:T(8,128)S(1)} %get-tuple-element.45.left_coef, ...), custom_call_target="tpu_custom_call" | custom-call | flops 4000000 | bytes 1048576 | tf_op jit(solution)/shard_map/halo_steps/pallas_call | solution.py:730
Async XLA Ops:
  1.7 7.0 %collective-permute-start = (f32[392,128]{1,0:T(8,128)S(1)}, f32[392,128]{1,0:T(8,128)S(1)}, u32[]{:S(2)}, u32[]{:S(2)}) collective-permute-start(f32[392,128]{1,0:T(8,128)S(1)} %get-tuple-element.31), channel_id=1, source_target_pairs={{0,4},{4,8},{8,12},{12,16},{16,20},{20,24},{24,28},{28,0},{1,5},{5... | collective-permute-start | bytes 602120 | tf_op jit(solution)/shard_map/ppermute | solution.py:52
  2.2 6.5 %collective-permute-start.1 = (f32[392,128]{1,0:T(8,128)S(1)}, f32[392,128]{1,0:T(8,128)S(1)}, u32[]{:S(2)}, u32[]{:S(2)}) collective-permute-start(f32[392,128]{1,0:T(8,128)S(1)} %get-tuple-element.32), channel_id=1, source_target_pairs={{0,28},{4,0},{8,4},{12,8},{16,12},{20,16},{24,20},{28,24},{1,29},{... | collective-permute-start | bytes 602120 | tf_op jit(solution)/shard_map/ppermute | solution.py:52
  9.2 7.1 %collective-permute-start.2 = (f32[112,128]{1,0:T(8,128)S(1)}, f32[112,128]{1,0:T(8,128)S(1)}, u32[]{:S(2)}, u32[]{:S(2)}) collective-permute-start(f32[112,128]{1,0:T(8,128)S(1)} %get-tuple-element.39.send_a), channel_id=1, source_target_pairs={{0,1},{1,0},{2,3},{3,2},{4,5},{5,4},{6,7},{7,6},{8,9},{9,8},{10,11... | collective-permute-start | bytes 172040 | tf_op jit(solution)/shard_map/ppermute | solution.py:47
  11.5 4.8 %collective-permute-start.3 = (f32[112,128]{1,0:T(8,128)S(1)}, f32[112,128]{1,0:T(8,128)S(1)}, u32[]{:S(2)}, u32[]{:S(2)}) collective-permute-start(f32[112,128]{1,0:T(8,128)S(1)} %get-tuple-element.40.send_b), channel_id=1, source_target_pairs={{0,4},{1,2},{2,1},{3,7},{4,0},{5,6},{6,5},{7,3},{8,12},{9,10},{10,... | collective-permute-start | bytes 172040 | tf_op jit(solution)/shard_map/ppermute | solution.py:47

commit v6 on v5

--- a/solution.py
+++ b/solution.py
@@ -70,7 +70,7 @@
     return lax.broadcasted_iota(jnp.int32, (rows, 128), 1)
 
 
-def fill_stencil(recon, weights, cells, codes, turned, spread, stencil, tiles):
+def fill_stencil(recon, weights, cells, codes, turned, spread, stencil, tiles, before_taps):
     zero = jnp.zeros((8, 128), F32)
     for g in range(tiles):
         rows = pl.ds(8 * g, 8)
@@ -94,6 +94,7 @@
                 turned[t, m * tiles + g] = value
 
     combos = 4 * tiles
+    before_taps()
 
     def five_taps(jx, carry):
         total = [[None] * combos for jy in range(5)]
@@ -153,14 +154,17 @@
     copies = [pltpu.make_async_copy(a, b, sems.at[i]) for i, (a, b) in enumerate(zip(sources, targets))]
     for copy in copies:
         copy.start()
-    for copy in copies:
+    for copy in copies[1:4]:
         copy.wait()
     stacks, width = mass.shape[:2]
     for target, source in ((edge_weights, weights), (edge_cells, cells), (edge_codes, codes)):
         for index in np.ndindex(*source.shape[:-2]):
             target[index + (slice(0, 3), slice(None))] = source[index + (slice(0, 3), slice(None))]
             target[index + (slice(3, 8), slice(None))] = source[index + (slice(width - 5, width), slice(None))]
-    fill_stencil(recon, edge_weights, edge_cells, edge_codes, turned, spread, edge_stencil, 1)
+    fill_stencil(
+        recon, edge_weights, edge_cells, edge_codes, turned, spread, edge_stencil, 1, copies[0].wait
+    )
+    copies[4].wait()
     for send, mass_at, stencil_at in ((send_down, width - 6, 5), (send_up, 0, 0)):
         for s in range(stacks):
             send[6 * s : 6 * s + 6, :] = mass[s, mass_at : mass_at + 6, :]
@@ -172,8 +176,7 @@
 def coefficients(recon_hbm, weights, cells, codes, stencil, recon, turned, spread, sem):
     copy = pltpu.make_async_copy(recon_hbm, recon, sem.at[0])
     copy.start()
-    copy.wait()
-    fill_stencil(recon, weights, cells, codes, turned, spread, stencil, stencil.shape[1] // 8)
+    fill_stencil(recon, weights, cells, codes, turned, spread, stencil, stencil.shape[1] // 8, copy.wait)
 
 
 def pack_stacks(load, stacks, tile):
@@ -274,31 +277,28 @@
     tiles = -(-stacks // PER)
     width = own_left.shape[0] // (tiles + 1)
     tall = width + 12
+    first, last = ends(ROW_AXES)
+    top_rows = lax.broadcasted_iota(jnp.int32, (8, 128), 0) < 3
+    ready = []
+    for got, outside, place, coef_place in (
+        (above, first, width, width), (below, last, width + 6, width + 3)
+    ):
+        coef = lambda o: got[6 * stacks + 3 * o : 6 * stacks + 3 * o + 8, :]
+        for tile in range(tiles):
+            packed = pack_stacks(lambda s: got[6 * s : 6 * s + 8, :], stacks, tile)
+            if tile == 0:
+                spare = add_spare(coef, *packed)
+                packed = [jnp.where(top_rows, new, old) for new, old in zip(spare, packed)]
+            ready.append((tall * tile + place, 6, outside, packed))
+        ready.append((tall * tiles + coef_place, 3, outside, pack_coefficients(coef)))
+    for at, count, outside, packed in ready:
+        for send, value in zip((left, right), packed):
+            send[at : at + count, :] = jnp.where(outside, 0.0, value[0:count])
     for send, own in ((left, own_left), (right, own_right)):
         for tile in range(tiles + 1):
             send[tall * tile : tall * tile + width, :] = own[width * tile : width * tile + width, :]
         end = tall * tiles + width + 6
         send[end:, :] = jnp.zeros((send.shape[0] - end, 128), F32)
-    first, last = ends(ROW_AXES)
-    for got, outside, place, coef_place in (
-        (above, first, width, width), (below, last, width + 6, width + 3)
-    ):
-        coef = lambda o: got[6 * stacks + 3 * o : 6 * stacks + 3 * o + 8, :]
-        for tile in range(tiles):
-            at = tall * tile + place
-            packed = pack_stacks(lambda s: got[6 * s : 6 * s + 8, :], stacks, tile)
-            if tile == 0:
-                spare = add_spare(coef, *packed)
-                packed = [
-                    jnp.where(lax.broadcasted_iota(jnp.int32, (8, 128), 0) < 3, with_spare, without)
-                    for with_spare, without in zip(spare, packed)
-                ]
-            left[at : at + 6, :] = jnp.where(outside, 0.0, packed[0][0:6])
-            right[at : at + 6, :] = jnp.where(outside, 0.0, packed[1][0:6])
-        at = tall * tiles + coef_place
-        packed = pack_coefficients(coef)
-        left[at : at + 3, :] = jnp.where(outside, 0.0, packed[0][0:3])
-        right[at : at + 3, :] = jnp.where(outside, 0.0, packed[1][0:3])
     choose(is_even(COLUMN_AXES), right, left, send_a, send_b)
 
 
@@ -331,16 +331,19 @@
     return total
 
 
-def shift_rows(load, store, dys=range(-3, 4)):
+def shift_rows(load, store):
     lane = lanes()
-    for dy in dys:
-        values = [turn(load(dx * 7 + dy + 3), dy) for dx in range(7)]
+    values = []
+    for o in range(OFFSETS):
+        dy = o % 7 - 3
+        value = turn(load(o), dy)
         if dy > 0:
-            values = [jnp.where(lane >= dy, value, 0.0) for value in values]
+            value = jnp.where(lane >= dy, value, 0.0)
         elif dy < 0:
-            values = [jnp.where(lane < 128 + dy, value, 0.0) for value in values]
-        for dx in range(7):
-            store(dx * 7 + dy + 3, values[dx])
+            value = jnp.where(lane < 128 + dy, value, 0.0)
+        values.append(value)
+    for o, value in enumerate(values):
+        store(o, value)
 
 
 def own_part(mass, stencil, near, middle, own_shifted, right_near, left_near):
@@ -538,23 +541,19 @@
         rows = pl.ds(8 * tile, 8)
         right_rows = [right_halo[t, rows, :] for t in range(2)]
         left_rows = [left_halo[t, rows, :] for t in range(2)]
-        for dy in range(7):
-            values = []
-            for dx in range(7):
-                o = dx * 7 + dy
-                if o < COEF_PER:
-                    right = turn(right_rows[0], 60 - 3 * o)
-                    left = turn(left_rows[0], 64 - 3 * o)
-                else:
-                    at = SPAN * (o - COEF_PER)
-                    right = turn(right_rows[1], 60 - at)
-                    left = turn(left_rows[1], 58 - at)
-                values.append(
-                    jnp.where(from_right, right, jnp.where(from_left, left, wide[o, rows, :]))
-                )
-            for dx in range(7):
-                at = tall * dx + 8 * tile
-                rows_of[dy, at : at + 8, :] = values[dx]
+        values = []
+        for o in range(OFFSETS):
+            if o < COEF_PER:
+                right = turn(right_rows[0], 60 - 3 * o)
+                left = turn(left_rows[0], 64 - 3 * o)
+            else:
+                at = SPAN * (o - COEF_PER)
+                right = turn(right_rows[1], 60 - at)
+                left = turn(left_rows[1], 58 - at)
+            values.append(jnp.where(from_right, right, jnp.where(from_left, left, wide[o, rows, :])))
+        for o, value in enumerate(values):
+            at = tall * (o // 7) + 8 * tile
+            rows_of[o % 7, at : at + 8, :] = value
 
     for dy in range(7):
         spread = replicate(rows_of[dy], picks[dy])
@@ -565,34 +564,33 @@
 
 def halo_steps(
     right_set, left_set, right_coef, left_coef, right_near, left_near, second, out_hbm,
-    right_next, left_next, right_out, left_out, out, sems,
+    right_next, left_next, out, sems,
 ):
     tiles = right_set.shape[0]
     stacks, width = out.shape[:2]
     place = place_in_group()
     everywhere = range(-3, 4)
-    for tile in range(right_next.shape[1] // 8):
+    row_tiles = range(right_next.shape[1] // 8)
+    sums = [
+        [
+            packed_sum(lambda t, at: side[t, at : at + 8, :], coef, 0, tile, tiles, everywhere)
+            for side, coef in ((right_set, right_coef), (left_set, left_coef))
+        ]
+        for tile in row_tiles
+    ]
+    for tile in row_tiles:
+        right, left = sums[tile]
         rows = pl.ds(8 * tile, 8)
-        right = packed_sum(
-            lambda t, at: right_set[t, at : at + 8, :], right_coef, 0, tile, tiles, everywhere
-        )
-        left = packed_sum(
-            lambda t, at: left_set[t, at : at + 8, :], left_coef, 0, tile, tiles, everywhere
-        )
         for t in range(tiles):
             right_next[t, rows, :] = jnp.where(place >= 3, turn(right[t], 3), 0.0)
             left_next[t, rows, :] = jnp.where(place < 6, turn(left[t], -3), 0.0)
-    for tile in range(width // 8):
-        rows = pl.ds(8 * tile, 8)
-        right = packed_sum(
-            lambda t, at: right_next[t, at : at + 8, :], right_near, 0, tile, tiles, everywhere
-        )
-        left = packed_sum(
-            lambda t, at: left_next[t, at : at + 8, :], left_near, 0, tile, tiles, everywhere
-        )
-        for t in range(tiles):
-            right_out[t, rows, :] = right[t]
-            left_out[t, rows, :] = left[t]
+    changes = [
+        [
+            packed_sum(lambda t, at: side[t, at : at + 8, :], coef, 0, tile, tiles, everywhere)
+            for side, coef in ((right_next, right_near), (left_next, left_near))
+        ]
+        for tile in range(width // 8)
+    ]
 
     lane = lanes()
     copies = []
@@ -600,7 +598,7 @@
         low, high = PER * t, min(stacks, PER * t + PER)
         for tile in range(width // 8):
             rows = pl.ds(8 * tile, 8)
-            right, left = right_out[t, rows, :], left_out[t, rows, :]
+            right, left = (side[t] for side in changes[tile])
             values = []
             for s in range(low, high):
                 at = SPAN * (s - low)
@@ -732,7 +730,7 @@
         out_shape=shape(stacks, width, columns),
         in_specs=[VMEM] * 7,
         out_specs=HBM,
-        scratch_shapes=[scratch(tiles, low, 128)] * 2 + [scratch(tiles, width, 128)] * 2
+        scratch_shapes=[scratch(tiles, low, 128)] * 2
         + [scratch(stacks, width, columns), pltpu.SemaphoreType.DMA((tiles,))],
         compiler_params=params(),
         cost_estimate=cost(4 * 10**6),

time: 18.6 us -> 18.4 us (0.989)
  no operation moved by 1% of the time
where the time goes in v6:
time: 18.4 us; the launch traced here: 18.2 us
  Pallas kernels  10.8 us (59%)
  starting transfers between devices  7.36 us (40%)
    ppermute x2, starting transfers between devices, column_swap(): return lax.ppermute(block, ROW_AXES + (COLUMN_AXES,), pairs)  3.91 us
    ppermute x2, starting transfers between devices, shift(): lax.ppermute(block, axes, [(index, (index + step) % count) for index in r...  3.45 us
    pallas_call x1, Pallas kernels, local(): pl.pallas_call(both_steps, out_shape=(shape(stacks, width, 128), shape(OF...  3.22 us
    pallas_call x1, Pallas kernels, local(): pl.pallas_call(edge_rows, out_shape=(whole(tracer_mass), whole(intersecti...  1.61 us
    pallas_call x1, Pallas kernels, local(): pl.pallas_call(coefficients, out_shape=shape(OFFSETS, width, 128), in_spe...  1.55 us
    pallas_call x1, Pallas kernels, local(): pl.pallas_call(halo_steps, out_shape=shape(stacks, width, columns), in_sp...  1.4 us
    pallas_call x1, Pallas kernels, local(): pl.pallas_call(own_part, out_shape=(shape(stacks, width - 8, 128),) + (sh...  1.27 us
    pallas_call x1, Pallas kernels, local(): pl.pallas_call(pack_own, out_shape=(shape(width * (tiles + 1), 128),) * 2...  0.66 us
  transfers between devices with their start and end apart: 4, of which 0 were waited for; matrix products, arithmetic and copies ran while one was open for 0% of the time, Pallas kernels for 37%

profile of v6, /device:TPU:0, one launch (start us, length us, event | category | flops | bytes accessed | tf_op | source)
XLA Modules:
  0.0 18.2 jit_solution(1566654591964996503)
XLA Ops:
  0.0 1.6 %edge_rows.1 = (f32[40,16,128]{2,1,0:T(8,128)S(1)}, f32[4,10,16,128]{3,2,1,0:T(8,128)S(1)}, s32[4,16,128]{2,1,0:T(8,128)S(1)}, s32[4,16,128]{2,1,0:T(8,128)S(1)}...) custom-call(f32[10,25]{1,0:T(8,128)} %recon_hbm.3, f32[40,16,128]{2,1,0:T(8,128)} %mass_hbm.1, ...), custom_call_target="tpu_custom_call" | custom-call | flops 4000000 | bytes 1048576 | tf_op jit(solution)/shard_map/edge_rows/pallas_call | solution.py:631
  1.6 0.5 %collective-permute-start = (f32[392,128]{1,0:T(8,128)S(1)}, f32[392,128]{1,0:T(8,128)S(1)}, u32[]{:S(2)}, u32[]{:S(2)}) collective-permute-start(f32[392,128]{1,0:T(8,128)S(1)} %get-tuple-element.31), channel_id=1, source_target_pairs={{0,4},{4,8},{8,12},{12,16},{16,20},{20,24},{24,28},{28,0},{1,5},{5... | collective-permute-start | bytes 602120 | tf_op jit(solution)/shard_map/ppermute | solution.py:52
  2.1 2.9 %collective-permute-start.1 = (f32[392,128]{1,0:T(8,128)S(1)}, f32[392,128]{1,0:T(8,128)S(1)}, u32[]{:S(2)}, u32[]{:S(2)}) collective-permute-start(f32[392,128]{1,0:T(8,128)S(1)} %get-tuple-element.32), channel_id=1, source_target_pairs={{0,28},{4,0},{8,4},{12,8},{16,12},{20,16},{24,20},{28,24},{1,29},{... | collective-permute-start | bytes 602120 | tf_op jit(solution)/shard_map/ppermute | solution.py:52
  5.1 1.6 %coefficients.1.stencil = f32[49,16,128]{2,1,0:T(8,128)S(1)} custom-call(f32[10,25]{1,0:T(8,128)} %recon_hbm.3, f32[4,10,16,128]{3,2,1,0:T(8,128)S(1)} %get-tuple-element.28.weights, s32[4,16,128]{2,1,0:T(8,128)S(1)} %get-tuple-element.29.cells, s32[4,16,128]{2,1,0:T(8,128)S(1)} %get-tuple-element.30.codes), custom_call_target="tpu_custom_call" | custom-call | flops 8000000 | bytes 1048576 | tf_op jit(solution)/shard_map/coefficients/pallas_call | solution.py:656
  6.6 0.7 %pack_own.1 = (f32[64,128]{1,0:T(8,128)S(1)}, f32[64,128]{1,0:T(8,128)S(1)}, bf16[7,256,256]{2,1,0:T(8,128)(2,1)S(1)}, bf16[7,256,256]{2,1,0:T(8,128)(2,1)S(1)}) custom-call(f32[40,16,128]{2,1,0:T(8,128)S(1)} %get-tuple-element.27.mass, f32[49,16,128]{2,1,0:T(8,128)S(1)} %coefficients.1.stencil), custom_call_target="tpu_custom_call" | custom-call | flops 1000000 | bytes 1048576 | tf_op jit(solution)/shard_map/pack_own/pallas_call | solution.py:672
  7.3 1.3 %own_part.1 = (f32[40,8,128]{2,1,0:T(8,128)S(1)}, f32[49,16,128]{2,1,0:T(8,128)S(1)}, f32[49,16,128]{2,1,0:T(8,128)S(1)}, f32[49,16,128]{2,1,0:T(8,128)S(1)}) custom-call(f32[40,16,128]{2,1,0:T(8,128)S(1)} %get-tuple-element.27.mass, f32[49,16,128]{2,1,0:T(8,128)S(1)} %coefficients.1.stencil, bf16[7,256,256]{2,1,0:T(8,128)(2,1)S(1)} %get-tuple-element.33.near), custom_call_target="tpu_custom_call" | custom-call | flops 4000000 | bytes 1048576 | tf_op jit(solution)/shard_map/own_part/pallas_call | solution.py:682
  8.6 0.0 collective-permute-done.above
  8.6 0.0 collective-permute-done.1.below
  8.6 0.4 %pack_all.1 = (f32[112,128]{1,0:T(8,128)S(1)}, f32[112,128]{1,0:T(8,128)S(1)}) custom-call(f32[64,128]{1,0:T(8,128)S(1)} %get-tuple-element.37.own_left, f32[64,128]{1,0:T(8,128)S(1)} %get-tuple-element.38.own_right, f32[392,128]{1,0:T(8,128)S(1)} %collective-permute-done.above, f32[392,128]{1,0:T(8,128)S(1)} %collective-permute-done.1.below, ...), custom_call_target="tpu_custom_call" | custom-call | flops 1000000 | bytes 1048576 | tf_op jit(solution)/shard_map/pack_all/pallas_call | solution.py:693
  9.0 2.3 %collective-permute-start.2 = (f32[112,128]{1,0:T(8,128)S(1)}, f32[112,128]{1,0:T(8,128)S(1)}, u32[]{:S(2)}, u32[]{:S(2)}) collective-permute-start(f32[112,128]{1,0:T(8,128)S(1)} %get-tuple-element.39.send_a), channel_id=1, source_target_pairs={{0,1},{1,0},{2,3},{3,2},{4,5},{5,4},{6,7},{7,6},{8,9},{9,8},{10,11... | collective-permute-start | bytes 172040 | tf_op jit(solution)/shard_map/ppermute | solution.py:47
  11.4 1.6 %collective-permute-start.3 = (f32[112,128]{1,0:T(8,128)S(1)}, f32[112,128]{1,0:T(8,128)S(1)}, u32[]{:S(2)}, u32[]{:S(2)}) collective-permute-start(f32[112,128]{1,0:T(8,128)S(1)} %get-tuple-element.40.send_b), channel_id=1, source_target_pairs={{0,4},{1,2},{2,1},{3,7},{4,0},{5,6},{6,5},{7,3},{8,12},{9,10},{10,... | collective-permute-start | bytes 172040 | tf_op jit(solution)/shard_map/ppermute | solution.py:47
  13.0 3.2 %both_steps.1 = (f32[40,16,128]{2,1,0:T(8,128)S(1)}, f32[49,24,128]{2,1,0:T(8,128)S(1)}) custom-call(f32[40,16,128]{2,1,0:T(8,128)S(1)} %get-tuple-element.27.mass, f32[49,16,128]{2,1,0:T(8,128)S(1)} %coefficients.1.stencil, f32[392,128]{1,0:T(8,128)S(1)} %collective-permute-done.above, f32[392,128]{1,0:T(8,128)S(1)} %collective-permute-done.1.below, ...), custom_call_target="tpu_custom_call" | custom-call | flops 12000000 | bytes 1048576 | tf_op jit(solution)/shard_map/both_steps/pallas_call | solution.py:706
  16.2 0.0 collective-permute-done.2.got_a
  16.2 0.0 collective-permute-done.3.got_b
  16.2 0.6 %side_coefficients.1 = (f32[3,32,128]{2,1,0:T(8,128)S(1)}, f32[3,32,128]{2,1,0:T(8,128)S(1)}, f32[49,24,128]{2,1,0:T(8,128)S(1)}, f32[49,24,128]{2,1,0:T(8,128)S(1)}) custom-call(f32[49,24,128]{2,1,0:T(8,128)S(1)} %get-tuple-element.36.wide, f32[112,128]{1,0:T(8,128)S(1)} %get-tuple-element.39.send_a, f32[112,128]{1,0:T(8,128)S(1)} %get-tuple-element.40.send_b, ...), custom_call_target="tpu_custom_call" | custom-call | flops 4000000 | bytes 1048576 | tf_op jit(solution)/shard_map/side_coefficients/pallas_call | solution.py:717
  16.8 1.4 %halo_steps.1 = f32[40,16,128]{2,1,0:T(8,128)} custom-call(f32[3,32,128]{2,1,0:T(8,128)S(1)} %get-tuple-element.42.right_set, f32[3,32,128]{2,1,0:T(8,128)S(1)} %get-tuple-element.43.left_set, f32[49,24,128]{2,1,0:T(8,128)S(1)} %get-tuple-element.44.right_coef, f32[49,24,128]{2,1,0:T(8,128)S(1)} %get-tuple-element.45.left_coef, ...), custom_call_target="tpu_custom_call" | custom-call | flops 4000000 | bytes 1048576 | tf_op jit(solution)/shard_map/halo_steps/pallas_call | solution.py:728
Async XLA Ops:
  1.6 7.0 %collective-permute-start = (f32[392,128]{1,0:T(8,128)S(1)}, f32[392,128]{1,0:T(8,128)S(1)}, u32[]{:S(2)}, u32[]{:S(2)}) collective-permute-start(f32[392,128]{1,0:T(8,128)S(1)} %get-tuple-element.31), channel_id=1, source_target_pairs={{0,4},{4,8},{8,12},{12,16},{16,20},{20,24},{24,28},{28,0},{1,5},{5... | collective-permute-start | bytes 602120 | tf_op jit(solution)/shard_map/ppermute | solution.py:52
  2.1 6.5 %collective-permute-start.1 = (f32[392,128]{1,0:T(8,128)S(1)}, f32[392,128]{1,0:T(8,128)S(1)}, u32[]{:S(2)}, u32[]{:S(2)}) collective-permute-start(f32[392,128]{1,0:T(8,128)S(1)} %get-tuple-element.32), channel_id=1, source_target_pairs={{0,28},{4,0},{8,4},{12,8},{16,12},{20,16},{24,20},{28,24},{1,29},{... | collective-permute-start | bytes 602120 | tf_op jit(solution)/shard_map/ppermute | solution.py:52
  9.0 7.1 %collective-permute-start.2 = (f32[112,128]{1,0:T(8,128)S(1)}, f32[112,128]{1,0:T(8,128)S(1)}, u32[]{:S(2)}, u32[]{:S(2)}) collective-permute-start(f32[112,128]{1,0:T(8,128)S(1)} %get-tuple-element.39.send_a), channel_id=1, source_target_pairs={{0,1},{1,0},{2,3},{3,2},{4,5},{5,4},{6,7},{7,6},{8,9},{9,8},{10,11... | collective-permute-start | bytes 172040 | tf_op jit(solution)/shard_map/ppermute | solution.py:47
  11.4 4.8 %collective-permute-start.3 = (f32[112,128]{1,0:T(8,128)S(1)}, f32[112,128]{1,0:T(8,128)S(1)}, u32[]{:S(2)}, u32[]{:S(2)}) collective-permute-start(f32[112,128]{1,0:T(8,128)S(1)} %get-tuple-element.40.send_b), channel_id=1, source_target_pairs={{0,4},{1,2},{2,1},{3,7},{4,0},{5,6},{6,5},{7,3},{8,12},{9,10},{10,... | collective-permute-start | bytes 172040 | tf_op jit(solution)/shard_map/ppermute | solution.py:47

commit v7 on v6

--- a/solution.py
+++ b/solution.py
@@ -443,7 +443,7 @@
 
 
 def per_turn(stacks):
-    return 2 * GROUP if stacks % (2 * GROUP) == 0 else GROUP
+    return next(GROUP * groups for groups in (5, 2, 1) if stacks % (GROUP * groups) == 0)
 
 
 def turns(stacks):
@@ -486,7 +486,7 @@
 
 
 def side_coefficients(
-    wide, send_a, send_b, got_a, got_b, picks,
+    wide, send_a, send_b, got_b, got_a, picks,
     right_set, left_set, right_coef, left_coef, right_halo, left_halo, rows_of,
 ):
     tall = wide.shape[1]
@@ -700,8 +700,8 @@
         cost_estimate=cost(10**6),
         name="pack_all",
     )(own_left, own_right, above, below, middle)
+    column_b = column_swap(send_b, True)
     column_a = column_swap(send_a, False)
-    column_b = column_swap(send_b, True)
 
     second, wide = pl.pallas_call(
         both_steps,
@@ -723,7 +723,7 @@
         compiler_params=params(),
         cost_estimate=cost(4 * 10**6),
         name="side_coefficients",
-    )(wide, send_a, send_b, column_a, column_b, picks)
+    )(wide, send_a, send_b, column_b, column_a, picks)
 
     return pl.pallas_call(
         halo_steps,

time: 18.4 us -> 18.1 us (0.984)
  Pallas kernels: 10.8 us -> 10.4 us
    pallas_call x1, Pallas kernels: 3.22 us -> 2.97 us  [local(): pl.pallas_call(both_steps, out_shape=(shape(stacks, width, 128), shape(OF...]
  transfers between devices with their start and end apart: 4 -> 4, of which waited for: 0 -> 0; matrix products, arithmetic and copies ran while one was open for 0% -> 0% of each run, Pallas kernels for 37% -> 35%
where the time goes in v7:
time: 18.1 us; the launch traced here: 18 us
  Pallas kernels  10.4 us (57%)
  starting transfers between devices  7.49 us (41%)
    ppermute x2, starting transfers between devices, column_swap(): return lax.ppermute(block, ROW_AXES + (COLUMN_AXES,), pairs)  4.04 us
    ppermute x2, starting transfers between devices, shift(): lax.ppermute(block, axes, [(index, (index + step) % count) for index in r...  3.45 us
    pallas_call x1, Pallas kernels, local(): pl.pallas_call(both_steps, out_shape=(shape(stacks, width, 128), shape(OF...  2.97 us
    pallas_call x1, Pallas kernels, local(): pl.pallas_call(edge_rows, out_shape=(whole(tracer_mass), whole(intersecti...  1.61 us
    pallas_call x1, Pallas kernels, local(): pl.pallas_call(coefficients, out_shape=shape(OFFSETS, width, 128), in_spe...  1.55 us
    pallas_call x1, Pallas kernels, local(): pl.pallas_call(halo_steps, out_shape=shape(stacks, width, columns), in_sp...  1.4 us
    pallas_call x1, Pallas kernels, local(): pl.pallas_call(own_part, out_shape=(shape(stacks, width - 8, 128),) + (sh...  1.11 us
    pallas_call x1, Pallas kernels, local(): pl.pallas_call(pack_own, out_shape=(shape(width * (tiles + 1), 128),) * 2...  0.66 us
  transfers between devices with their start and end apart: 4, of which 0 were waited for; matrix products, arithmetic and copies ran while one was open for 0% of the time, Pallas kernels for 35%

profile of v7, /device:TPU:0, one launch (start us, length us, event | category | flops | bytes accessed | tf_op | source)
XLA Modules:
  0.0 18.0 jit_solution(7676431182747124019)
XLA Ops:
  0.0 1.6 %edge_rows.1 = (f32[40,16,128]{2,1,0:T(8,128)S(1)}, f32[4,10,16,128]{3,2,1,0:T(8,128)S(1)}, s32[4,16,128]{2,1,0:T(8,128)S(1)}, s32[4,16,128]{2,1,0:T(8,128)S(1)}...) custom-call(f32[10,25]{1,0:T(8,128)} %recon_hbm.3, f32[40,16,128]{2,1,0:T(8,128)} %mass_hbm.1, ...), custom_call_target="tpu_custom_call" | custom-call | flops 4000000 | bytes 1048576 | tf_op jit(solution)/shard_map/edge_rows/pallas_call | solution.py:631
  1.6 0.5 %collective-permute-start = (f32[392,128]{1,0:T(8,128)S(1)}, f32[392,128]{1,0:T(8,128)S(1)}, u32[]{:S(2)}, u32[]{:S(2)}) collective-permute-start(f32[392,128]{1,0:T(8,128)S(1)} %get-tuple-element.31), channel_id=1, source_target_pairs={{0,4},{4,8},{8,12},{12,16},{16,20},{20,24},{24,28},{28,0},{1,5},{5... | collective-permute-start | bytes 602120 | tf_op jit(solution)/shard_map/ppermute | solution.py:52
  2.1 2.9 %collective-permute-start.1 = (f32[392,128]{1,0:T(8,128)S(1)}, f32[392,128]{1,0:T(8,128)S(1)}, u32[]{:S(2)}, u32[]{:S(2)}) collective-permute-start(f32[392,128]{1,0:T(8,128)S(1)} %get-tuple-element.32), channel_id=1, source_target_pairs={{0,28},{4,0},{8,4},{12,8},{16,12},{20,16},{24,20},{28,24},{1,29},{... | collective-permute-start | bytes 602120 | tf_op jit(solution)/shard_map/ppermute | solution.py:52
  5.1 1.6 %coefficients.1.stencil = f32[49,16,128]{2,1,0:T(8,128)S(1)} custom-call(f32[10,25]{1,0:T(8,128)} %recon_hbm.3, f32[4,10,16,128]{3,2,1,0:T(8,128)S(1)} %get-tuple-element.28.weights, s32[4,16,128]{2,1,0:T(8,128)S(1)} %get-tuple-element.29.cells, s32[4,16,128]{2,1,0:T(8,128)S(1)} %get-tuple-element.30.codes), custom_call_target="tpu_custom_call" | custom-call | flops 8000000 | bytes 1048576 | tf_op jit(solution)/shard_map/coefficients/pallas_call | solution.py:656
  6.6 0.7 %pack_own.1 = (f32[64,128]{1,0:T(8,128)S(1)}, f32[64,128]{1,0:T(8,128)S(1)}, bf16[7,256,256]{2,1,0:T(8,128)(2,1)S(1)}, bf16[7,256,256]{2,1,0:T(8,128)(2,1)S(1)}) custom-call(f32[40,16,128]{2,1,0:T(8,128)S(1)} %get-tuple-element.27.mass, f32[49,16,128]{2,1,0:T(8,128)S(1)} %coefficients.1.stencil), custom_call_target="tpu_custom_call" | custom-call | flops 1000000 | bytes 1048576 | tf_op jit(solution)/shard_map/pack_own/pallas_call | solution.py:672
  7.3 1.1 %own_part.1 = (f32[40,8,128]{2,1,0:T(8,128)S(1)}, f32[49,16,128]{2,1,0:T(8,128)S(1)}, f32[49,16,128]{2,1,0:T(8,128)S(1)}, f32[49,16,128]{2,1,0:T(8,128)S(1)}) custom-call(f32[40,16,128]{2,1,0:T(8,128)S(1)} %get-tuple-element.27.mass, f32[49,16,128]{2,1,0:T(8,128)S(1)} %coefficients.1.stencil, bf16[7,256,256]{2,1,0:T(8,128)(2,1)S(1)} %get-tuple-element.33.near), custom_call_target="tpu_custom_call" | custom-call | flops 4000000 | bytes 1048576 | tf_op jit(solution)/shard_map/own_part/pallas_call | solution.py:682
  8.4 0.0 collective-permute-done.above
  8.5 0.0 collective-permute-done.1.below
  8.5 0.4 %pack_all.1 = (f32[112,128]{1,0:T(8,128)S(1)}, f32[112,128]{1,0:T(8,128)S(1)}) custom-call(f32[64,128]{1,0:T(8,128)S(1)} %get-tuple-element.37.own_left, f32[64,128]{1,0:T(8,128)S(1)} %get-tuple-element.38.own_right, f32[392,128]{1,0:T(8,128)S(1)} %collective-permute-done.above, f32[392,128]{1,0:T(8,128)S(1)} %collective-permute-done.1.below, ...), custom_call_target="tpu_custom_call" | custom-call | flops 1000000 | bytes 1048576 | tf_op jit(solution)/shard_map/pack_all/pallas_call | solution.py:693
  8.9 2.5 %collective-permute-start.3 = (f32[112,128]{1,0:T(8,128)S(1)}, f32[112,128]{1,0:T(8,128)S(1)}, u32[]{:S(2)}, u32[]{:S(2)}) collective-permute-start(f32[112,128]{1,0:T(8,128)S(1)} %get-tuple-element.39.send_a), channel_id=1, source_target_pairs={{0,1},{1,0},{2,3},{3,2},{4,5},{5,4},{6,7},{7,6},{8,9},{9,8},{10,11... | collective-permute-start | bytes 172040 | tf_op jit(solution)/shard_map/ppermute | solution.py:47
  11.4 1.6 %collective-permute-start.2 = (f32[112,128]{1,0:T(8,128)S(1)}, f32[112,128]{1,0:T(8,128)S(1)}, u32[]{:S(2)}, u32[]{:S(2)}) collective-permute-start(f32[112,128]{1,0:T(8,128)S(1)} %get-tuple-element.40.send_b), channel_id=1, source_target_pairs={{0,4},{1,2},{2,1},{3,7},{4,0},{5,6},{6,5},{7,3},{8,12},{9,10},{10,... | collective-permute-start | bytes 172040 | tf_op jit(solution)/shard_map/ppermute | solution.py:47
  13.0 3.0 %both_steps.1 = (f32[40,16,128]{2,1,0:T(8,128)S(1)}, f32[49,24,128]{2,1,0:T(8,128)S(1)}) custom-call(f32[40,16,128]{2,1,0:T(8,128)S(1)} %get-tuple-element.27.mass, f32[49,16,128]{2,1,0:T(8,128)S(1)} %coefficients.1.stencil, f32[392,128]{1,0:T(8,128)S(1)} %collective-permute-done.above, f32[392,128]{1,0:T(8,128)S(1)} %collective-permute-done.1.below, ...), custom_call_target="tpu_custom_call" | custom-call | flops 12000000 | bytes 1048576 | tf_op jit(solution)/shard_map/both_steps/pallas_call | solution.py:706
  15.9 0.0 collective-permute-done.3.got_a
  15.9 0.0 collective-permute-done.2.got_b
  15.9 0.6 %side_coefficients.1 = (f32[3,32,128]{2,1,0:T(8,128)S(1)}, f32[3,32,128]{2,1,0:T(8,128)S(1)}, f32[49,24,128]{2,1,0:T(8,128)S(1)}, f32[49,24,128]{2,1,0:T(8,128)S(1)}) custom-call(f32[49,24,128]{2,1,0:T(8,128)S(1)} %get-tuple-element.36.wide, f32[112,128]{1,0:T(8,128)S(1)} %get-tuple-element.39.send_a, f32[112,128]{1,0:T(8,128)S(1)} %get-tuple-element.40.send_b, ...), custom_call_target="tpu_custom_call" | custom-call | flops 4000000 | bytes 1048576 | tf_op jit(solution)/shard_map/side_coefficients/pallas_call | solution.py:717
  16.6 1.4 %halo_steps.1 = f32[40,16,128]{2,1,0:T(8,128)} custom-call(f32[3,32,128]{2,1,0:T(8,128)S(1)} %get-tuple-element.42.right_set, f32[3,32,128]{2,1,0:T(8,128)S(1)} %get-tuple-element.43.left_set, f32[49,24,128]{2,1,0:T(8,128)S(1)} %get-tuple-element.44.right_coef, f32[49,24,128]{2,1,0:T(8,128)S(1)} %get-tuple-element.45.left_coef, ...), custom_call_target="tpu_custom_call" | custom-call | flops 4000000 | bytes 1048576 | tf_op jit(solution)/shard_map/halo_steps/pallas_call | solution.py:728
Async XLA Ops:
  1.6 6.8 %collective-permute-start = (f32[392,128]{1,0:T(8,128)S(1)}, f32[392,128]{1,0:T(8,128)S(1)}, u32[]{:S(2)}, u32[]{:S(2)}) collective-permute-start(f32[392,128]{1,0:T(8,128)S(1)} %get-tuple-element.31), channel_id=1, source_target_pairs={{0,4},{4,8},{8,12},{12,16},{16,20},{20,24},{24,28},{28,0},{1,5},{5... | collective-permute-start | bytes 602120 | tf_op jit(solution)/shard_map/ppermute | solution.py:52
  2.1 6.3 %collective-permute-start.1 = (f32[392,128]{1,0:T(8,128)S(1)}, f32[392,128]{1,0:T(8,128)S(1)}, u32[]{:S(2)}, u32[]{:S(2)}) collective-permute-start(f32[392,128]{1,0:T(8,128)S(1)} %get-tuple-element.32), channel_id=1, source_target_pairs={{0,28},{4,0},{8,4},{12,8},{16,12},{20,16},{24,20},{28,24},{1,29},{... | collective-permute-start | bytes 602120 | tf_op jit(solution)/shard_map/ppermute | solution.py:52
  8.9 7.0 %collective-permute-start.3 = (f32[112,128]{1,0:T(8,128)S(1)}, f32[112,128]{1,0:T(8,128)S(1)}, u32[]{:S(2)}, u32[]{:S(2)}) collective-permute-start(f32[112,128]{1,0:T(8,128)S(1)} %get-tuple-element.39.send_a), channel_id=1, source_target_pairs={{0,1},{1,0},{2,3},{3,2},{4,5},{5,4},{6,7},{7,6},{8,9},{9,8},{10,11... | collective-permute-start | bytes 172040 | tf_op jit(solution)/shard_map/ppermute | solution.py:47
  11.4 4.6 %collective-permute-start.2 = (f32[112,128]{1,0:T(8,128)S(1)}, f32[112,128]{1,0:T(8,128)S(1)}, u32[]{:S(2)}, u32[]{:S(2)}) collective-permute-start(f32[112,128]{1,0:T(8,128)S(1)} %get-tuple-element.40.send_b), channel_id=1, source_target_pairs={{0,4},{1,2},{2,1},{3,7},{4,0},{5,6},{6,5},{7,3},{8,12},{9,10},{10,... | collective-permute-start | bytes 172040 | tf_op jit(solution)/shard_map/ppermute | solution.py:47

commit v8 on v7

--- a/solution.py
+++ b/solution.py
@@ -461,6 +461,10 @@
         for s, tile, value in sums:
             store(s, tile, value)
     return sums
+
+
+def take_first(got, after, out):
+    out[...] = got[...]
 
 
 def packed_sum(load, coef, coef_at, tile, tiles, dys):
@@ -714,6 +718,16 @@
         name="both_steps",
     )(mass, stencil, above, below, middle, own_shifted)
 
+    column_b = pl.pallas_call(
+        take_first,
+        out_shape=shape(*send),
+        in_specs=[VMEM, ANY],
+        out_specs=VMEM,
+        compiler_params=params(),
+        cost_estimate=cost(10**4),
+        name="take_first",
+    )(column_b, second)
+
     sides = pl.pallas_call(
         side_coefficients,
         out_shape=(shape(tiles, tall, 128),) * 2 + (shape(OFFSETS, low, 128),) * 2,

time: 18.1 us -> 19 us (1.050)
  the two profiles are of different devices: /device:TPU:0 before, /device:TPU:1 now
where the time goes in v8:
time: 19 us; the launch traced here: 18.8 us
  Pallas kernels  10.4 us (55%)
  starting transfers between devices  6.06 us (32%)
  waiting for transfers between devices  2.28 us (12%)
    ppermute x2, starting transfers between devices, column_swap(): return lax.ppermute(block, ROW_AXES + (COLUMN_AXES,), pairs)  3.38 us
    pallas_call x1, Pallas kernels, local(): pl.pallas_call(both_steps, out_shape=(shape(stacks, width, 128), shape(OF...  2.94 us
    ppermute x2, starting transfers between devices, shift(): lax.ppermute(block, axes, [(index, (index + step) % count) for index in r...  2.68 us
    ppermute x2, waiting for transfers between devices, shift(): lax.ppermute(block, axes, [(index, (index + step) % count) for index in r...  2.27 us
    pallas_call x1, Pallas kernels, local(): pl.pallas_call(edge_rows, out_shape=(whole(tracer_mass), whole(intersecti...  1.61 us
    pallas_call x1, Pallas kernels, local(): pl.pallas_call(coefficients, out_shape=shape(OFFSETS, width, 128), in_spe...  1.55 us
    pallas_call x1, Pallas kernels, local(): pl.pallas_call(halo_steps, out_shape=shape(stacks, width, columns), in_sp...  1.41 us
    pallas_call x1, Pallas kernels, local(): pl.pallas_call(own_part, out_shape=(shape(stacks, width - 8, 128),) + (sh...  1.11 us
  transfers between devices with their start and end apart: 4, of which 1 were waited for; matrix products, arithmetic and copies ran while one was open for 0% of the time, Pallas kernels for 33%

profile of v8, /device:TPU:1, one launch (start us, length us, event | category | flops | bytes accessed | tf_op | source)
XLA Modules:
  0.0 18.8 jit_solution(2151746521865416896)
XLA Ops:
  0.0 1.6 %edge_rows.1 = (f32[40,16,128]{2,1,0:T(8,128)S(1)}, f32[4,10,16,128]{3,2,1,0:T(8,128)S(1)}, s32[4,16,128]{2,1,0:T(8,128)S(1)}, s32[4,16,128]{2,1,0:T(8,128)S(1)}...) custom-call(f32[10,25]{1,0:T(8,128)} %recon_hbm.3, f32[40,16,128]{2,1,0:T(8,128)} %mass_hbm.1, ...), custom_call_target="tpu_custom_call" | custom-call | flops 4000000 | bytes 1048576 | tf_op jit(solution)/shard_map/edge_rows/pallas_call | solution.py:635
  1.6 2.7 %collective-permute-start = (f32[392,128]{1,0:T(8,128)S(1)}, f32[392,128]{1,0:T(8,128)S(1)}, u32[]{:S(2)}, u32[]{:S(2)}) collective-permute-start(f32[392,128]{1,0:T(8,128)S(1)} %get-tuple-element.31), channel_id=1, source_target_pairs={{0,4},{4,8},{8,12},{12,16},{16,20},{20,24},{24,28},{28,0},{1,5},{5... | collective-permute-start | bytes 602120 | tf_op jit(solution)/shard_map/ppermute | solution.py:52
  4.3 0.0 collective-permute-start.1
  4.3 1.6 %coefficients.1.stencil = f32[49,16,128]{2,1,0:T(8,128)S(1)} custom-call(f32[10,25]{1,0:T(8,128)} %recon_hbm.3, f32[4,10,16,128]{3,2,1,0:T(8,128)S(1)} %get-tuple-element.28.weights, s32[4,16,128]{2,1,0:T(8,128)S(1)} %get-tuple-element.29.cells, s32[4,16,128]{2,1,0:T(8,128)S(1)} %get-tuple-element.30.codes), custom_call_target="tpu_custom_call" | custom-call | flops 8000000 | bytes 1048576 | tf_op jit(solution)/shard_map/coefficients/pallas_call | solution.py:660
  5.9 0.7 %pack_own.1 = (f32[64,128]{1,0:T(8,128)S(1)}, f32[64,128]{1,0:T(8,128)S(1)}, bf16[7,256,256]{2,1,0:T(8,128)(2,1)S(1)}, bf16[7,256,256]{2,1,0:T(8,128)(2,1)S(1)}) custom-call(f32[40,16,128]{2,1,0:T(8,128)S(1)} %get-tuple-element.27.mass, f32[49,16,128]{2,1,0:T(8,128)S(1)} %coefficients.1.stencil), custom_call_target="tpu_custom_call" | custom-call | flops 1000000 | bytes 1048576 | tf_op jit(solution)/shard_map/pack_own/pallas_call | solution.py:676
  6.5 1.1 %own_part.1 = (f32[40,8,128]{2,1,0:T(8,128)S(1)}, f32[49,16,128]{2,1,0:T(8,128)S(1)}, f32[49,16,128]{2,1,0:T(8,128)S(1)}, f32[49,16,128]{2,1,0:T(8,128)S(1)}) custom-call(f32[40,16,128]{2,1,0:T(8,128)S(1)} %get-tuple-element.27.mass, f32[49,16,128]{2,1,0:T(8,128)S(1)} %coefficients.1.stencil, bf16[7,256,256]{2,1,0:T(8,128)(2,1)S(1)} %get-tuple-element.33.near), custom_call_target="tpu_custom_call" | custom-call | flops 4000000 | bytes 1048576 | tf_op jit(solution)/shard_map/own_part/pallas_call | solution.py:686
  7.6 0.0 collective-permute-done.above
  7.7 2.3 %collective-permute-done.1.below = f32[392,128]{1,0:T(8,128)S(1)} collective-permute-done((f32[392,128]{1,0:T(8,128)S(1)}, f32[392,128]{1,0:T(8,128)S(1)}, u32[]{:S(2)}, u32[]{:S(2)}) %collective-permute-start.1) | collective-permute-done | bytes 200736 | tf_op jit(solution)/shard_map/ppermute | solution.py:52
  9.9 0.4 %pack_all.1 = (f32[112,128]{1,0:T(8,128)S(1)}, f32[112,128]{1,0:T(8,128)S(1)}) custom-call(f32[64,128]{1,0:T(8,128)S(1)} %get-tuple-element.37.own_left, f32[64,128]{1,0:T(8,128)S(1)} %get-tuple-element.38.own_right, f32[392,128]{1,0:T(8,128)S(1)} %collective-permute-done.above, f32[392,128]{1,0:T(8,128)S(1)} %collective-permute-done.1.below, ...), custom_call_target="tpu_custom_call" | custom-call | flops 1000000 | bytes 1048576 | tf_op jit(solution)/shard_map/pack_all/pallas_call | solution.py:697
  10.4 0.0 collective-permute-start.2
  10.4 3.3 %collective-permute-start.3 = (f32[112,128]{1,0:T(8,128)S(1)}, f32[112,128]{1,0:T(8,128)S(1)}, u32[]{:S(2)}, u32[]{:S(2)}) collective-permute-start(f32[112,128]{1,0:T(8,128)S(1)} %get-tuple-element.39.send_a), channel_id=1, source_target_pairs={{0,1},{1,0},{2,3},{3,2},{4,5},{5,4},{6,7},{7,6},{8,9},{9,8},{10,11... | collective-permute-start | bytes 172040 | tf_op jit(solution)/shard_map/ppermute | solution.py:47
  13.8 2.9 %both_steps.1 = (f32[40,16,128]{2,1,0:T(8,128)S(1)}, f32[49,24,128]{2,1,0:T(8,128)S(1)}) custom-call(f32[40,16,128]{2,1,0:T(8,128)S(1)} %get-tuple-element.27.mass, f32[49,16,128]{2,1,0:T(8,128)S(1)} %coefficients.1.stencil, f32[392,128]{1,0:T(8,128)S(1)} %collective-permute-done.above, f32[392,128]{1,0:T(8,128)S(1)} %collective-permute-done.1.below, ...), custom_call_target="tpu_custom_call" | custom-call | flops 12000000 | bytes 1048576 | tf_op jit(solution)/shard_map/both_steps/pallas_call | solution.py:710
  16.7 0.0 collective-permute-done.2.got
  16.7 0.0 collective-permute-done.3.got_a
  16.7 0.6 %side_coefficients.1 = (f32[3,32,128]{2,1,0:T(8,128)S(1)}, f32[3,32,128]{2,1,0:T(8,128)S(1)}, f32[49,24,128]{2,1,0:T(8,128)S(1)}, f32[49,24,128]{2,1,0:T(8,128)S(1)}) custom-call(f32[49,24,128]{2,1,0:T(8,128)S(1)} %get-tuple-element.36.wide, f32[112,128]{1,0:T(8,128)S(1)} %get-tuple-element.39.send_a, f32[112,128]{1,0:T(8,128)S(1)} %get-tuple-element.40.send_b, ...), custom_call_target="tpu_custom_call" | custom-call | flops 4000000 | bytes 1048576 | tf_op jit(solution)/shard_map/side_coefficients/pallas_call | solution.py:731
  17.4 1.4 %halo_steps.1 = f32[40,16,128]{2,1,0:T(8,128)} custom-call(f32[3,32,128]{2,1,0:T(8,128)S(1)} %get-tuple-element.43.right_set, f32[3,32,128]{2,1,0:T(8,128)S(1)} %get-tuple-element.44.left_set, f32[49,24,128]{2,1,0:T(8,128)S(1)} %get-tuple-element.45.right_coef, f32[49,24,128]{2,1,0:T(8,128)S(1)} %get-tuple-element.46.left_coef, ...), custom_call_target="tpu_custom_call" | custom-call | flops 4000000 | bytes 1048576 | tf_op jit(solution)/shard_map/halo_steps/pallas_call | solution.py:742
  (1 shorter events, 0.0 us)
Async XLA Ops:
  1.6 6.0 %collective-permute-start = (f32[392,128]{1,0:T(8,128)S(1)}, f32[392,128]{1,0:T(8,128)S(1)}, u32[]{:S(2)}, u32[]{:S(2)}) collective-permute-start(f32[392,128]{1,0:T(8,128)S(1)} %get-tuple-element.31), channel_id=1, source_target_pairs={{0,4},{4,8},{8,12},{12,16},{16,20},{20,24},{24,28},{28,0},{1,5},{5... | collective-permute-start | bytes 602120 | tf_op jit(solution)/shard_map/ppermute | solution.py:52
  4.3 5.6 %collective-permute-start.1 = (f32[392,128]{1,0:T(8,128)S(1)}, f32[392,128]{1,0:T(8,128)S(1)}, u32[]{:S(2)}, u32[]{:S(2)}) collective-permute-start(f32[392,128]{1,0:T(8,128)S(1)} %get-tuple-element.32), channel_id=1, source_target_pairs={{0,28},{4,0},{8,4},{12,8},{16,12},{20,16},{24,20},{28,24},{1,29},{... | collective-permute-start | bytes 602120 | tf_op jit(solution)/shard_map/ppermute | solution.py:52
  10.4 6.3 %collective-permute-start.2 = (f32[112,128]{1,0:T(8,128)S(1)}, f32[112,128]{1,0:T(8,128)S(1)}, u32[]{:S(2)}, u32[]{:S(2)}) collective-permute-start(f32[112,128]{1,0:T(8,128)S(1)} %get-tuple-element.40.send_b), channel_id=1, source_target_pairs={{0,4},{1,2},{2,1},{3,7},{4,0},{5,6},{6,5},{7,3},{8,12},{9,10},{10,... | collective-permute-start | bytes 172040 | tf_op jit(solution)/shard_map/ppermute | solution.py:47
  10.4 6.3 %collective-permute-start.3 = (f32[112,128]{1,0:T(8,128)S(1)}, f32[112,128]{1,0:T(8,128)S(1)}, u32[]{:S(2)}, u32[]{:S(2)}) collective-permute-start(f32[112,128]{1,0:T(8,128)S(1)} %get-tuple-element.39.send_a), channel_id=1, source_target_pairs={{0,1},{1,0},{2,3},{3,2},{4,5},{5,4},{6,7},{7,6},{8,9},{9,8},{10,11... | collective-permute-start | bytes 172040 | tf_op jit(solution)/shard_map/ppermute | solution.py:47

commit v9 on v7

--- a/solution.py
+++ b/solution.py
@@ -47,9 +47,19 @@
     return lax.ppermute(block, ROW_AXES + (COLUMN_AXES,), pairs)
 
 
-def shift(block, axes, step):
-    count = lax.axis_size(axes)
-    return lax.ppermute(block, axes, [(index, (index + step) % count) for index in range(count)])
+def row_swap(block, odd_first):
+    chains, count = lax.axis_size(ROW_AXES), lax.axis_size(COLUMN_AXES)
+    chain_of = list(range(chains))
+    for low in range(1 if odd_first else 0, chains - 1, 2):
+        chain_of[low], chain_of[low + 1] = low + 1, low
+    pairs = []
+    for chain in range(chains):
+        for place in range(count):
+            target = (chain_of[chain], place)
+            if chain_of[chain] == chain and count % 2 == 0:
+                target = (chain, place ^ 1)
+            pairs.append((chain * count + place, target[0] * count + target[1]))
+    return lax.ppermute(block, ROW_AXES + (COLUMN_AXES,), pairs)
 
 
 def ends(axes):
@@ -146,7 +156,7 @@
 
 def edge_rows(
     recon_hbm, mass_hbm, weights_hbm, cells_hbm, codes_hbm,
-    mass, weights, cells, codes, send_down, send_up,
+    mass, weights, cells, codes, send_a, send_b,
     recon, edge_weights, edge_cells, edge_codes, edge_stencil, turned, spread, sems,
 ):
     sources = (recon_hbm, codes_hbm, weights_hbm, cells_hbm, mass_hbm)
@@ -165,12 +175,15 @@
         recon, edge_weights, edge_cells, edge_codes, turned, spread, edge_stencil, 1, copies[0].wait
     )
     copies[4].wait()
-    for send, mass_at, stencil_at in ((send_down, width - 6, 5), (send_up, 0, 0)):
+    even = is_even(ROW_AXES)
+    for send, low_edge in ((send_a, jnp.logical_not(even)), (send_b, even)):
+        mass_at = jnp.where(low_edge, 0, width - 6)
+        stencil_at = jnp.where(low_edge, 0, 5)
         for s in range(stacks):
-            send[6 * s : 6 * s + 6, :] = mass[s, mass_at : mass_at + 6, :]
+            send[6 * s : 6 * s + 6, :] = mass[s, pl.ds(mass_at, 6), :]
         for o in range(OFFSETS):
             at = 6 * stacks + 3 * o
-            send[at : at + 3, :] = edge_stencil[o, stencil_at : stencil_at + 3, :]
+            send[at : at + 3, :] = edge_stencil[o, pl.ds(stencil_at, 3), :]
 
 
 def coefficients(recon_hbm, weights, cells, codes, stencil, recon, turned, spread, sem):
@@ -461,6 +474,14 @@
         for s, tile, value in sums:
             store(s, tile, value)
     return sums
+
+
+def take_first(got, after, out):
+    out[...] = got[...]
+
+
+def in_order(got_a, got_b, above, below):
+    choose(is_even(ROW_AXES), got_b, got_a, above, below)
 
 
 def packed_sum(load, coef, coef_at, tile, tiles, dys):
@@ -628,7 +649,7 @@
     picks = jax.ShapeDtypeStruct((7, 256, 256), jnp.bfloat16)
     regions = intersection_cells.shape[0]
 
-    mass, weights, cells, codes, send_down, send_up = pl.pallas_call(
+    mass, weights, cells, codes, send_a, send_b = pl.pallas_call(
         edge_rows,
         out_shape=(
             whole(tracer_mass), whole(intersection_weights), whole(intersection_cells),
@@ -650,8 +671,8 @@
         cost_estimate=cost(4 * 10**6),
         name="edge_rows",
     )(*fixed(recon_table, tracer_mass, intersection_weights, intersection_cells, rotation_codes))
-    above = shift(send_down, ROW_AXES, 1)
-    below = shift(send_up, ROW_AXES, -1)
+    got_b = row_swap(send_b, True)
+    got_a = row_swap(send_a, False)
 
     stencil = pl.pallas_call(
         coefficients,
@@ -689,6 +710,25 @@
         name="own_part",
     )(mass, stencil, near)
 
+    got_b = pl.pallas_call(
+        take_first,
+        out_shape=shape(edge, 128),
+        in_specs=[VMEM, ANY],
+        out_specs=VMEM,
+        compiler_params=params(),
+        cost_estimate=cost(10**4),
+        name="take_first",
+    )(got_b, middle)
+    above, below = pl.pallas_call(
+        in_order,
+        out_shape=(shape(edge, 128),) * 2,
+        in_specs=[VMEM] * 2,
+        out_specs=(VMEM,) * 2,
+        compiler_params=params(),
+        cost_estimate=cost(10**4),
+        name="in_order",
+    )(got_a, got_b)
+
     send = ((width + 12) * (tiles + 1), 128)
     send_a, send_b = pl.pallas_call(
         functools.partial(pack_all, stacks),

time: 18.1 us -> 18 us (level)
  the two profiles are of different devices: /device:TPU:0 before, /device:TPU:12 now
where the time goes in v9:
time: 18 us; the launch traced here: 17.8 us
  Pallas kernels  10.5 us (58%)
  starting transfers between devices  4.82 us (27%)
  waiting for transfers between devices  2.41 us (13%)
    ppermute x2, starting transfers between devices, column_swap(): return lax.ppermute(block, ROW_AXES + (COLUMN_AXES,), pairs)  3.22 us
    pallas_call x1, Pallas kernels, local(): pl.pallas_call(both_steps, out_shape=(shape(stacks, width, 128), shape(OF...  2.94 us
    ppermute x2, waiting for transfers between devices, row_swap(): return lax.ppermute(block, ROW_AXES + (COLUMN_AXES,), pairs)  2.4 us
    pallas_call x1, Pallas kernels, local(): pl.pallas_call(edge_rows, out_shape=(whole(tracer_mass), whole(intersecti...  1.63 us
    ppermute x2, starting transfers between devices, row_swap(): return lax.ppermute(block, ROW_AXES + (COLUMN_AXES,), pairs)  1.61 us
    pallas_call x1, Pallas kernels, local(): pl.pallas_call(coefficients, out_shape=shape(OFFSETS, width, 128), in_spe...  1.55 us
    pallas_call x1, Pallas kernels, local(): pl.pallas_call(halo_steps, out_shape=shape(stacks, width, columns), in_sp...  1.42 us
    pallas_call x1, Pallas kernels, local(): pl.pallas_call(own_part, out_shape=(shape(stacks, width - 8, 128),) + (sh...  1.12 us
  transfers between devices with their start and end apart: 4, of which 1 were waited for; matrix products, arithmetic and copies ran while one was open for 0% of the time, Pallas kernels for 35%

profile of v9, /device:TPU:12, one launch (start us, length us, event | category | flops | bytes accessed | tf_op | source)
XLA Modules:
  0.0 17.8 jit_solution(5721553564849249429)
XLA Ops:
  0.0 1.6 %edge_rows.1 = (f32[40,16,128]{2,1,0:T(8,128)S(1)}, f32[4,10,16,128]{3,2,1,0:T(8,128)S(1)}, s32[4,16,128]{2,1,0:T(8,128)S(1)}, s32[4,16,128]{2,1,0:T(8,128)S(1)}...) custom-call(f32[10,25]{1,0:T(8,128)} %recon_hbm.3, f32[40,16,128]{2,1,0:T(8,128)} %mass_hbm.1, ...), custom_call_target="tpu_custom_call" | custom-call | flops 4000000 | bytes 1048576 | tf_op jit(solution)/shard_map/edge_rows/pallas_call | solution.py:652
  1.6 0.1 collective-permute-start.1
  1.7 1.5 %collective-permute-start = (f32[392,128]{1,0:T(8,128)S(1)}, f32[392,128]{1,0:T(8,128)S(1)}, u32[]{:S(2)}, u32[]{:S(2)}) collective-permute-start(f32[392,128]{1,0:T(8,128)S(1)} %get-tuple-element.33), channel_id=1, source_target_pairs={{0,4},{1,5},{2,6},{3,7},{4,0},{5,1},{6,2},{7,3},{8,12},{9,13},{10,... | collective-permute-start | bytes 602120 | tf_op jit(solution)/shard_map/ppermute | solution.py:62
  3.3 1.6 %coefficients.1.stencil = f32[49,16,128]{2,1,0:T(8,128)S(1)} custom-call(f32[10,25]{1,0:T(8,128)} %recon_hbm.3, f32[4,10,16,128]{3,2,1,0:T(8,128)S(1)} %get-tuple-element.30.weights, s32[4,16,128]{2,1,0:T(8,128)S(1)} %get-tuple-element.31.cells, s32[4,16,128]{2,1,0:T(8,128)S(1)} %get-tuple-element.32.codes), custom_call_target="tpu_custom_call" | custom-call | flops 8000000 | bytes 1048576 | tf_op jit(solution)/shard_map/coefficients/pallas_call | solution.py:677
  4.8 0.7 %pack_own.1 = (f32[64,128]{1,0:T(8,128)S(1)}, f32[64,128]{1,0:T(8,128)S(1)}, bf16[7,256,256]{2,1,0:T(8,128)(2,1)S(1)}, bf16[7,256,256]{2,1,0:T(8,128)(2,1)S(1)}) custom-call(f32[40,16,128]{2,1,0:T(8,128)S(1)} %get-tuple-element.29.mass, f32[49,16,128]{2,1,0:T(8,128)S(1)} %coefficients.1.stencil), custom_call_target="tpu_custom_call" | custom-call | flops 1000000 | bytes 1048576 | tf_op jit(solution)/shard_map/pack_own/pallas_call | solution.py:693
  5.5 1.1 %own_part.1 = (f32[40,8,128]{2,1,0:T(8,128)S(1)}, f32[49,16,128]{2,1,0:T(8,128)S(1)}, f32[49,16,128]{2,1,0:T(8,128)S(1)}, f32[49,16,128]{2,1,0:T(8,128)S(1)}) custom-call(f32[40,16,128]{2,1,0:T(8,128)S(1)} %get-tuple-element.29.mass, f32[49,16,128]{2,1,0:T(8,128)S(1)} %coefficients.1.stencil, bf16[7,256,256]{2,1,0:T(8,128)(2,1)S(1)} %get-tuple-element.35.near), custom_call_target="tpu_custom_call" | custom-call | flops 4000000 | bytes 1048576 | tf_op jit(solution)/shard_map/own_part/pallas_call | solution.py:703
  6.6 2.4 %collective-permute-done.1.got = f32[392,128]{1,0:T(8,128)S(1)} collective-permute-done((f32[392,128]{1,0:T(8,128)S(1)}, f32[392,128]{1,0:T(8,128)S(1)}, u32[]{:S(2)}, u32[]{:S(2)}) %collective-permute-start.1) | collective-permute-done | bytes 200736 | tf_op jit(solution)/shard_map/ppermute | solution.py:62
  9.0 0.0 collective-permute-done.got_a
  9.1 0.5 %pack_all.1 = (f32[112,128]{1,0:T(8,128)S(1)}, f32[112,128]{1,0:T(8,128)S(1)}) custom-call(f32[64,128]{1,0:T(8,128)S(1)} %get-tuple-element.41.own_left, f32[64,128]{1,0:T(8,128)S(1)} %get-tuple-element.42.own_right, f32[392,128]{1,0:T(8,128)S(1)} %get-tuple-element.37.above, f32[392,128]{1,0:T(8,128)S(1)} %get-tuple-element.38.below, ...), custom_call_target="tpu_custom_call" | custom-call | flops 1000000 | bytes 1048576 | tf_op jit(solution)/shard_map/pack_all/pallas_call | solution.py:733
  9.5 0.5 %collective-permute-start.3 = (f32[112,128]{1,0:T(8,128)S(1)}, f32[112,128]{1,0:T(8,128)S(1)}, u32[]{:S(2)}, u32[]{:S(2)}) collective-permute-start(f32[112,128]{1,0:T(8,128)S(1)} %get-tuple-element.43.send_a), channel_id=1, source_target_pairs={{0,1},{1,0},{2,3},{3,2},{4,5},{5,4},{6,7},{7,6},{8,9},{9,8},{10,11... | collective-permute-start | bytes 172040 | tf_op jit(solution)/shard_map/ppermute | solution.py:47
  10.0 2.7 %collective-permute-start.2 = (f32[112,128]{1,0:T(8,128)S(1)}, f32[112,128]{1,0:T(8,128)S(1)}, u32[]{:S(2)}, u32[]{:S(2)}) collective-permute-start(f32[112,128]{1,0:T(8,128)S(1)} %get-tuple-element.44.send_b), channel_id=1, source_target_pairs={{0,4},{1,2},{2,1},{3,7},{4,0},{5,6},{6,5},{7,3},{8,12},{9,10},{10,... | collective-permute-start | bytes 172040 | tf_op jit(solution)/shard_map/ppermute | solution.py:47
  12.8 2.9 %both_steps.1 = (f32[40,16,128]{2,1,0:T(8,128)S(1)}, f32[49,24,128]{2,1,0:T(8,128)S(1)}) custom-call(f32[40,16,128]{2,1,0:T(8,128)S(1)} %get-tuple-element.29.mass, f32[49,16,128]{2,1,0:T(8,128)S(1)} %coefficients.1.stencil, f32[392,128]{1,0:T(8,128)S(1)} %get-tuple-element.37.above, f32[392,128]{1,0:T(8,128)S(1)} %get-tuple-element.38.below, ...), custom_call_target="tpu_custom_call" | custom-call | flops 12000000 | bytes 1048576 | tf_op jit(solution)/shard_map/both_steps/pallas_call | solution.py:746
  15.7 0.0 collective-permute-done.3.got_a
  15.7 0.0 collective-permute-done.2.got_b
  15.7 0.6 %side_coefficients.1 = (f32[3,32,128]{2,1,0:T(8,128)S(1)}, f32[3,32,128]{2,1,0:T(8,128)S(1)}, f32[49,24,128]{2,1,0:T(8,128)S(1)}, f32[49,24,128]{2,1,0:T(8,128)S(1)}) custom-call(f32[49,24,128]{2,1,0:T(8,128)S(1)} %get-tuple-element.40.wide, f32[112,128]{1,0:T(8,128)S(1)} %get-tuple-element.43.send_a, f32[112,128]{1,0:T(8,128)S(1)} %get-tuple-element.44.send_b, ...), custom_call_target="tpu_custom_call" | custom-call | flops 4000000 | bytes 1048576 | tf_op jit(solution)/shard_map/side_coefficients/pallas_call | solution.py:757
  16.3 1.4 %halo_steps.1 = f32[40,16,128]{2,1,0:T(8,128)} custom-call(f32[3,32,128]{2,1,0:T(8,128)S(1)} %get-tuple-element.46.right_set, f32[3,32,128]{2,1,0:T(8,128)S(1)} %get-tuple-element.47.left_set, f32[49,24,128]{2,1,0:T(8,128)S(1)} %get-tuple-element.48.right_coef, f32[49,24,128]{2,1,0:T(8,128)S(1)} %get-tuple-element.49.left_coef, ...), custom_call_target="tpu_custom_call" | custom-call | flops 4000000 | bytes 1048576 | tf_op jit(solution)/shard_map/halo_steps/pallas_call | solution.py:768
  (2 shorter events, 0.1 us)
Async XLA Ops:
  1.6 7.4 %collective-permute-start.1 = (f32[392,128]{1,0:T(8,128)S(1)}, f32[392,128]{1,0:T(8,128)S(1)}, u32[]{:S(2)}, u32[]{:S(2)}) collective-permute-start(f32[392,128]{1,0:T(8,128)S(1)} %get-tuple-element.34), channel_id=1, source_target_pairs={{0,1},{1,0},{2,3},{3,2},{4,8},{5,9},{6,10},{7,11},{8,4},{9,5},{10,... | collective-permute-start | bytes 602120 | tf_op jit(solution)/shard_map/ppermute | solution.py:62
  1.7 7.3 %collective-permute-start = (f32[392,128]{1,0:T(8,128)S(1)}, f32[392,128]{1,0:T(8,128)S(1)}, u32[]{:S(2)}, u32[]{:S(2)}) collective-permute-start(f32[392,128]{1,0:T(8,128)S(1)} %get-tuple-element.33), channel_id=1, source_target_pairs={{0,4},{1,5},{2,6},{3,7},{4,0},{5,1},{6,2},{7,3},{8,12},{9,13},{10,... | collective-permute-start | bytes 602120 | tf_op jit(solution)/shard_map/ppermute | solution.py:62
  9.5 6.2 %collective-permute-start.3 = (f32[112,128]{1,0:T(8,128)S(1)}, f32[112,128]{1,0:T(8,128)S(1)}, u32[]{:S(2)}, u32[]{:S(2)}) collective-permute-start(f32[112,128]{1,0:T(8,128)S(1)} %get-tuple-element.43.send_a), channel_id=1, source_target_pairs={{0,1},{1,0},{2,3},{3,2},{4,5},{5,4},{6,7},{7,6},{8,9},{9,8},{10,11... | collective-permute-start | bytes 172040 | tf_op jit(solution)/shard_map/ppermute | solution.py:47
  10.0 5.7 %collective-permute-start.2 = (f32[112,128]{1,0:T(8,128)S(1)}, f32[112,128]{1,0:T(8,128)S(1)}, u32[]{:S(2)}, u32[]{:S(2)}) collective-permute-start(f32[112,128]{1,0:T(8,128)S(1)} %get-tuple-element.44.send_b), channel_id=1, source_target_pairs={{0,4},{1,2},{2,1},{3,7},{4,0},{5,6},{6,5},{7,3},{8,12},{9,10},{10,... | collective-permute-start | bytes 172040 | tf_op jit(solution)/shard_map/ppermute | solution.py:47

commit v10 on v9

--- a/solution.py
+++ b/solution.py
@@ -456,7 +456,7 @@
 
 
 def per_turn(stacks):
-    return next(GROUP * groups for groups in (5, 2, 1) if stacks % (GROUP * groups) == 0)
+    return next(GROUP * groups for groups in (10, 5, 2, 1) if stacks % (GROUP * groups) == 0)
 
 
 def turns(stacks):

time: 18 us -> 17.6 us (0.978)
  Pallas kernels: 10.5 us -> 9.83 us
  waiting for transfers between devices: 2.41 us -> 2.65 us
    pallas_call x1, Pallas kernels: 2.94 us -> 2.56 us  [local(): pl.pallas_call(both_steps, out_shape=(shape(stacks, width, 128), shape(OF...]
    ppermute x2, waiting for transfers between devices: 2.4 us -> 2.64 us  [row_swap(): return lax.ppermute(block, ROW_AXES + (COLUMN_AXES,), pairs)]
    pallas_call x1, Pallas kernels: 1.12 us -> 0.88 us  [local(): pl.pallas_call(own_part, out_shape=(shape(stacks, width - 8, 128),) + (sh...]
  transfers between devices with their start and end apart: 4 -> 4, of which waited for: 1 -> 1; matrix products, arithmetic and copies ran while one was open for 0% -> 0% of each run, Pallas kernels for 35% -> 33%
where the time goes in v10:
time: 17.6 us; the launch traced here: 17.4 us
  Pallas kernels  9.83 us (56%)
  starting transfers between devices  4.82 us (27%)
  waiting for transfers between devices  2.65 us (15%)
    ppermute x2, starting transfers between devices, column_swap(): return lax.ppermute(block, ROW_AXES + (COLUMN_AXES,), pairs)  3.22 us
    ppermute x2, waiting for transfers between devices, row_swap(): return lax.ppermute(block, ROW_AXES + (COLUMN_AXES,), pairs)  2.64 us
    pallas_call x1, Pallas kernels, local(): pl.pallas_call(both_steps, out_shape=(shape(stacks, width, 128), shape(OF...  2.56 us
    pallas_call x1, Pallas kernels, local(): pl.pallas_call(edge_rows, out_shape=(whole(tracer_mass), whole(intersecti...  1.63 us
    ppermute x2, starting transfers between devices, row_swap(): return lax.ppermute(block, ROW_AXES + (COLUMN_AXES,), pairs)  1.61 us
    pallas_call x1, Pallas kernels, local(): pl.pallas_call(coefficients, out_shape=shape(OFFSETS, width, 128), in_spe...  1.55 us
    pallas_call x1, Pallas kernels, local(): pl.pallas_call(halo_steps, out_shape=shape(stacks, width, columns), in_sp...  1.42 us
    pallas_call x1, Pallas kernels, local(): pl.pallas_call(own_part, out_shape=(shape(stacks, width - 8, 128),) + (sh...  0.88 us
  transfers between devices with their start and end apart: 4, of which 1 were waited for; matrix products, arithmetic and copies ran while one was open for 0% of the time, Pallas kernels for 33%

profile of v10, /device:TPU:12, one launch (start us, length us, event | category | flops | bytes accessed | tf_op | source)
XLA Modules:
  0.0 17.4 jit_solution(13206778872989452728)
XLA Ops:
  0.0 1.6 %edge_rows.1 = (f32[40,16,128]{2,1,0:T(8,128)S(1)}, f32[4,10,16,128]{3,2,1,0:T(8,128)S(1)}, s32[4,16,128]{2,1,0:T(8,128)S(1)}, s32[4,16,128]{2,1,0:T(8,128)S(1)}...) custom-call(f32[10,25]{1,0:T(8,128)} %recon_hbm.3, f32[40,16,128]{2,1,0:T(8,128)} %mass_hbm.1, ...), custom_call_target="tpu_custom_call" | custom-call | flops 4000000 | bytes 1048576 | tf_op jit(solution)/shard_map/edge_rows/pallas_call | solution.py:652
  1.6 0.1 collective-permute-start.1
  1.7 1.5 %collective-permute-start = (f32[392,128]{1,0:T(8,128)S(1)}, f32[392,128]{1,0:T(8,128)S(1)}, u32[]{:S(2)}, u32[]{:S(2)}) collective-permute-start(f32[392,128]{1,0:T(8,128)S(1)} %get-tuple-element.33), channel_id=1, source_target_pairs={{0,4},{1,5},{2,6},{3,7},{4,0},{5,1},{6,2},{7,3},{8,12},{9,13},{10,... | collective-permute-start | bytes 602120 | tf_op jit(solution)/shard_map/ppermute | solution.py:62
  3.3 1.6 %coefficients.1.stencil = f32[49,16,128]{2,1,0:T(8,128)S(1)} custom-call(f32[10,25]{1,0:T(8,128)} %recon_hbm.3, f32[4,10,16,128]{3,2,1,0:T(8,128)S(1)} %get-tuple-element.30.weights, s32[4,16,128]{2,1,0:T(8,128)S(1)} %get-tuple-element.31.cells, s32[4,16,128]{2,1,0:T(8,128)S(1)} %get-tuple-element.32.codes), custom_call_target="tpu_custom_call" | custom-call | flops 8000000 | bytes 1048576 | tf_op jit(solution)/shard_map/coefficients/pallas_call | solution.py:677
  4.8 0.7 %pack_own.1 = (f32[64,128]{1,0:T(8,128)S(1)}, f32[64,128]{1,0:T(8,128)S(1)}, bf16[7,256,256]{2,1,0:T(8,128)(2,1)S(1)}, bf16[7,256,256]{2,1,0:T(8,128)(2,1)S(1)}) custom-call(f32[40,16,128]{2,1,0:T(8,128)S(1)} %get-tuple-element.29.mass, f32[49,16,128]{2,1,0:T(8,128)S(1)} %coefficients.1.stencil), custom_call_target="tpu_custom_call" | custom-call | flops 1000000 | bytes 1048576 | tf_op jit(solution)/shard_map/pack_own/pallas_call | solution.py:693
  5.5 0.9 %own_part.1 = (f32[40,8,128]{2,1,0:T(8,128)S(1)}, f32[49,16,128]{2,1,0:T(8,128)S(1)}, f32[49,16,128]{2,1,0:T(8,128)S(1)}, f32[49,16,128]{2,1,0:T(8,128)S(1)}) custom-call(f32[40,16,128]{2,1,0:T(8,128)S(1)} %get-tuple-element.29.mass, f32[49,16,128]{2,1,0:T(8,128)S(1)} %coefficients.1.stencil, bf16[7,256,256]{2,1,0:T(8,128)(2,1)S(1)} %get-tuple-element.35.near), custom_call_target="tpu_custom_call" | custom-call | flops 4000000 | bytes 1048576 | tf_op jit(solution)/shard_map/own_part/pallas_call | solution.py:703
  6.3 2.6 %collective-permute-done.1.got = f32[392,128]{1,0:T(8,128)S(1)} collective-permute-done((f32[392,128]{1,0:T(8,128)S(1)}, f32[392,128]{1,0:T(8,128)S(1)}, u32[]{:S(2)}, u32[]{:S(2)}) %collective-permute-start.1) | collective-permute-done | bytes 200736 | tf_op jit(solution)/shard_map/ppermute | solution.py:62
  9.0 0.0 collective-permute-done.got_a
  9.1 0.5 %pack_all.1 = (f32[112,128]{1,0:T(8,128)S(1)}, f32[112,128]{1,0:T(8,128)S(1)}) custom-call(f32[64,128]{1,0:T(8,128)S(1)} %get-tuple-element.41.own_left, f32[64,128]{1,0:T(8,128)S(1)} %get-tuple-element.42.own_right, f32[392,128]{1,0:T(8,128)S(1)} %get-tuple-element.37.above, f32[392,128]{1,0:T(8,128)S(1)} %get-tuple-element.38.below, ...), custom_call_target="tpu_custom_call" | custom-call | flops 1000000 | bytes 1048576 | tf_op jit(solution)/shard_map/pack_all/pallas_call | solution.py:733
  9.5 0.5 %collective-permute-start.3 = (f32[112,128]{1,0:T(8,128)S(1)}, f32[112,128]{1,0:T(8,128)S(1)}, u32[]{:S(2)}, u32[]{:S(2)}) collective-permute-start(f32[112,128]{1,0:T(8,128)S(1)} %get-tuple-element.43.send_a), channel_id=1, source_target_pairs={{0,1},{1,0},{2,3},{3,2},{4,5},{5,4},{6,7},{7,6},{8,9},{9,8},{10,11... | collective-permute-start | bytes 172040 | tf_op jit(solution)/shard_map/ppermute | solution.py:47
  10.0 2.7 %collective-permute-start.2 = (f32[112,128]{1,0:T(8,128)S(1)}, f32[112,128]{1,0:T(8,128)S(1)}, u32[]{:S(2)}, u32[]{:S(2)}) collective-permute-start(f32[112,128]{1,0:T(8,128)S(1)} %get-tuple-element.44.send_b), channel_id=1, source_target_pairs={{0,4},{1,2},{2,1},{3,7},{4,0},{5,6},{6,5},{7,3},{8,12},{9,10},{10,... | collective-permute-start | bytes 172040 | tf_op jit(solution)/shard_map/ppermute | solution.py:47
  12.8 2.6 %both_steps.1 = (f32[40,16,128]{2,1,0:T(8,128)S(1)}, f32[49,24,128]{2,1,0:T(8,128)S(1)}) custom-call(f32[40,16,128]{2,1,0:T(8,128)S(1)} %get-tuple-element.29.mass, f32[49,16,128]{2,1,0:T(8,128)S(1)} %coefficients.1.stencil, f32[392,128]{1,0:T(8,128)S(1)} %get-tuple-element.37.above, f32[392,128]{1,0:T(8,128)S(1)} %get-tuple-element.38.below, ...), custom_call_target="tpu_custom_call" | custom-call | flops 12000000 | bytes 1048576 | tf_op jit(solution)/shard_map/both_steps/pallas_call | solution.py:746
  15.3 0.0 collective-permute-done.3.got_a
  15.3 0.0 collective-permute-done.2.got_b
  15.3 0.6 %side_coefficients.1 = (f32[3,32,128]{2,1,0:T(8,128)S(1)}, f32[3,32,128]{2,1,0:T(8,128)S(1)}, f32[49,24,128]{2,1,0:T(8,128)S(1)}, f32[49,24,128]{2,1,0:T(8,128)S(1)}) custom-call(f32[49,24,128]{2,1,0:T(8,128)S(1)} %get-tuple-element.40.wide, f32[112,128]{1,0:T(8,128)S(1)} %get-tuple-element.43.send_a, f32[112,128]{1,0:T(8,128)S(1)} %get-tuple-element.44.send_b, ...), custom_call_target="tpu_custom_call" | custom-call | flops 4000000 | bytes 1048576 | tf_op jit(solution)/shard_map/side_coefficients/pallas_call | solution.py:757
  16.0 1.4 %halo_steps.1 = f32[40,16,128]{2,1,0:T(8,128)} custom-call(f32[3,32,128]{2,1,0:T(8,128)S(1)} %get-tuple-element.46.right_set, f32[3,32,128]{2,1,0:T(8,128)S(1)} %get-tuple-element.47.left_set, f32[49,24,128]{2,1,0:T(8,128)S(1)} %get-tuple-element.48.right_coef, f32[49,24,128]{2,1,0:T(8,128)S(1)} %get-tuple-element.49.left_coef, ...), custom_call_target="tpu_custom_call" | custom-call | flops 4000000 | bytes 1048576 | tf_op jit(solution)/shard_map/halo_steps/pallas_call | solution.py:768
  (2 shorter events, 0.1 us)
Async XLA Ops:
  1.6 7.4 %collective-permute-start.1 = (f32[392,128]{1,0:T(8,128)S(1)}, f32[392,128]{1,0:T(8,128)S(1)}, u32[]{:S(2)}, u32[]{:S(2)}) collective-permute-start(f32[392,128]{1,0:T(8,128)S(1)} %get-tuple-element.34), channel_id=1, source_target_pairs={{0,1},{1,0},{2,3},{3,2},{4,8},{5,9},{6,10},{7,11},{8,4},{9,5},{10,... | collective-permute-start | bytes 602120 | tf_op jit(solution)/shard_map/ppermute | solution.py:62
  1.7 7.3 %collective-permute-start = (f32[392,128]{1,0:T(8,128)S(1)}, f32[392,128]{1,0:T(8,128)S(1)}, u32[]{:S(2)}, u32[]{:S(2)}) collective-permute-start(f32[392,128]{1,0:T(8,128)S(1)} %get-tuple-element.33), channel_id=1, source_target_pairs={{0,4},{1,5},{2,6},{3,7},{4,0},{5,1},{6,2},{7,3},{8,12},{9,13},{10,... | collective-permute-start | bytes 602120 | tf_op jit(solution)/shard_map/ppermute | solution.py:62
  9.5 5.8 %collective-permute-start.3 = (f32[112,128]{1,0:T(8,128)S(1)}, f32[112,128]{1,0:T(8,128)S(1)}, u32[]{:S(2)}, u32[]{:S(2)}) collective-permute-start(f32[112,128]{1,0:T(8,128)S(1)} %get-tuple-element.43.send_a), channel_id=1, source_target_pairs={{0,1},{1,0},{2,3},{3,2},{4,5},{5,4},{6,7},{7,6},{8,9},{9,8},{10,11... | collective-permute-start | bytes 172040 | tf_op jit(solution)/shard_map/ppermute | solution.py:47
  10.0 5.3 %collective-permute-start.2 = (f32[112,128]{1,0:T(8,128)S(1)}, f32[112,128]{1,0:T(8,128)S(1)}, u32[]{:S(2)}, u32[]{:S(2)}) collective-permute-start(f32[112,128]{1,0:T(8,128)S(1)} %get-tuple-element.44.send_b), channel_id=1, source_target_pairs={{0,4},{1,2},{2,1},{3,7},{4,0},{5,6},{6,5},{7,3},{8,12},{9,10},{10,... | collective-permute-start | bytes 172040 | tf_op jit(solution)/shard_map/ppermute | solution.py:47

commit v11 on v10

--- a/solution.py
+++ b/solution.py
@@ -120,7 +120,8 @@
                 spread[5 * jx + jy, c] = total[jy][c]
         return carry
 
-    lax.fori_loop(0, 5, five_taps, 0)
+    for jx in range(5):
+        five_taps(jx, 0)
 
     for g in range(tiles):
         rows = pl.ds(8 * g, 8)

time: 17.6 us -> 17.5 us (level)
  transfers between devices with their start and end apart: 4 -> 4, of which waited for: 1 -> 1; matrix products, arithmetic and copies ran while one was open for 0% -> 0% of each run, Pallas kernels for 33% -> 32%
where the time goes in v11:
time: 17.5 us; the launch traced here: 17.3 us
  Pallas kernels  9.73 us (56%)
  starting transfers between devices  4.82 us (28%)
  waiting for transfers between devices  2.69 us (15%)
    ppermute x2, starting transfers between devices, column_swap(): return lax.ppermute(block, ROW_AXES + (COLUMN_AXES,), pairs)  3.22 us
    ppermute x2, waiting for transfers between devices, row_swap(): return lax.ppermute(block, ROW_AXES + (COLUMN_AXES,), pairs)  2.69 us
    pallas_call x1, Pallas kernels, local(): pl.pallas_call(both_steps, out_shape=(shape(stacks, width, 128), shape(OF...  2.56 us
    ppermute x2, starting transfers between devices, row_swap(): return lax.ppermute(block, ROW_AXES + (COLUMN_AXES,), pairs)  1.61 us
    pallas_call x1, Pallas kernels, local(): pl.pallas_call(edge_rows, out_shape=(whole(tracer_mass), whole(intersecti...  1.57 us
    pallas_call x1, Pallas kernels, local(): pl.pallas_call(coefficients, out_shape=shape(OFFSETS, width, 128), in_spe...  1.51 us
    pallas_call x1, Pallas kernels, local(): pl.pallas_call(halo_steps, out_shape=shape(stacks, width, columns), in_sp...  1.42 us
    pallas_call x1, Pallas kernels, local(): pl.pallas_call(own_part, out_shape=(shape(stacks, width - 8, 128),) + (sh...  0.88 us
  transfers between devices with their start and end apart: 4, of which 1 were waited for; matrix products, arithmetic and copies ran while one was open for 0% of the time, Pallas kernels for 32%

profile of v11, /device:TPU:12, one launch (start us, length us, event | category | flops | bytes accessed | tf_op | source)
XLA Modules:
  0.0 17.3 jit_solution(7182116473210828354)
XLA Ops:
  0.0 1.6 %edge_rows.1 = (f32[40,16,128]{2,1,0:T(8,128)S(1)}, f32[4,10,16,128]{3,2,1,0:T(8,128)S(1)}, s32[4,16,128]{2,1,0:T(8,128)S(1)}, s32[4,16,128]{2,1,0:T(8,128)S(1)}...) custom-call(f32[10,25]{1,0:T(8,128)} %recon_hbm.3, f32[40,16,128]{2,1,0:T(8,128)} %mass_hbm.1, ...), custom_call_target="tpu_custom_call" | custom-call | flops 4000000 | bytes 1048576 | tf_op jit(solution)/shard_map/edge_rows/pallas_call | solution.py:653
  1.6 0.1 collective-permute-start.1
  1.7 1.5 %collective-permute-start = (f32[392,128]{1,0:T(8,128)S(1)}, f32[392,128]{1,0:T(8,128)S(1)}, u32[]{:S(2)}, u32[]{:S(2)}) collective-permute-start(f32[392,128]{1,0:T(8,128)S(1)} %get-tuple-element.33), channel_id=1, source_target_pairs={{0,4},{1,5},{2,6},{3,7},{4,0},{5,1},{6,2},{7,3},{8,12},{9,13},{10,... | collective-permute-start | bytes 602120 | tf_op jit(solution)/shard_map/ppermute | solution.py:62
  3.2 1.5 %coefficients.1.stencil = f32[49,16,128]{2,1,0:T(8,128)S(1)} custom-call(f32[10,25]{1,0:T(8,128)} %recon_hbm.3, f32[4,10,16,128]{3,2,1,0:T(8,128)S(1)} %get-tuple-element.30.weights, s32[4,16,128]{2,1,0:T(8,128)S(1)} %get-tuple-element.31.cells, s32[4,16,128]{2,1,0:T(8,128)S(1)} %get-tuple-element.32.codes), custom_call_target="tpu_custom_call" | custom-call | flops 8000000 | bytes 1048576 | tf_op jit(solution)/shard_map/coefficients/pallas_call | solution.py:678
  4.7 0.7 %pack_own.1 = (f32[64,128]{1,0:T(8,128)S(1)}, f32[64,128]{1,0:T(8,128)S(1)}, bf16[7,256,256]{2,1,0:T(8,128)(2,1)S(1)}, bf16[7,256,256]{2,1,0:T(8,128)(2,1)S(1)}) custom-call(f32[40,16,128]{2,1,0:T(8,128)S(1)} %get-tuple-element.29.mass, f32[49,16,128]{2,1,0:T(8,128)S(1)} %coefficients.1.stencil), custom_call_target="tpu_custom_call" | custom-call | flops 1000000 | bytes 1048576 | tf_op jit(solution)/shard_map/pack_own/pallas_call | solution.py:694
  5.4 0.9 %own_part.1 = (f32[40,8,128]{2,1,0:T(8,128)S(1)}, f32[49,16,128]{2,1,0:T(8,128)S(1)}, f32[49,16,128]{2,1,0:T(8,128)S(1)}, f32[49,16,128]{2,1,0:T(8,128)S(1)}) custom-call(f32[40,16,128]{2,1,0:T(8,128)S(1)} %get-tuple-element.29.mass, f32[49,16,128]{2,1,0:T(8,128)S(1)} %coefficients.1.stencil, bf16[7,256,256]{2,1,0:T(8,128)(2,1)S(1)} %get-tuple-element.35.near), custom_call_target="tpu_custom_call" | custom-call | flops 4000000 | bytes 1048576 | tf_op jit(solution)/shard_map/own_part/pallas_call | solution.py:704
  6.2 2.7 %collective-permute-done.1.got = f32[392,128]{1,0:T(8,128)S(1)} collective-permute-done((f32[392,128]{1,0:T(8,128)S(1)}, f32[392,128]{1,0:T(8,128)S(1)}, u32[]{:S(2)}, u32[]{:S(2)}) %collective-permute-start.1) | collective-permute-done | bytes 200736 | tf_op jit(solution)/shard_map/ppermute | solution.py:62
  9.0 0.0 collective-permute-done.got_a
  9.0 0.5 %pack_all.1 = (f32[112,128]{1,0:T(8,128)S(1)}, f32[112,128]{1,0:T(8,128)S(1)}) custom-call(f32[64,128]{1,0:T(8,128)S(1)} %get-tuple-element.41.own_left, f32[64,128]{1,0:T(8,128)S(1)} %get-tuple-element.42.own_right, f32[392,128]{1,0:T(8,128)S(1)} %get-tuple-element.37.above, f32[392,128]{1,0:T(8,128)S(1)} %get-tuple-element.38.below, ...), custom_call_target="tpu_custom_call" | custom-call | flops 1000000 | bytes 1048576 | tf_op jit(solution)/shard_map/pack_all/pallas_call | solution.py:734
  9.5 0.5 %collective-permute-start.3 = (f32[112,128]{1,0:T(8,128)S(1)}, f32[112,128]{1,0:T(8,128)S(1)}, u32[]{:S(2)}, u32[]{:S(2)}) collective-permute-start(f32[112,128]{1,0:T(8,128)S(1)} %get-tuple-element.43.send_a), channel_id=1, source_target_pairs={{0,1},{1,0},{2,3},{3,2},{4,5},{5,4},{6,7},{7,6},{8,9},{9,8},{10,11... | collective-permute-start | bytes 172040 | tf_op jit(solution)/shard_map/ppermute | solution.py:47
  10.0 2.7 %collective-permute-start.2 = (f32[112,128]{1,0:T(8,128)S(1)}, f32[112,128]{1,0:T(8,128)S(1)}, u32[]{:S(2)}, u32[]{:S(2)}) collective-permute-start(f32[112,128]{1,0:T(8,128)S(1)} %get-tuple-element.44.send_b), channel_id=1, source_target_pairs={{0,4},{1,2},{2,1},{3,7},{4,0},{5,6},{6,5},{7,3},{8,12},{9,10},{10,... | collective-permute-start | bytes 172040 | tf_op jit(solution)/shard_map/ppermute | solution.py:47
  12.7 2.6 %both_steps.1 = (f32[40,16,128]{2,1,0:T(8,128)S(1)}, f32[49,24,128]{2,1,0:T(8,128)S(1)}) custom-call(f32[40,16,128]{2,1,0:T(8,128)S(1)} %get-tuple-element.29.mass, f32[49,16,128]{2,1,0:T(8,128)S(1)} %coefficients.1.stencil, f32[392,128]{1,0:T(8,128)S(1)} %get-tuple-element.37.above, f32[392,128]{1,0:T(8,128)S(1)} %get-tuple-element.38.below, ...), custom_call_target="tpu_custom_call" | custom-call | flops 12000000 | bytes 1048576 | tf_op jit(solution)/shard_map/both_steps/pallas_call | solution.py:747
  15.3 0.0 collective-permute-done.3.got_a
  15.3 0.0 collective-permute-done.2.got_b
  15.3 0.6 %side_coefficients.1 = (f32[3,32,128]{2,1,0:T(8,128)S(1)}, f32[3,32,128]{2,1,0:T(8,128)S(1)}, f32[49,24,128]{2,1,0:T(8,128)S(1)}, f32[49,24,128]{2,1,0:T(8,128)S(1)}) custom-call(f32[49,24,128]{2,1,0:T(8,128)S(1)} %get-tuple-element.40.wide, f32[112,128]{1,0:T(8,128)S(1)} %get-tuple-element.43.send_a, f32[112,128]{1,0:T(8,128)S(1)} %get-tuple-element.44.send_b, ...), custom_call_target="tpu_custom_call" | custom-call | flops 4000000 | bytes 1048576 | tf_op jit(solution)/shard_map/side_coefficients/pallas_call | solution.py:758
  15.9 1.4 %halo_steps.1 = f32[40,16,128]{2,1,0:T(8,128)} custom-call(f32[3,32,128]{2,1,0:T(8,128)S(1)} %get-tuple-element.46.right_set, f32[3,32,128]{2,1,0:T(8,128)S(1)} %get-tuple-element.47.left_set, f32[49,24,128]{2,1,0:T(8,128)S(1)} %get-tuple-element.48.right_coef, f32[49,24,128]{2,1,0:T(8,128)S(1)} %get-tuple-element.49.left_coef, ...), custom_call_target="tpu_custom_call" | custom-call | flops 4000000 | bytes 1048576 | tf_op jit(solution)/shard_map/halo_steps/pallas_call | solution.py:769
  (2 shorter events, 0.1 us)
Async XLA Ops:
  1.6 7.4 %collective-permute-start.1 = (f32[392,128]{1,0:T(8,128)S(1)}, f32[392,128]{1,0:T(8,128)S(1)}, u32[]{:S(2)}, u32[]{:S(2)}) collective-permute-start(f32[392,128]{1,0:T(8,128)S(1)} %get-tuple-element.34), channel_id=1, source_target_pairs={{0,1},{1,0},{2,3},{3,2},{4,8},{5,9},{6,10},{7,11},{8,4},{9,5},{10,... | collective-permute-start | bytes 602120 | tf_op jit(solution)/shard_map/ppermute | solution.py:62
  1.7 7.3 %collective-permute-start = (f32[392,128]{1,0:T(8,128)S(1)}, f32[392,128]{1,0:T(8,128)S(1)}, u32[]{:S(2)}, u32[]{:S(2)}) collective-permute-start(f32[392,128]{1,0:T(8,128)S(1)} %get-tuple-element.33), channel_id=1, source_target_pairs={{0,4},{1,5},{2,6},{3,7},{4,0},{5,1},{6,2},{7,3},{8,12},{9,13},{10,... | collective-permute-start | bytes 602120 | tf_op jit(solution)/shard_map/ppermute | solution.py:62
  9.5 5.8 %collective-permute-start.3 = (f32[112,128]{1,0:T(8,128)S(1)}, f32[112,128]{1,0:T(8,128)S(1)}, u32[]{:S(2)}, u32[]{:S(2)}) collective-permute-start(f32[112,128]{1,0:T(8,128)S(1)} %get-tuple-element.43.send_a), channel_id=1, source_target_pairs={{0,1},{1,0},{2,3},{3,2},{4,5},{5,4},{6,7},{7,6},{8,9},{9,8},{10,11... | collective-permute-start | bytes 172040 | tf_op jit(solution)/shard_map/ppermute | solution.py:47
  10.0 5.3 %collective-permute-start.2 = (f32[112,128]{1,0:T(8,128)S(1)}, f32[112,128]{1,0:T(8,128)S(1)}, u32[]{:S(2)}, u32[]{:S(2)}) collective-permute-start(f32[112,128]{1,0:T(8,128)S(1)} %get-tuple-element.44.send_b), channel_id=1, source_target_pairs={{0,4},{1,2},{2,1},{3,7},{4,0},{5,6},{6,5},{7,3},{8,12},{9,10},{10,... | collective-permute-start | bytes 172040 | tf_op jit(solution)/shard_map/ppermute | solution.py:47

commit v12 on v11

--- a/solution.py
+++ b/solution.py
@@ -15,7 +15,7 @@
 POWERS = ((0, 0), (1, 0), (0, 1), (2, 0), (1, 1), (0, 2), (3, 0), (2, 1), (1, 2), (0, 3))
 TERMS = 10
 OFFSETS = 49
-GROUP = 4
+GROUP = 5
 SPAN = 9
 PER = 14
 COEF_PER = 42
@@ -457,7 +457,7 @@
 
 
 def per_turn(stacks):
-    return next(GROUP * groups for groups in (10, 5, 2, 1) if stacks % (GROUP * groups) == 0)
+    return next(GROUP * groups for groups in (8, 4, 2, 1) if stacks % (GROUP * groups) == 0)
 
 
 def turns(stacks):

time: 17.5 us -> 17.7 us (1.011)
  transfers between devices with their start and end apart: 4 -> 4, of which waited for: 1 -> 1; matrix products, arithmetic and copies ran while one was open for 0% -> 0% of each run, Pallas kernels for 32% -> 33%
where the time goes in v12:
time: 17.7 us; the launch traced here: 17.5 us
  Pallas kernels  9.89 us (56%)
  starting transfers between devices  4.82 us (27%)
  waiting for transfers between devices  2.68 us (15%)
    ppermute x2, starting transfers between devices, column_swap(): return lax.ppermute(block, ROW_AXES + (COLUMN_AXES,), pairs)  3.22 us
    pallas_call x1, Pallas kernels, local(): pl.pallas_call(both_steps, out_shape=(shape(stacks, width, 128), shape(OF...  2.71 us
    ppermute x2, waiting for transfers between devices, row_swap(): return lax.ppermute(block, ROW_AXES + (COLUMN_AXES,), pairs)  2.67 us
    ppermute x2, starting transfers between devices, row_swap(): return lax.ppermute(block, ROW_AXES + (COLUMN_AXES,), pairs)  1.61 us
    pallas_call x1, Pallas kernels, local(): pl.pallas_call(edge_rows, out_shape=(whole(tracer_mass), whole(intersecti...  1.57 us
    pallas_call x1, Pallas kernels, local(): pl.pallas_call(coefficients, out_shape=shape(OFFSETS, width, 128), in_spe...  1.51 us
    pallas_call x1, Pallas kernels, local(): pl.pallas_call(halo_steps, out_shape=shape(stacks, width, columns), in_sp...  1.42 us
    pallas_call x1, Pallas kernels, local(): pl.pallas_call(own_part, out_shape=(shape(stacks, width - 8, 128),) + (sh...  0.89 us
  transfers between devices with their start and end apart: 4, of which 1 were waited for; matrix products, arithmetic and copies ran while one was open for 0% of the time, Pallas kernels for 33%

profile of v12, /device:TPU:12, one launch (start us, length us, event | category | flops | bytes accessed | tf_op | source)
XLA Modules:
  0.0 17.5 jit_solution(17984186846226437693)
XLA Ops:
  0.0 1.6 %edge_rows.1 = (f32[40,16,128]{2,1,0:T(8,128)S(1)}, f32[4,10,16,128]{3,2,1,0:T(8,128)S(1)}, s32[4,16,128]{2,1,0:T(8,128)S(1)}, s32[4,16,128]{2,1,0:T(8,128)S(1)}...) custom-call(f32[10,25]{1,0:T(8,128)} %recon_hbm.3, f32[40,16,128]{2,1,0:T(8,128)} %mass_hbm.1, ...), custom_call_target="tpu_custom_call" | custom-call | flops 4000000 | bytes 1048576 | tf_op jit(solution)/shard_map/edge_rows/pallas_call | solution.py:653
  1.6 0.1 collective-permute-start.1
  1.7 1.5 %collective-permute-start = (f32[392,128]{1,0:T(8,128)S(1)}, f32[392,128]{1,0:T(8,128)S(1)}, u32[]{:S(2)}, u32[]{:S(2)}) collective-permute-start(f32[392,128]{1,0:T(8,128)S(1)} %get-tuple-element.33), channel_id=1, source_target_pairs={{0,4},{1,5},{2,6},{3,7},{4,0},{5,1},{6,2},{7,3},{8,12},{9,13},{10,... | collective-permute-start | bytes 602120 | tf_op jit(solution)/shard_map/ppermute | solution.py:62
  3.2 1.5 %coefficients.1.stencil = f32[49,16,128]{2,1,0:T(8,128)S(1)} custom-call(f32[10,25]{1,0:T(8,128)} %recon_hbm.3, f32[4,10,16,128]{3,2,1,0:T(8,128)S(1)} %get-tuple-element.30.weights, s32[4,16,128]{2,1,0:T(8,128)S(1)} %get-tuple-element.31.cells, s32[4,16,128]{2,1,0:T(8,128)S(1)} %get-tuple-element.32.codes), custom_call_target="tpu_custom_call" | custom-call | flops 8000000 | bytes 1048576 | tf_op jit(solution)/shard_map/coefficients/pallas_call | solution.py:678
  4.7 0.7 %pack_own.1 = (f32[64,128]{1,0:T(8,128)S(1)}, f32[64,128]{1,0:T(8,128)S(1)}, bf16[7,256,256]{2,1,0:T(8,128)(2,1)S(1)}, bf16[7,256,256]{2,1,0:T(8,128)(2,1)S(1)}) custom-call(f32[40,16,128]{2,1,0:T(8,128)S(1)} %get-tuple-element.29.mass, f32[49,16,128]{2,1,0:T(8,128)S(1)} %coefficients.1.stencil), custom_call_target="tpu_custom_call" | custom-call | flops 1000000 | bytes 1048576 | tf_op jit(solution)/shard_map/pack_own/pallas_call | solution.py:694
  5.4 0.9 %own_part.1 = (f32[40,8,128]{2,1,0:T(8,128)S(1)}, f32[49,16,128]{2,1,0:T(8,128)S(1)}, f32[49,16,128]{2,1,0:T(8,128)S(1)}, f32[49,16,128]{2,1,0:T(8,128)S(1)}) custom-call(f32[40,16,128]{2,1,0:T(8,128)S(1)} %get-tuple-element.29.mass, f32[49,16,128]{2,1,0:T(8,128)S(1)} %coefficients.1.stencil, bf16[7,256,256]{2,1,0:T(8,128)(2,1)S(1)} %get-tuple-element.35.near), custom_call_target="tpu_custom_call" | custom-call | flops 4000000 | bytes 1048576 | tf_op jit(solution)/shard_map/own_part/pallas_call | solution.py:704
  6.3 2.7 %collective-permute-done.1.got = f32[392,128]{1,0:T(8,128)S(1)} collective-permute-done((f32[392,128]{1,0:T(8,128)S(1)}, f32[392,128]{1,0:T(8,128)S(1)}, u32[]{:S(2)}, u32[]{:S(2)}) %collective-permute-start.1) | collective-permute-done | bytes 200736 | tf_op jit(solution)/shard_map/ppermute | solution.py:62
  9.0 0.0 collective-permute-done.got_a
  9.0 0.5 %pack_all.1 = (f32[112,128]{1,0:T(8,128)S(1)}, f32[112,128]{1,0:T(8,128)S(1)}) custom-call(f32[64,128]{1,0:T(8,128)S(1)} %get-tuple-element.41.own_left, f32[64,128]{1,0:T(8,128)S(1)} %get-tuple-element.42.own_right, f32[392,128]{1,0:T(8,128)S(1)} %get-tuple-element.37.above, f32[392,128]{1,0:T(8,128)S(1)} %get-tuple-element.38.below, ...), custom_call_target="tpu_custom_call" | custom-call | flops 1000000 | bytes 1048576 | tf_op jit(solution)/shard_map/pack_all/pallas_call | solution.py:734
  9.5 0.5 %collective-permute-start.3 = (f32[112,128]{1,0:T(8,128)S(1)}, f32[112,128]{1,0:T(8,128)S(1)}, u32[]{:S(2)}, u32[]{:S(2)}) collective-permute-start(f32[112,128]{1,0:T(8,128)S(1)} %get-tuple-element.43.send_a), channel_id=1, source_target_pairs={{0,1},{1,0},{2,3},{3,2},{4,5},{5,4},{6,7},{7,6},{8,9},{9,8},{10,11... | collective-permute-start | bytes 172040 | tf_op jit(solution)/shard_map/ppermute | solution.py:47
  10.0 2.7 %collective-permute-start.2 = (f32[112,128]{1,0:T(8,128)S(1)}, f32[112,128]{1,0:T(8,128)S(1)}, u32[]{:S(2)}, u32[]{:S(2)}) collective-permute-start(f32[112,128]{1,0:T(8,128)S(1)} %get-tuple-element.44.send_b), channel_id=1, source_target_pairs={{0,4},{1,2},{2,1},{3,7},{4,0},{5,6},{6,5},{7,3},{8,12},{9,10},{10,... | collective-permute-start | bytes 172040 | tf_op jit(solution)/shard_map/ppermute | solution.py:47
  12.7 2.7 %both_steps.1 = (f32[40,16,128]{2,1,0:T(8,128)S(1)}, f32[49,24,128]{2,1,0:T(8,128)S(1)}) custom-call(f32[40,16,128]{2,1,0:T(8,128)S(1)} %get-tuple-element.29.mass, f32[49,16,128]{2,1,0:T(8,128)S(1)} %coefficients.1.stencil, f32[392,128]{1,0:T(8,128)S(1)} %get-tuple-element.37.above, f32[392,128]{1,0:T(8,128)S(1)} %get-tuple-element.38.below, ...), custom_call_target="tpu_custom_call" | custom-call | flops 12000000 | bytes 1048576 | tf_op jit(solution)/shard_map/both_steps/pallas_call | solution.py:747
  15.4 0.0 collective-permute-done.3.got_a
  15.4 0.0 collective-permute-done.2.got_b
  15.4 0.6 %side_coefficients.1 = (f32[3,32,128]{2,1,0:T(8,128)S(1)}, f32[3,32,128]{2,1,0:T(8,128)S(1)}, f32[49,24,128]{2,1,0:T(8,128)S(1)}, f32[49,24,128]{2,1,0:T(8,128)S(1)}) custom-call(f32[49,24,128]{2,1,0:T(8,128)S(1)} %get-tuple-element.40.wide, f32[112,128]{1,0:T(8,128)S(1)} %get-tuple-element.43.send_a, f32[112,128]{1,0:T(8,128)S(1)} %get-tuple-element.44.send_b, ...), custom_call_target="tpu_custom_call" | custom-call | flops 4000000 | bytes 1048576 | tf_op jit(solution)/shard_map/side_coefficients/pallas_call | solution.py:758
  16.1 1.4 %halo_steps.1 = f32[40,16,128]{2,1,0:T(8,128)} custom-call(f32[3,32,128]{2,1,0:T(8,128)S(1)} %get-tuple-element.46.right_set, f32[3,32,128]{2,1,0:T(8,128)S(1)} %get-tuple-element.47.left_set, f32[49,24,128]{2,1,0:T(8,128)S(1)} %get-tuple-element.48.right_coef, f32[49,24,128]{2,1,0:T(8,128)S(1)} %get-tuple-element.49.left_coef, ...), custom_call_target="tpu_custom_call" | custom-call | flops 4000000 | bytes 1048576 | tf_op jit(solution)/shard_map/halo_steps/pallas_call | solution.py:769
  (2 shorter events, 0.1 us)
Async XLA Ops:
  1.6 7.4 %collective-permute-start.1 = (f32[392,128]{1,0:T(8,128)S(1)}, f32[392,128]{1,0:T(8,128)S(1)}, u32[]{:S(2)}, u32[]{:S(2)}) collective-permute-start(f32[392,128]{1,0:T(8,128)S(1)} %get-tuple-element.34), channel_id=1, source_target_pairs={{0,1},{1,0},{2,3},{3,2},{4,8},{5,9},{6,10},{7,11},{8,4},{9,5},{10,... | collective-permute-start | bytes 602120 | tf_op jit(solution)/shard_map/ppermute | solution.py:62
  1.7 7.3 %collective-permute-start = (f32[392,128]{1,0:T(8,128)S(1)}, f32[392,128]{1,0:T(8,128)S(1)}, u32[]{:S(2)}, u32[]{:S(2)}) collective-permute-start(f32[392,128]{1,0:T(8,128)S(1)} %get-tuple-element.33), channel_id=1, source_target_pairs={{0,4},{1,5},{2,6},{3,7},{4,0},{5,1},{6,2},{7,3},{8,12},{9,13},{10,... | collective-permute-start | bytes 602120 | tf_op jit(solution)/shard_map/ppermute | solution.py:62
  9.5 5.9 %collective-permute-start.3 = (f32[112,128]{1,0:T(8,128)S(1)}, f32[112,128]{1,0:T(8,128)S(1)}, u32[]{:S(2)}, u32[]{:S(2)}) collective-permute-start(f32[112,128]{1,0:T(8,128)S(1)} %get-tuple-element.43.send_a), channel_id=1, source_target_pairs={{0,1},{1,0},{2,3},{3,2},{4,5},{5,4},{6,7},{7,6},{8,9},{9,8},{10,11... | collective-permute-start | bytes 172040 | tf_op jit(solution)/shard_map/ppermute | solution.py:47
  10.0 5.5 %collective-permute-start.2 = (f32[112,128]{1,0:T(8,128)S(1)}, f32[112,128]{1,0:T(8,128)S(1)}, u32[]{:S(2)}, u32[]{:S(2)}) collective-permute-start(f32[112,128]{1,0:T(8,128)S(1)} %get-tuple-element.44.send_b), channel_id=1, source_target_pairs={{0,4},{1,2},{2,1},{3,7},{4,0},{5,6},{6,5},{7,3},{8,12},{9,10},{10,... | collective-permute-start | bytes 172040 | tf_op jit(solution)/shard_map/ppermute | solution.py:47
